TPU v7x, 128 devices: a whole 4x4x4 slice. The times are simulated.
128 devices in a mesh: ctx: 32 (over y, x, core), dp: 4 (over z).
Axes of the slice: x: 4, y: 4, z: 4, core: 2. Of those that a mesh axis runs over, the one named last changes fastest.
Arguments:
- tokens: bfloat16 [4, 16384, 2048], P('dp', 'ctx'), may hold values from -6 to 6
- w_query: bfloat16 [2048, 1024], replicated, may hold values from -0.125 to 0.125
- w_key: bfloat16 [2048, 1024], replicated, may hold values from -0.125 to 0.125
- w_value: bfloat16 [2048, 1024], replicated, may hold values from -0.125 to 0.125
- cotangent: bfloat16 [4, 16384, 1024], P('dp', 'ctx'), may hold values from -6 to 6
Outputs:
- attn_out: bfloat16 [4, 16384, 1024], P('dp', 'ctx')
- input_grad: bfloat16 [4, 16384, 2048], P('dp', 'ctx')
- grad_query: float32 [2048, 1024], P(('ctx', 'dp'))
- grad_key: float32 [2048, 1024], P(('ctx', 'dp'))
- grad_value: float32 [2048, 1024], P(('ctx', 'dp'))
All inputs are finite; a program needn't handle non-finite values.
Results may differ from a plain program's by a relative error of at most 0.022.
Values may be sent and summed in bfloat16 or wider, within the bound.
No kernel may reach another device: no remote copies, remote signals or barrier semaphores. Data moves between devices by JAX's collectives and lax.ppermute only.
A program may use at most 192 MiB of HBM per device.

v0:
```python
import jax
import jax.numpy as jnp
from jax import lax
from jax.experimental import pallas as pl
from jax.experimental.pallas import tpu as pltpu
from jax.sharding import Mesh
from jax.sharding import PartitionSpec as P

DH = 128
TOK = 512
EPS = 1e-05
CTX = ("y", "x", "c")
CTX_DP = ("y", "x", "c", "z")
BF = jnp.bfloat16
F32 = jnp.float32
MB = 1 << 20


def dot(a, b, ca=1, cb=0):
    return lax.dot_general(a, b, (((ca,), (cb,)), ((), ())), preferred_element_type=F32)


def causal(x, turned=False):
    rows = lax.broadcasted_iota(jnp.int32, x.shape, 0)
    cols = lax.broadcasted_iota(jnp.int32, x.shape, 1)
    keep = rows <= cols if turned else rows >= cols
    return jnp.where(keep, x, 0.0).astype(BF)


def head(h):
    if isinstance(h, int):
        return slice(h * DH, (h + 1) * DH)
    return pl.ds(pl.multiple_of(h * DH, DH), DH)


def each_head(body):
    def step(h, carry):
        body(h)
        return carry

    lax.fori_loop(0, 4, step, 0)


def call(kernel, core, grid, ins, outs, flops, moved, limit=20):
    return pl.pallas_call(
        kernel,
        out_shape=[jax.ShapeDtypeStruct(s, d) for s, d, _, _ in outs],
        grid_spec=pltpu.PrefetchScalarGridSpec(
            num_scalar_prefetch=1,
            grid=(grid,),
            in_specs=[pl.BlockSpec(b, m) for _, b, m in ins],
            out_specs=[pl.BlockSpec(b, m) for _, _, b, m in outs],
        ),
        compiler_params=pltpu.CompilerParams(
            dimension_semantics=("arbitrary",), vmem_limit_bytes=limit * MB
        ),
        cost_estimate=pl.CostEstimate(flops=flops, bytes_accessed=moved, transcendentals=0),
    )(core, *[a for a, _, _ in ins])


def local(kernel, core, ins, outs, hbm_in=0, hbm_out=0, scratch=()):
    vmem, hbm = pl.BlockSpec(memory_space=pltpu.VMEM), pl.BlockSpec(memory_space=pltpu.HBM)
    return pl.pallas_call(
        kernel,
        out_shape=[jax.ShapeDtypeStruct(s, d) for s, d in outs],
        in_specs=[pl.BlockSpec(memory_space=pltpu.SMEM)]
        + [vmem] * (len(ins) - hbm_in)
        + [hbm] * hbm_in,
        out_specs=[vmem] * (len(outs) - hbm_out) + [hbm] * hbm_out,
        scratch_shapes=list(scratch),
        compiler_params=pltpu.CompilerParams(vmem_limit_bytes=20 * MB),
        cost_estimate=pl.CostEstimate(flops=1000000, bytes_accessed=1000, transcendentals=0),
    )(core, *ins)


def whole(j, c):
    return (0, 0)


def tall(j, c):
    return (j, 0)


def wide(j, c):
    return (0, j)


def mine(j, c):
    return (0, c[0] * 2 + j)


def in_hbm(*arrays):
    return [pltpu.with_memory_space_constraint(t, pltpu.HBM) for t in arrays]


def half_of(which):
    return pl.ds(pl.multiple_of(which * 512, 512), 512)


def project_own(core, tok, wk, wv):
    def kernel(c, t, b, d, k, v, s, bh, dh, tv, sems):
        copies = [pltpu.make_async_copy(t, tv, sems.at[0])]
        copies.append(pltpu.make_async_copy(b.at[:, half_of(c[0])], bh, sems.at[1]))
        copies.append(pltpu.make_async_copy(d.at[:, half_of(c[0])], dh, sems.at[2]))
        for copy in copies:
            copy.start()
        copies[0].wait()
        copies[1].wait()
        k[...] = dot(tv[...], bh[...]).astype(BF)
        copies[2].wait()
        v[...] = dot(tv[...], dh[...]).astype(BF)
        for h in range(4):
            s[head(h), :] = dot(k[:, head(h)], v[:, head(h)], 0, 0).astype(BF)

    row, weight = ((TOK, 512), BF), ((2048, 512), BF)
    return local(
        kernel,
        core,
        in_hbm(tok, wk, wv),
        [row] * 2 + [((512, DH), BF)] + [weight] * 2,
        hbm_in=3,
        scratch=[pltpu.VMEM((TOK, 2048), BF), pltpu.SemaphoreType.DMA((3,))],
    )


def project_partner(core, tok, wk, wv, state, wq):
    def kernel(c, t, b, d, so, a, k, v, s, total, ah, sem):
        copy = pltpu.make_async_copy(a.at[:, half_of(c[0])], ah, sem)
        copy.start()
        k[...] = dot(t[...], b[...]).astype(BF)
        v[...] = dot(t[...], d[...]).astype(BF)
        for h in range(4):
            st = dot(k[:, head(h)], v[:, head(h)], 0, 0).astype(BF)
            s[head(h), :] = st
            total[head(h), :] = (st.astype(F32) + so[head(h), :].astype(F32)).astype(BF)
        copy.wait()

    row = ((TOK, 512), BF)
    return local(
        kernel,
        core,
        [tok, wk, wv, state, *in_hbm(wq)],
        [row] * 2 + [((512, DH), BF)] * 2 + [((2048, 512), BF)],
        hbm_in=1,
        scratch=[pltpu.SemaphoreType.DMA],
    )


LOW = slice(0, 256)
HIGH = slice(256, 512)


def forward_pairs(q, k, v):
    s00 = causal(dot(q[LOW], k[LOW], 1, 1))
    s10 = dot(q[HIGH], k[LOW], 1, 1).astype(BF)
    s11 = causal(dot(q[HIGH], k[HIGH], 1, 1))
    return dot(s00, v[LOW]), dot(s10, v[LOW]) + dot(s11, v[HIGH])


def backward_pairs(q, k, x):
    s00 = causal(dot(k[LOW], q[LOW], 1, 1), True)
    s01 = dot(k[LOW], q[HIGH], 1, 1).astype(BF)
    s11 = causal(dot(k[HIGH], q[HIGH], 1, 1), True)
    return dot(s00, x[LOW]) + dot(s01, x[HIGH]), dot(s11, x[HIGH])


def masked_sum(refs, at, reverse):
    total = None
    for r, d in zip(refs, (1, 3, 2)):
        passed = at + (4 - d) < 4 if reverse else at >= d
        piece = r[...].astype(F32) * jnp.where(passed, 1.0, 0.0)
        total = piece if total is None else total + piece
    return total


def within(core, tok_o, tok_p, wq, k_o, v_o, k_p, v_p, cot):
    def kernel(c, to, tp, a, ko, vo, kp, vp, ct, qo, qp, out, mine_ct, other_ct, sems):
        copies = [
            pltpu.make_async_copy(ct.at[:, half_of(1 - c[0])], other_ct, sems.at[0]),
            pltpu.make_async_copy(ct.at[:, half_of(c[0])], mine_ct, sems.at[1]),
        ]
        for copy in copies:
            copy.start()
        qo[...] = dot(to[...], a[...]).astype(BF)
        qp[...] = dot(tp[...], a[...]).astype(BF)

        @each_head
        def _(h):
            for n, (q, k, v) in enumerate(((qo, ko, vo), (qp, kp, vp))):
                low, high = forward_pairs(q[:, head(h)], k[:, head(h)], v[:, head(h)])
                out[n * TOK : n * TOK + 256, head(h)] = low
                out[n * TOK + 256 : n * TOK + 512, head(h)] = high

        for copy in copies:
            copy.wait()

    return local(
        kernel,
        core,
        [tok_o, tok_p, wq, k_o, v_o, k_p, v_p, *in_hbm(cot)],
        [((TOK, 512), BF)] * 2 + [((2 * TOK, 512), F32)] + [((TOK, 512), BF)] * 2,
        hbm_in=1,
        scratch=[pltpu.SemaphoreType.DMA((2,))],
    )


def turned(core, tok_o, tok_p):
    def kernel(c, to, tp, out):
        out[:, :TOK] = to[...].T
        out[:, TOK:] = tp[...].T

    return call(
        kernel,
        core,
        4,
        [(tok_o, (TOK, 512), wide), (tok_p, (TOK, 512), wide)],
        [((2048, 2 * TOK), BF, (512, 2 * TOK), tall)],
        1000000,
        8 * MB,
    )[0]


def normed(core, intra, q_o, q_p, state_o, state_p, along_x, along_y, cot, cot_p):
    def kernel(c, it, qo, qp, so, sp, x1, x3, x2, y1, y3, y2, co, cp, *outs):
        ao, ap, g, po, pp, bo, bp, total = outs
        before = masked_sum((x1, x3, x2), c[2], False) + masked_sum((y1, y3, y2), c[1], False)
        late = c[0].astype(F32)
        po[...] = (before + sp[...].astype(F32) * late).astype(BF)
        pp[...] = (before + so[...].astype(F32) * (1.0 - late)).astype(BF)

        @each_head
        def _(h):
            backs = []
            for n, (q, p, a, b) in enumerate(((qo, po, ao, bo), (qp, pp, ap, bp))):
                rows = slice(n * TOK, n * TOK + TOK)
                qh = q[:, head(h)]
                mixed = it[rows, head(h)] + dot(qh, p[head(h), :])
                inverse = lax.rsqrt(jnp.mean(mixed * mixed, axis=-1, keepdims=True) + EPS)
                nm = mixed * inverse
                up = (co if n == 0 else cp)[:, head(h)].astype(F32)
                a[:, head(h)] = nm.astype(BF)
                gm = ((up - nm * jnp.mean(up * nm, axis=-1, keepdims=True)) * inverse).astype(BF)
                g[rows, head(h)] = gm
                back = dot(qh, gm, 0, 0).astype(BF)
                b[head(h), :] = back
                backs.append(back.astype(F32))
            total[head(h), :] = (backs[0] + backs[1]).astype(BF)

    state = ((512, DH), BF)
    return local(
        kernel,
        core,
        [intra, q_o, q_p, state_o, state_p, *along_x, *along_y, cot, cot_p],
        [((TOK, 512), BF)] * 2 + [((2 * TOK, 512), BF)] + [state] * 5,
    )


def grad_q_of(core, k_o, k_p, v_o, v_p, g, p_o, p_p):
    def kernel(c, ko, kp, vo, vp, gr, po, pp, dq):
        @each_head
        def _(h):
            for n, (k, v, p) in enumerate(((ko, vo, po), (kp, vp, pp))):
                gh = gr[n * TOK : n * TOK + TOK, head(h)]
                past = dot(gh, p[head(h), :], 1, 1)
                low, high = forward_pairs(gh, v[:, head(h)], k[:, head(h)])
                dq[n * TOK : n * TOK + 256, head(h)] = (low + past[LOW]).astype(BF)
                dq[n * TOK + 256 : n * TOK + 512, head(h)] = (high + past[HIGH]).astype(BF)

    return local(
        kernel,
        core,
        [k_o, k_p, v_o, v_p, g, p_o, p_p],
        [((2 * TOK, 512), BF)],
    )[0]


def grads_within(core, q_o, q_p, k_o, k_p, v_o, v_p, g):
    def kernel(c, qo, qp, ko, kp, vo, vp, gr, dk, dv):
        @each_head
        def _(h):
            for n, (q, k, v) in enumerate(((qo, ko, vo), (qp, kp, vp))):
                qh, kh, vh = q[:, head(h)], k[:, head(h)], v[:, head(h)]
                gh = gr[n * TOK : n * TOK + TOK, head(h)]
                for left, right, x, out in ((gh, vh, qh, dk), (qh, kh, gh, dv)):
                    low, high = backward_pairs(left, right, x)
                    out[n * TOK : n * TOK + 256, head(h)] = low
                    out[n * TOK + 256 : n * TOK + 512, head(h)] = high

    return local(
        kernel,
        core,
        [q_o, q_p, k_o, k_p, v_o, v_p, g],
        [((2 * TOK, 512), F32)] * 2,
    )


def grads_after(core, k_o, k_p, v_o, v_p, dk, dv, back_o, back_p, along_x, along_y):
    def kernel(c, ko, kp, vo, vp, ak, av, bo, bp, x1, x3, x2, y1, y3, y2, ok, ov):
        after = masked_sum((x1, x3, x2), c[2], True) + masked_sum((y1, y3, y2), c[1], True)
        late = c[0].astype(F32)
        s_o = (after + bp[...].astype(F32) * (1.0 - late)).astype(BF)
        s_p = (after + bo[...].astype(F32) * late).astype(BF)
        for n, (k, v, s) in enumerate(((ko, vo, s_o), (kp, vp, s_p))):
            rows = slice(n * TOK, n * TOK + TOK)
            for h in range(4):
                sh = s[head(h), :]
                ok[rows, head(h)] = (ak[rows, head(h)] + dot(v[:, head(h)], sh, 1, 1)).astype(BF)
                ov[rows, head(h)] = (av[rows, head(h)] + dot(k[:, head(h)], sh)).astype(BF)

    return local(
        kernel,
        core,
        [k_o, k_p, v_o, v_p, dk, dv, back_o, back_p, *along_x, *along_y],
        [((2 * TOK, 512), BF)] * 2,
    )


def weight_grad(core, tt, jobs):
    n = len(jobs)

    def kernel(c, t, *refs):
        for m, (_, axis, step) in enumerate(jobs):
            g, out = refs[m], refs[n + m]
            if axis == "x":
                rows = t[:, (c[2] + step) % 4]
            elif axis == "y":
                rows = t[(c[1] + step) % 4]
            part = dot(rows.reshape(512, 2 * TOK), g[...]).astype(BF)
            for a in range(4):
                at = (a - c[1] + 4) % 4 if axis == "x" else (a - c[2] + 4) % 4
                for core_at in range(2):
                    for z in range(4):
                        row = a * 128 + core_at * 64 + z * 16
                        out[at, (z - c[3] + 4) % 4, core_at * 16 : core_at * 16 + 16, :] = part[
                            row : row + 16, :
                        ]

    return local(
        kernel,
        core,
        [tt.reshape(4, 4, 128, 2 * TOK)] + [g for g, _, _ in jobs],
        [((4, 4, 32, 512), BF)] * n,
    )


def weight_grad_all(core, tt, grad):
    def kernel(c, t, g, out):
        def at_y(y, carry):
            part = dot(t[y].reshape(512, 2 * TOK), g[...]).astype(BF)
            dy = (y - c[1] + 4) % 4
            for x in range(4):
                dx = (x - c[2] + 4) % 4
                for core_at in range(2):
                    for z in range(4):
                        row = x * 128 + core_at * 64 + z * 16
                        here = slice(core_at * 16, core_at * 16 + 16)
                        out[dx, dy, (z - c[3] + 4) % 4, here, :] = part[row : row + 16, :]
            return carry

        lax.fori_loop(0, 4, at_y, 0)

    return local(
        kernel,
        core,
        [tt.reshape(4, 4, 128, 2 * TOK), grad],
        [((4, 4, 4, 32, 512), BF)],
    )[0]


def joined_heads(core, own, received):
    def kernel(c, o, r, out, sems):
        copies = [
            pltpu.make_async_copy(o, out.at[:, half_of(c[0])], sems.at[0]),
            pltpu.make_async_copy(r, out.at[:, half_of(1 - c[0])], sems.at[1]),
        ]
        for copy in copies:
            copy.start()
        for copy in copies:
            copy.wait()

    return local(
        kernel,
        core,
        [own, received],
        [((TOK, 1024), BF)],
        hbm_out=1,
        scratch=[pltpu.SemaphoreType.DMA((2,))],
    )[0]


def assembled(core, summed, came):
    def kernel(c, qkv, r, *outs):
        scale = 65536.0**-0.5
        mine = pl.ds(pl.multiple_of(c[0] * 16, 16), 16)
        here = pl.ds(pl.multiple_of(c[0] * 512, 512), 512)
        there = pl.ds(pl.multiple_of((1 - c[0]) * 512, 512), 512)
        for m, out in enumerate(outs):
            out[:, here] = qkv[mine, m * 512 : m * 512 + 512].astype(F32) * scale
            out[:, there] = r[:, m * 512 : m * 512 + 512].astype(F32) * scale

    return local(kernel, core, [summed, came], [((16, 1024), F32)] * 3)


def input_part(core, slot, grads, weights, received=None):
    final = received is not None

    def kernel(c, *refs):
        rows = slice(slot * TOK, slot * TOK + TOK)
        out = refs[7] if final else refs[6]
        def columns(j, carry):
            at = pl.ds(pl.multiple_of(j * 512, 512), 512)
            total = dot(refs[0][rows, :], refs[3][at, :], 1, 1)
            total = total + dot(refs[1][rows, :], refs[4][at, :], 1, 1)
            total = total + dot(refs[2][rows, :], refs[5][at, :], 1, 1)
            if final:
                held, sems = refs[8:]
                held[:, at] = (total + refs[6][:, at].astype(F32)).astype(BF)
                pltpu.make_async_copy(held.at[:, at], out.at[:, at], sems.at[j]).start()
            else:
                out[:, at] = total.astype(BF)
            return carry

        lax.fori_loop(0, 4, columns, 0)
        if final:
            held, sems = refs[8:]
            for j in range(4):
                at = pl.ds(j * 512, 512)
                pltpu.make_async_copy(held.at[:, at], out.at[:, at], sems.at[j]).wait()

    return local(
        kernel,
        core,
        [*grads, *weights] + ([received] if final else []),
        [((TOK, 2048), BF)],
        hbm_out=1 if final else 0,
        scratch=[pltpu.VMEM((TOK, 2048), BF), pltpu.SemaphoreType.DMA((4,))] if final else [],
    )[0]


def shift(v, axis, d):
    n = lax.axis_size(axis)
    return lax.ppermute(v, axis, [(i, (i + d) % n) for i in range(n)])


def swap(v):
    return lax.ppermute(v, "c", [(0, 1), (1, 0)])


def pieces(v, axis):
    return [shift(v, axis, d) for d in (1, 3, 2)]


def together(*values):
    return lax.optimization_barrier(values)


def f32_sum(*parts):
    total = parts[0].astype(F32)
    for p in parts[1:]:
        total = total + p.astype(F32)
    return total.astype(BF)


def ring_out(far, axis):
    return shift(far[:2], axis, 1), shift(far[2:], axis, 3)


def ring_near(up, down, came, axis):
    from_left, from_right = came
    up = jnp.concatenate([f32_sum(up[:2], from_left), up[2:]], axis=0)
    down = jnp.concatenate([down[:2], f32_sum(down[2:], from_right)], axis=0)
    return shift(up, axis, 1), shift(down, axis, 3)


def spread(blocks, axis):
    return f32_sum(blocks[0], *[shift(blocks[d], axis, d) for d in (2, 1, 3)])


def per_device(tokens, w_query, w_key, w_value, cotangent):
    c = lax.axis_index("c")
    core = jnp.stack([lax.axis_index(a) for a in ("c", "y", "x", "z")]).astype(jnp.int32)
    tok_o = tokens[0]
    tok_p = swap(tok_o)
    late = c == 1

    k_o, v_o, state_o, w_k, w_v = project_own(core, tok_o, w_key, w_value)
    k_p, v_p, state_p, total, w_q = project_partner(core, tok_p, w_k, w_v, state_o, w_query)
    weights = (w_q, w_k, w_v)
    along_x = pieces(total, "x")
    q_o, q_p, intra, cot, cot_s = within(
        core, tok_o, tok_p, w_q, k_o, v_o, k_p, v_p, cotangent[0]
    )
    row, intra, q_o, q_p, tok_t, cot_s = together(
        f32_sum(total, *along_x), intra, q_o, q_p, tok_o, cot_s
    )
    along_y = pieces(row, "y")
    cot_p = swap(cot_s)
    tt = turned(core, tok_t, tok_p)
    *along_y, tt, cot_p = together(*along_y, tt, cot_p)
    a_o, a_p, g, p_o, p_p, back_o, back_p, total = normed(
        core, intra, q_o, q_p, state_o, state_p, along_x, along_y, cot, cot_p
    )
    along_x = pieces(total, "x")
    a_r = swap(a_p)
    dq = grad_q_of(core, k_o, k_p, v_o, v_p, g, p_o, p_p)
    part_q = weight_grad_all(core, tt, dq)
    row, part_q, g, a_r = together(f32_sum(total, *along_x), part_q, g, a_r)
    along_y = pieces(row, "y")
    came_q = ring_out(part_q[2], "x")
    dk, dv = grads_within(core, q_o, q_p, k_o, k_p, v_o, v_p, g)
    *along_y, dk, dv, c0, c1 = together(*along_y, dk, dv, *came_q)
    last_q = ring_near(part_q[1], part_q[3], (c0, c1), "x")
    dk, dv = grads_after(
        core, k_o, k_p, v_o, v_p, dk, dv, back_o, back_p, along_x, along_y
    )
    far_k, far_v = weight_grad(core, tt, [(dk, "x", 2), (dv, "y", 2)])
    far_k, far_v, dk, dv = together(far_k, far_v, dk, dv)
    came_k, came_v = ring_out(far_k, "x"), shift(far_v, "y", 1)
    near = weight_grad(core, tt, [(dk, "x", 1), (dk, "x", 3), (dv, "y", 1), (dv, "y", 3)])
    here_k, here_v = weight_grad(core, tt, [(dk, "x", 0), (dv, "y", 0)])
    attn_out = joined_heads(core, a_o, a_r)
    ig_p = input_part(core, 1, (dq, dk, dv), weights)
    *near, dk, dv, here_k, here_v, ig_p, attn_out, k0, k1, came_v, q0, q1 = together(
        *near, dk, dv, here_k, here_v, ig_p, attn_out, *came_k, came_v, *last_q
    )
    last_k = ring_near(near[0], near[1], (k0, k1), "x")
    sum_q = f32_sum(part_q[0], q0, q1)
    flat = (16, 32, 512)
    up = jnp.concatenate([f32_sum(near[2], came_v).reshape(flat), sum_q[2, :2]], axis=0)
    down = jnp.concatenate([near[3].reshape(flat), sum_q[2, 2:]], axis=0)
    last_v = [shift(up, "y", 1), shift(down, "y", 3)]
    ig_r = swap(ig_p)
    input_grad = input_part(core, 0, (dq, dk, dv), weights, ig_r)
    sum_q, input_grad, k0, k1, v0, v1 = together(sum_q, input_grad, *last_k, *last_v)
    sum_k = f32_sum(here_k, k0, k1)
    sum_v = f32_sum(here_v.reshape(flat), v0[:16], v1[:16]).reshape(4, 4, 32, 512)
    up_q = jnp.concatenate([f32_sum(sum_q[1, :2], v0[16:]), sum_q[1, 2:]], axis=0)
    down_q = jnp.concatenate([sum_q[3, :2], f32_sum(sum_q[3, 2:], v1[16:])], axis=0)
    up, down = jnp.stack([sum_k[1], up_q]), jnp.stack([sum_k[3], down_q])
    up, down, far = shift(up, "y", 1), shift(down, "y", 3), shift(sum_k[2], "y", 2)
    sum_v = spread(sum_v, "x")
    sum_k = f32_sum(sum_k[0], up[0], down[0], far)
    sum_q = f32_sum(sum_q[0], up[1], down[1])
    summed = spread(jnp.concatenate([sum_q, sum_k, sum_v], axis=-1), "z")
    came = swap(jnp.where(late, summed[:16], summed[16:]))
    return (attn_out[None], input_grad[None], *assembled(core, summed, came))


def solution(mesh):
    finer = Mesh(mesh.devices.reshape(4, 4, 2, mesh.shape["dp"]), ("y", "x", "c", "z"))
    return jax.shard_map(
        per_device,
        mesh=finer,
        in_specs=(P("z", CTX, None), P(), P(), P(), P("z", CTX, None)),
        out_specs=(
            P("z", CTX, None),
            P("z", CTX, None),
            P(CTX_DP, None),
            P(CTX_DP, None),
            P(CTX_DP, None),
        ),
        check_vma=False,
    )
```

profile of v0, /device:TPU:1, one launch (start us, length us, event | category | flops | bytes accessed | tf_op | source)
XLA Modules:
  0.0 133.3 jit_solution(397137133621952003)
XLA Ops:
  2.2 5.6 %shard_map.92 = (bf16[512,512]{1,0:T(8,128)(2,1)S(1)}, bf16[512,512]{1,0:T(8,128)(2,1)S(1)}, bf16[512,128]{1,0:T(8,128)(2,1)S(1)}, bf16[2048,512]{1,0:T(8,128)(2,1)S(1)}, bf16[2048,512]{1,0:T(8,128)(2,1)S(1)}) custom-call(s32[4]{0:T(128)S(1)} %pad_add_fusion.c, bf16[512,2048]{1,0:T(8,128)(2,1)} %bitcast.73, bf16[2048,1024]{1,0:T(8,128)(2,1)} %b.1, ...), custom_call_target="tpu_custom_call" | custom-call | flops 1000000 | bytes 1000 | tf_op jit(solution)/shard_map/pallas_call | solution.py:63
  7.8 3.2 %shard_map.93 = (bf16[512,512]{1,0:T(8,128)(2,1)S(1)}, bf16[512,512]{1,0:T(8,128)(2,1)S(1)}, bf16[512,128]{1,0:T(8,128)(2,1)S(1)}, bf16[512,128]{1,0:T(8,128)(2,1)S(1)}, bf16[2048,512]{1,0:T(8,128)(2,1)S(1)}) custom-call(s32[4]{0:T(128)S(1)} %pad_add_fusion.c, bf16[512,2048]{1,0:T(8,128)(2,1)S(1)} %collective-permute-done.t.tp, ...), custom_call_target="tpu_custom_call" | custom-call | flops 1000000 | bytes 1000 | tf_op jit(solution)/shard_map/pallas_call | solution.py:63
  11.1 2.9 %collective-permute-start.3 = (bf16[512,128]{1,0:T(8,128)(2,1)S(1)}, bf16[512,128]{1,0:T(8,128)(2,1)S(1)}, u32[]{:S(2)}, u32[]{:S(2)}) collective-permute-start(bf16[512,128]{1,0:T(8,128)(2,1)S(1)} %get-tuple-element.93), channel_id=1, source_target_pairs={{0,16},{8,24},{16,0},{24,8},{1,17},{9,25},{17,1},{25,9},{2,18},{10... | collective-permute-start | bytes 393224 | tf_op jit(solution)/shard_map/ppermute | solution.py:442
  15.5 5.6 %shard_map.94 = (bf16[512,512]{1,0:T(8,128)(2,1)S(1)}, bf16[512,512]{1,0:T(8,128)(2,1)S(1)}, f32[1024,512]{1,0:T(8,128)S(1)}, bf16[512,512]{1,0:T(8,128)(2,1)S(1)}, bf16[512,512]{1,0:T(8,128)(2,1)S(1)}) custom-call(s32[4]{0:T(128)S(1)} %pad_add_fusion.c, bf16[512,2048]{1,0:T(8,128)(2,1)S(1)} %bitcast.74, bf16[512,2048]{1,0:T(8,128)(2,1)S(1)} %collective-permute-done.t.tp, ...), custom_call_target="tpu_custom_call" | custom-call | flops 1000000 | bytes 1000 | tf_op jit(solution)/shard_map/pallas_call | solution.py:63
  22.2 2.9 %collective-permute-start.6 = (bf16[512,128]{1,0:T(8,128)(2,1)S(1)}, bf16[512,128]{1,0:T(8,128)(2,1)S(1)}, u32[]{:S(2)}, u32[]{:S(2)}) collective-permute-start(bf16[512,128]{1,0:T(8,128)(2,1)S(1)} %add_convert_fusion.7), channel_id=1, source_target_pairs={{0,64},{32,96},{64,0},{96,32},{1,65},{33,97},{65,1},{97,33},{2,66}... | collective-permute-start | bytes 393224 | tf_op jit(solution)/shard_map/ppermute | solution.py:442
  26.6 2.3 %shard_map.95 = bf16[2048,1024]{1,0:T(8,128)(2,1)S(1)} custom-call(s32[4]{0:T(128)S(1)} %pad_add_fusion.c, bf16[512,2048]{1,0:T(8,128)(2,1)S(1)} %bitcast.75, bf16[512,2048]{1,0:T(8,128)(2,1)S(1)} %collective-permute-done.t.tp), custom_call_target="tpu_custom_call" | custom-call | flops 1000000 | bytes 8388608 | tf_op jit(solution)/shard_map/pallas_call | solution.py:45
  28.9 3.0 %collective-permute-done.5.y3 = bf16[512,128]{1,0:T(8,128)(2,1)S(1)} collective-permute-done((bf16[512,128]{1,0:T(8,128)(2,1)S(1)}, bf16[512,128]{1,0:T(8,128)(2,1)S(1)}, u32[]{:S(2)}, u32[]{:S(2)}) %collective-permute-start.5) | collective-permute-done | bytes 131104 | tf_op jit(solution)/shard_map/ppermute | solution.py:442
  31.9 3.7 %shard_map.96 = (bf16[512,512]{1,0:T(8,128)(2,1)S(1)}, bf16[512,512]{1,0:T(8,128)(2,1)S(1)}, bf16[1024,512]{1,0:T(8,128)(2,1)S(1)}, bf16[512,128]{1,0:T(8,128)(2...) custom-call(s32[4]{0:T(128)S(1)} %pad_add_fusion.c, ...), custom_call_target="tpu_custom_call" | custom-call | flops 1000000 | bytes 1000 | tf_op jit(solution)/shard_map/pallas_call | solution.py:63
  36.8 2.2 %collective-permute-start.10 = (bf16[512,128]{1,0:T(8,128)(2,1)S(1)}, bf16[512,128]{1,0:T(8,128)(2,1)S(1)}, u32[]{:S(2)}, u32[]{:S(2)}) collective-permute-start(bf16[512,128]{1,0:T(8,128)(2,1)S(1)} %get-tuple-element.116), channel_id=1, source_target_pairs={{0,16},{8,24},{16,0},{24,8},{1,17},{9,25},{17,1},{25,9},{2,18},{10... | collective-permute-start | bytes 393224 | tf_op jit(solution)/shard_map/ppermute | solution.py:442
  40.5 3.9 %shard_map.97.g.refs_0_ = bf16[1024,512]{1,0:T(8,128)(2,1)S(1)} custom-call(s32[4]{0:T(128)S(1)} %pad_add_fusion.c, bf16[512,512]{1,0:T(8,128)(2,1)S(1)} %get-tuple-element.95.ko, bf16[512,512]{1,0:T(8,128)(2,1)S(1)} %get-tuple-element.97.kp, bf16[512,512]{1,0:T(8,128)(2,1)S(1)} %get-tuple-element.96.vo, bf16[512,512]{1,0:T(8,128)(2,1)S(1)} %get-tuple-element.98.vp, ...), custom_call_target="tpu_custom_call" | custom-call | flops 1000000 | bytes 1000 | tf_op jit(solution)/shard_map/pallas_call | solution.py:63
  44.4 3.4 %shard_map.98 = bf16[4,4,4,32,512]{4,3,2,1,0:T(8,128)(2,1)S(1)} custom-call(s32[4]{0:T(128)S(1)} %pad_add_fusion.c, bf16[4,4,128,1024]{3,2,1,0:T(8,128)(2,1)S(1)} %bitcast.68, bf16[1024,512]{1,0:T(8,128)(2,1)S(1)} %shard_map.97.g.refs_0_), custom_call_target="tpu_custom_call" | custom-call | flops 1000000 | bytes 1000 | tf_op jit(solution)/shard_map/pallas_call | solution.py:63
  48.0 2.2 %collective-permute-start.16 = (bf16[2,4,32,512]{3,2,1,0:T(8,128)(2,1)S(1)}, bf16[2,4,32,512]{3,2,1,0:T(8,128)(2,1)S(1)}, u32[]{:S(2)}, u32[]{:S(2)}) collective-permute-start(bf16[2,4,32,512]{3,2,1,0:T(8,128)(2,1)S(1)} %get-tuple-element.177), channel_id=1, source_target_pairs={{0,24},{8,0},{16,8},{24,16},{1,25},{9,1},{17,9},{25,17},{2,26},{10... | collective-permute-start | bytes 786440 | tf_op jit(solution)/shard_map/ppermute | solution.py:442
  50.2 2.3 %collective-permute-start.14 = (bf16[512,128]{1,0:T(8,128)(2,1)S(1)}, bf16[512,128]{1,0:T(8,128)(2,1)S(1)}, u32[]{:S(2)}, u32[]{:S(2)}) collective-permute-start(bf16[512,128]{1,0:T(8,128)(2,1)S(1)} %add_convert_fusion.6), channel_id=1, source_target_pairs={{0,64},{32,96},{64,0},{96,32},{1,65},{33,97},{65,1},{97,33},{2,66}... | collective-permute-start | bytes 393224 | tf_op jit(solution)/shard_map/ppermute | solution.py:442
  54.0 5.3 %shard_map.99 = (f32[1024,512]{1,0:T(8,128)S(1)}, f32[1024,512]{1,0:T(8,128)S(1)}) custom-call(s32[4]{0:T(128)S(1)} %pad_add_fusion.c, bf16[512,512]{1,0:T(8,128)(2,1)S(1)} %get-tuple-element.108.qo, bf16[512,512]{1,0:T(8,128)(2,1)S(1)} %get-tuple-element.109.qp, bf16[512,512]{1,0:T(8,128)(2,1)S(1)} %get-tuple-element.95.ko, ...), custom_call_target="tpu_custom_call" | custom-call | flops 1000000 | bytes 1000 | tf_op jit(solution)/shard_map/pallas_call | solution.py:63
  59.9 2.7 %collective-permute-start.21 = (bf16[4,4,32,512]{3,2,1,0:T(8,128)(2,1)S(1)}, bf16[4,4,32,512]{3,2,1,0:T(8,128)(2,1)S(1)}, u32[]{:S(2)}, u32[]{:S(2)}) collective-permute-start(bf16[4,4,32,512]{3,2,1,0:T(8,128)(2,1)S(1)} %pad_maximum_fusion.3), channel_id=1, source_target_pairs={{0,24},{8,0},{16,8},{24,16},{1,25},{9,1},{17,9},{25,17},{2,26},{10... | collective-permute-start | bytes 1572872 | tf_op jit(solution)/shard_map/ppermute | solution.py:442
  64.0 1.8 %shard_map.101 = (bf16[4,4,32,512]{3,2,1,0:T(8,128)(2,1)S(1)}, bf16[4,4,32,512]{3,2,1,0:T(8,128)(2,1)S(1)}) custom-call(s32[4]{0:T(128)S(1)} %pad_add_fusion.c, bf16[4,4,128,1024]{3,2,1,0:T(8,128)(2,1)S(1)} %bitcast.69, bf16[1024,512]{1,0:T(8,128)(2,1)S(1)} %get-tuple-element.154.refs_0_.refs_1_, bf16[1024,512]{1,0:T(8,128)(2,1)S(1)} %get-tuple-element.155.refs_1_.refs_2_.refs_3_), custom_call_target="tpu_custom_call" | custom-call | flops 1000000 | bytes 1000 | tf_op jit(solution)/shard_map/pallas_call | solution.py:63
  68.1 1.5 %shard_map.105 = bf16[512,1024]{1,0:T(8,128)(2,1)} custom-call(s32[4]{0:T(128)S(1)} %pad_add_fusion.c, bf16[512,512]{1,0:T(8,128)(2,1)S(1)} %get-tuple-element.145.o, bf16[512,512]{1,0:T(8,128)(2,1)S(1)} %collective-permute-done.11.r), custom_call_target="tpu_custom_call" | custom-call | flops 1000000 | bytes 1000 | tf_op jit(solution)/shard_map/pallas_call | solution.py:63
  69.7 1.8 %shard_map.103 = (bf16[4,4,32,512]{3,2,1,0:T(8,128)(2,1)S(1)}, bf16[4,4,32,512]{3,2,1,0:T(8,128)(2,1)S(1)}) custom-call(s32[4]{0:T(128)S(1)} %pad_add_fusion.c, bf16[4,4,128,1024]{3,2,1,0:T(8,128)(2,1)S(1)} %bitcast.70, bf16[1024,512]{1,0:T(8,128)(2,1)S(1)} %get-tuple-element.154.refs_0_.refs_1_, bf16[1024,512]{1,0:T(8,128)(2,1)S(1)} %get-tuple-element.155.refs_1_.refs_2_.refs_3_), custom_call_target="tpu_custom_call" | custom-call | flops 1000000 | bytes 1000 | tf_op jit(solution)/shard_map/pallas_call | solution.py:63
  71.5 2.9 %shard_map.102 = (bf16[4,4,32,512]{3,2,1,0:T(8,128)(2,1)S(1)}, bf16[4,4,32,512]{3,2,1,0:T(8,128)(2,1)S(1)}, bf16[4,4,32,512]{3,2,1,0:T(8,128)(2,1)S(1)}, bf16[4,4,32,512]{3,2,1,0:T(8,128)(2,1)S(1)}) custom-call(s32[4]{0:T(128)S(1)} %pad_add_fusion.c, bf16[4,4,128,1024]{3,2,1,0:T(8,128)(2,1)S(1)} %bitcast.71, ...), custom_call_target="tpu_custom_call" | custom-call | flops 1000000 | bytes 1000 | tf_op jit(solution)/shard_map/pallas_call | solution.py:63
  74.3 4.6 %shard_map.104 = bf16[512,2048]{1,0:T(8,128)(2,1)S(1)} custom-call(s32[4]{0:T(128)S(1)} %pad_add_fusion.c, bf16[1024,512]{1,0:T(8,128)(2,1)S(1)} %shard_map.97.g.refs_0_, bf16[1024,512]{1,0:T(8,128)(2,1)S(1)} %get-tuple-element.154.refs_0_.refs_1_, bf16[1024,512]{1,0:T(8,128)(2,1)S(1)} %get-tuple-element.155.refs_1_.refs_2_.refs_3_, ...), custom_call_target="tpu_custom_call" | custom-call | flops 1000000 | bytes 1000 | tf_op jit(solution)/shard_map/pallas_call | solution.py:63
  79.0 3.1 %collective-permute-start.22 = (bf16[512,2048]{1,0:T(8,128)(2,1)S(1)}, bf16[512,2048]{1,0:T(8,128)(2,1)S(1)}, u32[]{:S(2)}, u32[]{:S(2)}) collective-permute-start(bf16[512,2048]{1,0:T(8,128)(2,1)S(1)} %shard_map.104), channel_id=1, source_target_pairs={{0,4},{4,0},{1,5},{5,1},{2,6},{6,2},{3,7},{7,3},{8,12},{12,8},{9,1... | collective-permute-start | bytes 6291464 | tf_op jit(solution)/shard_map/ppermute | solution.py:446
  82.2 3.0 %collective-permute-start.24 = (bf16[4,4,32,512]{3,2,1,0:T(8,128)(2,1)S(1)}, bf16[4,4,32,512]{3,2,1,0:T(8,128)(2,1)S(1)}, u32[]{:S(2)}, u32[]{:S(2)}) collective-permute-start(bf16[4,4,32,512]{3,2,1,0:T(8,128)(2,1)S(1)} %pad_maximum_fusion.5), channel_id=1, source_target_pairs={{0,24},{8,0},{16,8},{24,16},{1,25},{9,1},{17,9},{25,17},{2,26},{10... | collective-permute-start | bytes 1572872 | tf_op jit(solution)/shard_map/ppermute | solution.py:442
  86.3 2.4 %collective-permute-start.26 = (bf16[18,32,512]{2,1,0:T(8,128)(2,1)S(1)}, bf16[18,32,512]{2,1,0:T(8,128)(2,1)S(1)}, u32[]{:S(2)}, u32[]{:S(2)}) collective-permute-start(bf16[18,32,512]{2,1,0:T(8,128)(2,1)S(1)} %pad_maximum_fusion.1), channel_id=1, source_target_pairs={{0,96},{32,0},{64,32},{96,64},{1,97},{33,1},{65,33},{97,65},{2,98}... | collective-permute-start | bytes 1769480 | tf_op jit(solution)/shard_map/ppermute | solution.py:442
  89.1 5.4 %shard_map.106 = bf16[512,2048]{1,0:T(8,128)(2,1)} custom-call(s32[4]{0:T(128)S(1)} %pad_add_fusion.c, bf16[1024,512]{1,0:T(8,128)(2,1)S(1)} %shard_map.97.g.refs_0_, bf16[1024,512]{1,0:T(8,128)(2,1)S(1)} %get-tuple-element.154.refs_0_.refs_1_, bf16[1024,512]{1,0:T(8,128)(2,1)S(1)} %get-tuple-element.155.refs_1_.refs_2_.refs_3_, ...), custom_call_target="tpu_custom_call" | custom-call | flops 1000000 | bytes 1000 | tf_op jit(solution)/shard_map/pallas_call | solution.py:63
  94.5 2.1 %collective-permute-done.24 = bf16[4,4,32,512]{3,2,1,0:T(8,128)(2,1)S(1)} collective-permute-done((bf16[4,4,32,512]{3,2,1,0:T(8,128)(2,1)S(1)}, bf16[4,4,32,512]{3,2,1,0:T(8,128)(2,1)S(1)}, u32[]{:S(2)}, u32[]{:S(2)}) %collective-permute-start.24) | collective-permute-done | bytes 524320 | tf_op jit(solution)/shard_map/ppermute | solution.py:442
  96.6 6.3 %collective-permute-done.23 = bf16[4,4,32,512]{3,2,1,0:T(8,128)(2,1)S(1)} collective-permute-done((bf16[4,4,32,512]{3,2,1,0:T(8,128)(2,1)S(1)}, bf16[4,4,32,512]{3,2,1,0:T(8,128)(2,1)S(1)}, u32[]{:S(2)}, u32[]{:S(2)}) %collective-permute-start.23) | collective-permute-done | bytes 524320 | tf_op jit(solution)/shard_map/ppermute | solution.py:442
  106.8 3.5 %collective-permute-done.30 = bf16[4,32,512]{2,1,0:T(8,128)(2,1)S(1)} collective-permute-done((bf16[4,32,512]{2,1,0:T(8,128)(2,1)S(1)}, bf16[4,32,512]{2,1,0:T(8,128)(2,1)S(1)}, u32[]{:S(2)}, u32[]{:S(2)}) %collective-permute-start.30) | collective-permute-done | bytes 131104 | tf_op jit(solution)/shard_map/ppermute | solution.py:442
  113.5 3.4 %collective-permute-done.29 = bf16[4,32,512]{2,1,0:T(8,128)(2,1)S(1)} collective-permute-done((bf16[4,32,512]{2,1,0:T(8,128)(2,1)S(1)}, bf16[4,32,512]{2,1,0:T(8,128)(2,1)S(1)}, u32[]{:S(2)}, u32[]{:S(2)}) %collective-permute-start.29) | collective-permute-done | bytes 131104 | tf_op jit(solution)/shard_map/ppermute | solution.py:442
  117.0 3.7 %collective-permute-start.33 = (bf16[32,1536]{1,0:T(8,128)(2,1)S(1)}, bf16[32,1536]{1,0:T(8,128)(2,1)S(1)}, u32[]{:S(2)}, u32[]{:S(2)}) collective-permute-start(bf16[32,1536]{1,0:T(8,128)(2,1)S(1)} %get-tuple-element.195), channel_id=1, source_target_pairs={{0,2},{1,3},{2,0},{3,1},{4,6},{5,7},{6,4},{7,5},{8,10},{9,11},{10,... | collective-permute-start | bytes 294920 | tf_op jit(solution)/shard_map/ppermute | solution.py:442
  122.7 1.8 %collective-permute-done.35 = bf16[32,1536]{1,0:T(8,128)(2,1)S(1)} collective-permute-done((bf16[32,1536]{1,0:T(8,128)(2,1)S(1)}, bf16[32,1536]{1,0:T(8,128)(2,1)S(1)}, u32[]{:S(2)}, u32[]{:S(2)}) %collective-permute-start.35) | collective-permute-done | bytes 98336 | tf_op jit(solution)/shard_map/ppermute | solution.py:442
  124.5 2.3 %collective-permute-done.34 = bf16[32,1536]{1,0:T(8,128)(2,1)S(1)} collective-permute-done((bf16[32,1536]{1,0:T(8,128)(2,1)S(1)}, bf16[32,1536]{1,0:T(8,128)(2,1)S(1)}, u32[]{:S(2)}, u32[]{:S(2)}) %collective-permute-start.34) | collective-permute-done | bytes 98336 | tf_op jit(solution)/shard_map/ppermute | solution.py:442
  126.9 4.3 %collective-permute-start.36 = (bf16[16,1536]{1,0:T(8,128)(2,1)S(1)}, bf16[16,1536]{1,0:T(8,128)(2,1)S(1)}, u32[]{:S(2)}, u32[]{:S(2)}) collective-permute-start(bf16[16,1536]{1,0:T(8,128)(2,1)S(1)} %slice_select_fusion), channel_id=1, source_target_pairs={{0,4},{4,0},{1,5},{5,1},{2,6},{6,2},{3,7},{7,3},{8,12},{12,8},{9,1... | collective-permute-start | bytes 147464 | tf_op jit(solution)/shard_map/ppermute | solution.py:446
  (96 shorter events, 27.0 us)
Async XLA Ops:
  0.6 7.2 %collective-permute-start = (bf16[512,2048]{1,0:T(8,128)(2,1)}, bf16[512,2048]{1,0:T(8,128)(2,1)S(1)}, u32[]{:S(2)}, u32[]{:S(2)}) collective-permute-start(bf16[512,2048]{1,0:T(8,128)(2,1)} %bitcast.72), channel_id=1, source_target_pairs={{0,4},{4,0},{1,5},{5,1},{2,6},{6,2},{3,7},{7,3},{8,12},{12,8},{9,1... | collective-permute-start | bytes 6291464 | tf_op jit(solution)/shard_map/ppermute | solution.py:446
  11.1 10.0 %collective-permute-start.3 = (bf16[512,128]{1,0:T(8,128)(2,1)S(1)}, bf16[512,128]{1,0:T(8,128)(2,1)S(1)}, u32[]{:S(2)}, u32[]{:S(2)}) collective-permute-start(bf16[512,128]{1,0:T(8,128)(2,1)S(1)} %get-tuple-element.93), channel_id=1, source_target_pairs={{0,16},{8,24},{16,0},{24,8},{1,17},{9,25},{17,1},{25,9},{2,18},{10... | collective-permute-start | bytes 393224 | tf_op jit(solution)/shard_map/ppermute | solution.py:442
  14.0 7.1 %collective-permute-start.2 = (bf16[512,128]{1,0:T(8,128)(2,1)S(1)}, bf16[512,128]{1,0:T(8,128)(2,1)S(1)}, u32[]{:S(2)}, u32[]{:S(2)}) collective-permute-start(bf16[512,128]{1,0:T(8,128)(2,1)S(1)} %get-tuple-element.93), channel_id=1, source_target_pairs={{0,24},{8,0},{16,8},{24,16},{1,25},{9,1},{17,9},{25,17},{2,26},{10... | collective-permute-start | bytes 393224 | tf_op jit(solution)/shard_map/ppermute | solution.py:442
  14.9 6.3 %collective-permute-start.1 = (bf16[512,128]{1,0:T(8,128)(2,1)S(1)}, bf16[512,128]{1,0:T(8,128)(2,1)S(1)}, u32[]{:S(2)}, u32[]{:S(2)}) collective-permute-start(bf16[512,128]{1,0:T(8,128)(2,1)S(1)} %get-tuple-element.93), channel_id=1, source_target_pairs={{0,8},{8,16},{16,24},{24,0},{1,9},{9,17},{17,25},{25,1},{2,10},{10... | collective-permute-start | bytes 393224 | tf_op jit(solution)/shard_map/ppermute | solution.py:442
  21.2 10.7 %collective-permute-start.7 = (bf16[512,512]{1,0:T(8,128)(2,1)S(1)}, bf16[512,512]{1,0:T(8,128)(2,1)S(1)}, u32[]{:S(2)}, u32[]{:S(2)}) collective-permute-start(bf16[512,512]{1,0:T(8,128)(2,1)S(1)} %get-tuple-element.105), channel_id=1, source_target_pairs={{0,4},{4,0},{1,5},{5,1},{2,6},{6,2},{3,7},{7,3},{8,12},{12,8},{9,1... | collective-permute-start | bytes 1572872 | tf_op jit(solution)/shard_map/ppermute | solution.py:446
  22.2 6.7 %collective-permute-start.6 = (bf16[512,128]{1,0:T(8,128)(2,1)S(1)}, bf16[512,128]{1,0:T(8,128)(2,1)S(1)}, u32[]{:S(2)}, u32[]{:S(2)}) collective-permute-start(bf16[512,128]{1,0:T(8,128)(2,1)S(1)} %add_convert_fusion.7), channel_id=1, source_target_pairs={{0,64},{32,96},{64,0},{96,32},{1,65},{33,97},{65,1},{97,33},{2,66}... | collective-permute-start | bytes 393224 | tf_op jit(solution)/shard_map/ppermute | solution.py:442
  25.1 6.8 %collective-permute-start.5 = (bf16[512,128]{1,0:T(8,128)(2,1)S(1)}, bf16[512,128]{1,0:T(8,128)(2,1)S(1)}, u32[]{:S(2)}, u32[]{:S(2)}) collective-permute-start(bf16[512,128]{1,0:T(8,128)(2,1)S(1)} %add_convert_fusion.7), channel_id=1, source_target_pairs={{0,96},{32,0},{64,32},{96,64},{1,97},{33,1},{65,33},{97,65},{2,98}... | collective-permute-start | bytes 393224 | tf_op jit(solution)/shard_map/ppermute | solution.py:442
  25.9 6.0 %collective-permute-start.4 = (bf16[512,128]{1,0:T(8,128)(2,1)S(1)}, bf16[512,128]{1,0:T(8,128)(2,1)S(1)}, u32[]{:S(2)}, u32[]{:S(2)}) collective-permute-start(bf16[512,128]{1,0:T(8,128)(2,1)S(1)} %add_convert_fusion.7), channel_id=1, source_target_pairs={{0,32},{32,64},{64,96},{96,0},{1,33},{33,65},{65,97},{97,1},{2,34}... | collective-permute-start | bytes 393224 | tf_op jit(solution)/shard_map/ppermute | solution.py:442
  35.6 12.3 %collective-permute-start.11 = (bf16[512,512]{1,0:T(8,128)(2,1)S(1)}, bf16[512,512]{1,0:T(8,128)(2,1)S(1)}, u32[]{:S(2)}, u32[]{:S(2)}) collective-permute-start(bf16[512,512]{1,0:T(8,128)(2,1)S(1)} %get-tuple-element.120), channel_id=1, source_target_pairs={{0,4},{4,0},{1,5},{5,1},{2,6},{6,2},{3,7},{7,3},{8,12},{12,8},{9,1... | collective-permute-start | bytes 1572872 | tf_op jit(solution)/shard_map/ppermute | solution.py:446
  36.8 11.0 %collective-permute-start.10 = (bf16[512,128]{1,0:T(8,128)(2,1)S(1)}, bf16[512,128]{1,0:T(8,128)(2,1)S(1)}, u32[]{:S(2)}, u32[]{:S(2)}) collective-permute-start(bf16[512,128]{1,0:T(8,128)(2,1)S(1)} %get-tuple-element.116), channel_id=1, source_target_pairs={{0,16},{8,24},{16,0},{24,8},{1,17},{9,25},{17,1},{25,9},{2,18},{10... | collective-permute-start | bytes 393224 | tf_op jit(solution)/shard_map/ppermute | solution.py:442
  39.0 8.8 %collective-permute-start.9 = (bf16[512,128]{1,0:T(8,128)(2,1)S(1)}, bf16[512,128]{1,0:T(8,128)(2,1)S(1)}, u32[]{:S(2)}, u32[]{:S(2)}) collective-permute-start(bf16[512,128]{1,0:T(8,128)(2,1)S(1)} %get-tuple-element.116), channel_id=1, source_target_pairs={{0,24},{8,0},{16,8},{24,16},{1,25},{9,1},{17,9},{25,17},{2,26},{10... | collective-permute-start | bytes 393224 | tf_op jit(solution)/shard_map/ppermute | solution.py:442
  40.0 7.8 %collective-permute-start.8 = (bf16[512,128]{1,0:T(8,128)(2,1)S(1)}, bf16[512,128]{1,0:T(8,128)(2,1)S(1)}, u32[]{:S(2)}, u32[]{:S(2)}) collective-permute-start(bf16[512,128]{1,0:T(8,128)(2,1)S(1)} %get-tuple-element.116), channel_id=1, source_target_pairs={{0,8},{8,16},{16,24},{24,0},{1,9},{9,17},{17,25},{25,1},{2,10},{10... | collective-permute-start | bytes 393224 | tf_op jit(solution)/shard_map/ppermute | solution.py:442
  48.0 11.5 %collective-permute-start.16 = (bf16[2,4,32,512]{3,2,1,0:T(8,128)(2,1)S(1)}, bf16[2,4,32,512]{3,2,1,0:T(8,128)(2,1)S(1)}, u32[]{:S(2)}, u32[]{:S(2)}) collective-permute-start(bf16[2,4,32,512]{3,2,1,0:T(8,128)(2,1)S(1)} %get-tuple-element.177), channel_id=1, source_target_pairs={{0,24},{8,0},{16,8},{24,16},{1,25},{9,1},{17,9},{25,17},{2,26},{10... | collective-permute-start | bytes 786440 | tf_op jit(solution)/shard_map/ppermute | solution.py:442
  50.2 9.3 %collective-permute-start.15 = (bf16[2,4,32,512]{3,2,1,0:T(8,128)(2,1)S(1)}, bf16[2,4,32,512]{3,2,1,0:T(8,128)(2,1)S(1)}, u32[]{:S(2)}, u32[]{:S(2)}) collective-permute-start(bf16[2,4,32,512]{3,2,1,0:T(8,128)(2,1)S(1)} %get-tuple-element.178), channel_id=1, source_target_pairs={{0,8},{8,16},{16,24},{24,0},{1,9},{9,17},{17,25},{25,1},{2,10},{10... | collective-permute-start | bytes 786440 | tf_op jit(solution)/shard_map/ppermute | solution.py:442
  50.2 9.1 %collective-permute-start.14 = (bf16[512,128]{1,0:T(8,128)(2,1)S(1)}, bf16[512,128]{1,0:T(8,128)(2,1)S(1)}, u32[]{:S(2)}, u32[]{:S(2)}) collective-permute-start(bf16[512,128]{1,0:T(8,128)(2,1)S(1)} %add_convert_fusion.6), channel_id=1, source_target_pairs={{0,64},{32,96},{64,0},{96,32},{1,65},{33,97},{65,1},{97,33},{2,66}... | collective-permute-start | bytes 393224 | tf_op jit(solution)/shard_map/ppermute | solution.py:442
  52.5 6.8 %collective-permute-start.13 = (bf16[512,128]{1,0:T(8,128)(2,1)S(1)}, bf16[512,128]{1,0:T(8,128)(2,1)S(1)}, u32[]{:S(2)}, u32[]{:S(2)}) collective-permute-start(bf16[512,128]{1,0:T(8,128)(2,1)S(1)} %add_convert_fusion.6), channel_id=1, source_target_pairs={{0,96},{32,0},{64,32},{96,64},{1,97},{33,1},{65,33},{97,65},{2,98}... | collective-permute-start | bytes 393224 | tf_op jit(solution)/shard_map/ppermute | solution.py:442
  53.4 6.1 %collective-permute-start.12 = (bf16[512,128]{1,0:T(8,128)(2,1)S(1)}, bf16[512,128]{1,0:T(8,128)(2,1)S(1)}, u32[]{:S(2)}, u32[]{:S(2)}) collective-permute-start(bf16[512,128]{1,0:T(8,128)(2,1)S(1)} %add_convert_fusion.6), channel_id=1, source_target_pairs={{0,32},{32,64},{64,96},{96,0},{1,33},{33,65},{65,97},{97,1},{2,34}... | collective-permute-start | bytes 393224 | tf_op jit(solution)/shard_map/ppermute | solution.py:442
  59.8 19.2 %collective-permute-start.20 = (bf16[4,4,32,512]{3,2,1,0:T(8,128)(2,1)S(1)}, bf16[4,4,32,512]{3,2,1,0:T(8,128)(2,1)S(1)}, u32[]{:S(2)}, u32[]{:S(2)}) collective-permute-start(bf16[4,4,32,512]{3,2,1,0:T(8,128)(2,1)S(1)} %pad_maximum_fusion.2), channel_id=1, source_target_pairs={{0,8},{8,16},{16,24},{24,0},{1,9},{9,17},{17,25},{25,1},{2,10},{10... | collective-permute-start | bytes 1572872 | tf_op jit(solution)/shard_map/ppermute | solution.py:442
  59.9 19.0 %collective-permute-start.21 = (bf16[4,4,32,512]{3,2,1,0:T(8,128)(2,1)S(1)}, bf16[4,4,32,512]{3,2,1,0:T(8,128)(2,1)S(1)}, u32[]{:S(2)}, u32[]{:S(2)}) collective-permute-start(bf16[4,4,32,512]{3,2,1,0:T(8,128)(2,1)S(1)} %pad_maximum_fusion.3), channel_id=1, source_target_pairs={{0,24},{8,0},{16,8},{24,16},{1,25},{9,1},{17,9},{25,17},{2,26},{10... | collective-permute-start | bytes 1572872 | tf_op jit(solution)/shard_map/ppermute | solution.py:442
  65.8 13.2 %collective-permute-start.19 = (bf16[4,4,32,512]{3,2,1,0:T(8,128)(2,1)S(1)}, bf16[4,4,32,512]{3,2,1,0:T(8,128)(2,1)S(1)}, u32[]{:S(2)}, u32[]{:S(2)}) collective-permute-start(bf16[4,4,32,512]{3,2,1,0:T(8,128)(2,1)S(1)} %get-tuple-element.148), channel_id=1, source_target_pairs={{0,32},{32,64},{64,96},{96,0},{1,33},{33,65},{65,97},{97,1},{2,34}... | collective-permute-start | bytes 1572872 | tf_op jit(solution)/shard_map/ppermute | solution.py:442
  66.6 12.3 %collective-permute-start.18 = (bf16[2,4,32,512]{3,2,1,0:T(8,128)(2,1)S(1)}, bf16[2,4,32,512]{3,2,1,0:T(8,128)(2,1)S(1)}, u32[]{:S(2)}, u32[]{:S(2)}) collective-permute-start(bf16[2,4,32,512]{3,2,1,0:T(8,128)(2,1)S(1)} %get-tuple-element.193), channel_id=1, source_target_pairs={{0,24},{8,0},{16,8},{24,16},{1,25},{9,1},{17,9},{25,17},{2,26},{10... | collective-permute-start | bytes 786440 | tf_op jit(solution)/shard_map/ppermute | solution.py:442
  67.8 11.1 %collective-permute-start.17 = (bf16[2,4,32,512]{3,2,1,0:T(8,128)(2,1)S(1)}, bf16[2,4,32,512]{3,2,1,0:T(8,128)(2,1)S(1)}, u32[]{:S(2)}, u32[]{:S(2)}) collective-permute-start(bf16[2,4,32,512]{3,2,1,0:T(8,128)(2,1)S(1)} %get-tuple-element.194), channel_id=1, source_target_pairs={{0,8},{8,16},{16,24},{24,0},{1,9},{9,17},{17,25},{25,1},{2,10},{10... | collective-permute-start | bytes 786440 | tf_op jit(solution)/shard_map/ppermute | solution.py:442
  79.0 10.1 %collective-permute-start.22 = (bf16[512,2048]{1,0:T(8,128)(2,1)S(1)}, bf16[512,2048]{1,0:T(8,128)(2,1)S(1)}, u32[]{:S(2)}, u32[]{:S(2)}) collective-permute-start(bf16[512,2048]{1,0:T(8,128)(2,1)S(1)} %shard_map.104), channel_id=1, source_target_pairs={{0,4},{4,0},{1,5},{5,1},{2,6},{6,2},{3,7},{7,3},{8,12},{12,8},{9,1... | collective-permute-start | bytes 6291464 | tf_op jit(solution)/shard_map/ppermute | solution.py:446
  82.2 14.3 %collective-permute-start.24 = (bf16[4,4,32,512]{3,2,1,0:T(8,128)(2,1)S(1)}, bf16[4,4,32,512]{3,2,1,0:T(8,128)(2,1)S(1)}, u32[]{:S(2)}, u32[]{:S(2)}) collective-permute-start(bf16[4,4,32,512]{3,2,1,0:T(8,128)(2,1)S(1)} %pad_maximum_fusion.5), channel_id=1, source_target_pairs={{0,24},{8,0},{16,8},{24,16},{1,25},{9,1},{17,9},{25,17},{2,26},{10... | collective-permute-start | bytes 1572872 | tf_op jit(solution)/shard_map/ppermute | solution.py:442
  85.7 17.1 %collective-permute-start.25 = (bf16[18,32,512]{2,1,0:T(8,128)(2,1)S(1)}, bf16[18,32,512]{2,1,0:T(8,128)(2,1)S(1)}, u32[]{:S(2)}, u32[]{:S(2)}) collective-permute-start(bf16[18,32,512]{2,1,0:T(8,128)(2,1)S(1)} %pad_maximum_fusion), channel_id=1, source_target_pairs={{0,32},{32,64},{64,96},{96,0},{1,33},{33,65},{65,97},{97,1},{2,34}... | collective-permute-start | bytes 1769480 | tf_op jit(solution)/shard_map/ppermute | solution.py:442
  86.3 16.6 %collective-permute-start.26 = (bf16[18,32,512]{2,1,0:T(8,128)(2,1)S(1)}, bf16[18,32,512]{2,1,0:T(8,128)(2,1)S(1)}, u32[]{:S(2)}, u32[]{:S(2)}) collective-permute-start(bf16[18,32,512]{2,1,0:T(8,128)(2,1)S(1)} %pad_maximum_fusion.1), channel_id=1, source_target_pairs={{0,96},{32,0},{64,32},{96,64},{1,97},{33,1},{65,33},{97,65},{2,98}... | collective-permute-start | bytes 1769480 | tf_op jit(solution)/shard_map/ppermute | solution.py:442
  88.7 14.1 %collective-permute-start.23 = (bf16[4,4,32,512]{3,2,1,0:T(8,128)(2,1)S(1)}, bf16[4,4,32,512]{3,2,1,0:T(8,128)(2,1)S(1)}, u32[]{:S(2)}, u32[]{:S(2)}) collective-permute-start(bf16[4,4,32,512]{3,2,1,0:T(8,128)(2,1)S(1)} %pad_maximum_fusion.4), channel_id=1, source_target_pairs={{0,8},{8,16},{16,24},{24,0},{1,9},{9,17},{17,25},{25,1},{2,10},{10... | collective-permute-start | bytes 1572872 | tf_op jit(solution)/shard_map/ppermute | solution.py:442
  103.5 9.1 %collective-permute-start.28 = (bf16[2,4,32,512]{3,2,1,0:T(8,128)(2,1)S(1)}, bf16[2,4,32,512]{3,2,1,0:T(8,128)(2,1)S(1)}, u32[]{:S(2)}, u32[]{:S(2)}) collective-permute-start(bf16[2,4,32,512]{3,2,1,0:T(8,128)(2,1)S(1)} %pad_maximum_fusion.8), channel_id=1, source_target_pairs={{0,96},{32,0},{64,32},{96,64},{1,97},{33,1},{65,33},{97,65},{2,98}... | collective-permute-start | bytes 786440 | tf_op jit(solution)/shard_map/ppermute | solution.py:442
  105.0 6.0 %collective-permute-start.32 = (bf16[4,32,512]{2,1,0:T(8,128)(2,1)S(1)}, bf16[4,32,512]{2,1,0:T(8,128)(2,1)S(1)}, u32[]{:S(2)}, u32[]{:S(2)}) collective-permute-start(bf16[4,32,512]{2,1,0:T(8,128)(2,1)S(1)} %get-tuple-element.189), channel_id=1, source_target_pairs={{0,24},{8,0},{16,8},{24,16},{1,25},{9,1},{17,9},{25,17},{2,26},{10... | collective-permute-start | bytes 393224 | tf_op jit(solution)/shard_map/ppermute | solution.py:442
  106.3 6.3 %collective-permute-start.31 = (bf16[4,32,512]{2,1,0:T(8,128)(2,1)S(1)}, bf16[4,32,512]{2,1,0:T(8,128)(2,1)S(1)}, u32[]{:S(2)}, u32[]{:S(2)}) collective-permute-start(bf16[4,32,512]{2,1,0:T(8,128)(2,1)S(1)} %get-tuple-element.190), channel_id=1, source_target_pairs={{0,8},{8,16},{16,24},{24,0},{1,9},{9,17},{17,25},{25,1},{2,10},{10... | collective-permute-start | bytes 393224 | tf_op jit(solution)/shard_map/ppermute | solution.py:442
  106.6 6.8 %collective-permute-start.27 = (bf16[2,4,32,512]{3,2,1,0:T(8,128)(2,1)S(1)}, bf16[2,4,32,512]{3,2,1,0:T(8,128)(2,1)S(1)}, u32[]{:S(2)}, u32[]{:S(2)}) collective-permute-start(bf16[2,4,32,512]{3,2,1,0:T(8,128)(2,1)S(1)} %pad_maximum_fusion.7), channel_id=1, source_target_pairs={{0,32},{32,64},{64,96},{96,0},{1,33},{33,65},{65,97},{97,1},{2,34}... | collective-permute-start | bytes 786440 | tf_op jit(solution)/shard_map/ppermute | solution.py:442
  110.4 6.5 %collective-permute-start.29 = (bf16[4,32,512]{2,1,0:T(8,128)(2,1)S(1)}, bf16[4,32,512]{2,1,0:T(8,128)(2,1)S(1)}, u32[]{:S(2)}, u32[]{:S(2)}) collective-permute-start(bf16[4,32,512]{2,1,0:T(8,128)(2,1)S(1)} %get-tuple-element.182), channel_id=1, source_target_pairs={{0,64},{32,96},{64,0},{96,32},{1,65},{33,97},{65,1},{97,33},{2,66}... | collective-permute-start | bytes 393224 | tf_op jit(solution)/shard_map/ppermute | solution.py:442
  (6 other events, 33.5 us)
where the time goes:
time: 133 us
  Pallas kernels  53.6 us (40%)
  starting transfers between devices  49.7 us (37%)
  waiting for transfers between devices  26.4 us (20%)
  other arithmetic  2.18 us (2%)
    pallas_call x15, Pallas kernels, local(): pl.pallas_call(kernel, out_shape=[jax.ShapeDtypeStruct(s, d) for s, d in...  51.3 us
    ppermute x32, starting transfers between devices, shift(): return lax.ppermute(v, axis, [(i, (i + d) % n) for i in range(n)])  38.7 us
    ppermute x32, waiting for transfers between devices, shift(): return lax.ppermute(v, axis, [(i, (i + d) % n) for i in range(n)])  25.5 us
    ppermute x5, starting transfers between devices, swap(): return lax.ppermute(v, 'c', [(0, 1), (1, 0)])  11 us
  transfers between devices with their start and end apart: 37, of which 12 were waited for; matrix products, arithmetic and copies ran while one was open for 1% of the time, Pallas kernels for 34%

commit v1 on v0

--- a/solution.py
+++ b/solution.py
@@ -34,6 +34,11 @@
 
 
 def each_head(body):
+    for h in range(4):
+        body(h)
+
+
+def looped_head(body):
     def step(h, carry):
         body(h)
         return carry
@@ -99,16 +104,21 @@
 
 def project_own(core, tok, wk, wv):
     def kernel(c, t, b, d, k, v, s, bh, dh, tv, sems):
-        copies = [pltpu.make_async_copy(t, tv, sems.at[0])]
-        copies.append(pltpu.make_async_copy(b.at[:, half_of(c[0])], bh, sems.at[1]))
-        copies.append(pltpu.make_async_copy(d.at[:, half_of(c[0])], dh, sems.at[2]))
-        for copy in copies:
+        copies = [[], [], []]
+        for i in range(4):
+            rows, part = pl.ds(i * 512, 512), pl.ds(i * 128, 128)
+            copies[0].append(pltpu.make_async_copy(t.at[part], tv.at[part], sems.at[0, i]))
+            for n, (src, dst) in enumerate(((b, bh), (d, dh))):
+                half = src.at[rows, half_of(c[0])]
+                copies[n + 1].append(pltpu.make_async_copy(half, dst.at[rows], sems.at[n + 1, i]))
+        for copy in sum(copies, []):
             copy.start()
-        copies[0].wait()
-        copies[1].wait()
-        k[...] = dot(tv[...], bh[...]).astype(BF)
-        copies[2].wait()
-        v[...] = dot(tv[...], dh[...]).astype(BF)
+        for copy in copies[0]:
+            copy.wait()
+        for n, (w, out) in enumerate(((bh, k), (dh, v))):
+            for copy in copies[n + 1]:
+                copy.wait()
+            out[...] = dot(tv[...], w[...]).astype(BF)
         for h in range(4):
             s[head(h), :] = dot(k[:, head(h)], v[:, head(h)], 0, 0).astype(BF)
 
@@ -119,7 +129,7 @@
         in_hbm(tok, wk, wv),
         [row] * 2 + [((512, DH), BF)] + [weight] * 2,
         hbm_in=3,
-        scratch=[pltpu.VMEM((TOK, 2048), BF), pltpu.SemaphoreType.DMA((3,))],
+        scratch=[pltpu.VMEM((TOK, 2048), BF), pltpu.SemaphoreType.DMA((3, 4))],
     )
 
 
@@ -276,7 +286,7 @@
 
 def grads_within(core, q_o, q_p, k_o, k_p, v_o, v_p, g):
     def kernel(c, qo, qp, ko, kp, vo, vp, gr, dk, dv):
-        @each_head
+        @looped_head
         def _(h):
             for n, (q, k, v) in enumerate(((qo, ko, vo), (qp, kp, vp))):
                 qh, kh, vh = q[:, head(h)], k[:, head(h)], v[:, head(h)]
@@ -327,13 +337,12 @@
                 rows = t[(c[1] + step) % 4]
             part = dot(rows.reshape(512, 2 * TOK), g[...]).astype(BF)
             for a in range(4):
-                at = (a - c[1] + 4) % 4 if axis == "x" else (a - c[2] + 4) % 4
+                near = (a - c[1] + 4) % 4 if axis == "x" else (a - c[2] + 4) % 4
                 for core_at in range(2):
                     for z in range(4):
                         row = a * 128 + core_at * 64 + z * 16
-                        out[at, (z - c[3] + 4) % 4, core_at * 16 : core_at * 16 + 16, :] = part[
-                            row : row + 16, :
-                        ]
+                        here = slice(core_at * 16, core_at * 16 + 16)
+                        out[near, (z - c[3] + 4) % 4, here, :] = part[row : row + 16, :]
 
     return local(
         kernel,
@@ -518,10 +527,9 @@
     came_k, came_v = ring_out(far_k, "x"), shift(far_v, "y", 1)
     near = weight_grad(core, tt, [(dk, "x", 1), (dk, "x", 3), (dv, "y", 1), (dv, "y", 3)])
     here_k, here_v = weight_grad(core, tt, [(dk, "x", 0), (dv, "y", 0)])
-    attn_out = joined_heads(core, a_o, a_r)
     ig_p = input_part(core, 1, (dq, dk, dv), weights)
-    *near, dk, dv, here_k, here_v, ig_p, attn_out, k0, k1, came_v, q0, q1 = together(
-        *near, dk, dv, here_k, here_v, ig_p, attn_out, *came_k, came_v, *last_q
+    *near, dk, dv, here_k, here_v, ig_p, a_o, k0, k1, came_v, q0, q1 = together(
+        *near, dk, dv, here_k, here_v, ig_p, a_o, *came_k, came_v, *last_q
     )
     last_k = ring_near(near[0], near[1], (k0, k1), "x")
     sum_q = f32_sum(part_q[0], q0, q1)
@@ -530,8 +538,11 @@
     down = jnp.concatenate([near[3].reshape(flat), sum_q[2, 2:]], axis=0)
     last_v = [shift(up, "y", 1), shift(down, "y", 3)]
     ig_r = swap(ig_p)
+    attn_out = joined_heads(core, a_o, a_r)
     input_grad = input_part(core, 0, (dq, dk, dv), weights, ig_r)
-    sum_q, input_grad, k0, k1, v0, v1 = together(sum_q, input_grad, *last_k, *last_v)
+    sum_q, input_grad, attn_out, k0, k1, v0, v1 = together(
+        sum_q, input_grad, attn_out, *last_k, *last_v
+    )
     sum_k = f32_sum(here_k, k0, k1)
     sum_v = f32_sum(here_v.reshape(flat), v0[:16], v1[:16]).reshape(4, 4, 32, 512)
     up_q = jnp.concatenate([f32_sum(sum_q[1, :2], v0[16:]), sum_q[1, 2:]], axis=0)

time: 133 us -> 131 us (0.985)
  Pallas kernels: 53.6 us -> 52 us
    ppermute x5, starting transfers between devices: 11 us -> 13 us  [swap(): return lax.ppermute(v, 'c', [(0, 1), (1, 0)])]
    pallas_call x15, Pallas kernels: 51.3 us -> 49.7 us  [local(): pl.pallas_call(kernel, out_shape=[jax.ShapeDtypeStruct(s, d) for s, d in...]
    ppermute x32, starting transfers between devices: 38.7 us -> 37.2 us  [shift(): return lax.ppermute(v, axis, [(i, (i + d) % n) for i in range(n)])]
  transfers between devices with their start and end apart: 37 -> 37, of which waited for: 12 -> 14; matrix products, arithmetic and copies ran while one was open for 1% -> 1% of each run, Pallas kernels for 34% -> 34%
where the time goes in v1:
time: 131 us
  Pallas kernels  52 us (40%)
  starting transfers between devices  50.2 us (38%)
  waiting for transfers between devices  25.1 us (19%)
  other arithmetic  2.18 us (2%)
    pallas_call x15, Pallas kernels, local(): pl.pallas_call(kernel, out_shape=[jax.ShapeDtypeStruct(s, d) for s, d in...  49.7 us
    ppermute x32, starting transfers between devices, shift(): return lax.ppermute(v, axis, [(i, (i + d) % n) for i in range(n)])  37.2 us
    ppermute x32, waiting for transfers between devices, shift(): return lax.ppermute(v, axis, [(i, (i + d) % n) for i in range(n)])  24.2 us
    ppermute x5, starting transfers between devices, swap(): return lax.ppermute(v, 'c', [(0, 1), (1, 0)])  13 us
  transfers between devices with their start and end apart: 37, of which 14 were waited for; matrix products, arithmetic and copies ran while one was open for 1% of the time, Pallas kernels for 34%

profile of v1, /device:TPU:1, one launch (start us, length us, event | category | flops | bytes accessed | tf_op | source)
XLA Modules:
  0.0 130.9 jit_solution(11517325907512286466)
XLA Ops:
  2.2 5.6 %shard_map.92 = (bf16[512,512]{1,0:T(8,128)(2,1)S(1)}, bf16[512,512]{1,0:T(8,128)(2,1)S(1)}, bf16[512,128]{1,0:T(8,128)(2,1)S(1)}, bf16[2048,512]{1,0:T(8,128)(2,1)S(1)}, bf16[2048,512]{1,0:T(8,128)(2,1)S(1)}) custom-call(s32[4]{0:T(128)S(1)} %pad_add_fusion.c, bf16[512,2048]{1,0:T(8,128)(2,1)} %bitcast.73, bf16[2048,1024]{1,0:T(8,128)(2,1)} %b.1, ...), custom_call_target="tpu_custom_call" | custom-call | flops 1000000 | bytes 1000 | tf_op jit(solution)/shard_map/pallas_call | solution.py:68
  7.9 3.2 %shard_map.93 = (bf16[512,512]{1,0:T(8,128)(2,1)S(1)}, bf16[512,512]{1,0:T(8,128)(2,1)S(1)}, bf16[512,128]{1,0:T(8,128)(2,1)S(1)}, bf16[512,128]{1,0:T(8,128)(2,1)S(1)}, bf16[2048,512]{1,0:T(8,128)(2,1)S(1)}) custom-call(s32[4]{0:T(128)S(1)} %pad_add_fusion.c, bf16[512,2048]{1,0:T(8,128)(2,1)S(1)} %collective-permute-done.t.tp, ...), custom_call_target="tpu_custom_call" | custom-call | flops 1000000 | bytes 1000 | tf_op jit(solution)/shard_map/pallas_call | solution.py:68
  11.1 2.9 %collective-permute-start.3 = (bf16[512,128]{1,0:T(8,128)(2,1)S(1)}, bf16[512,128]{1,0:T(8,128)(2,1)S(1)}, u32[]{:S(2)}, u32[]{:S(2)}) collective-permute-start(bf16[512,128]{1,0:T(8,128)(2,1)S(1)} %get-tuple-element.94), channel_id=1, source_target_pairs={{0,16},{8,24},{16,0},{24,8},{1,17},{9,25},{17,1},{25,9},{2,18},{10... | collective-permute-start | bytes 393224 | tf_op jit(solution)/shard_map/ppermute | solution.py:451
  15.5 5.5 %shard_map.94 = (bf16[512,512]{1,0:T(8,128)(2,1)S(1)}, bf16[512,512]{1,0:T(8,128)(2,1)S(1)}, f32[1024,512]{1,0:T(8,128)S(1)}, bf16[512,512]{1,0:T(8,128)(2,1)S(1)}, bf16[512,512]{1,0:T(8,128)(2,1)S(1)}) custom-call(s32[4]{0:T(128)S(1)} %pad_add_fusion.c, bf16[512,2048]{1,0:T(8,128)(2,1)S(1)} %bitcast.74, bf16[512,2048]{1,0:T(8,128)(2,1)S(1)} %collective-permute-done.t.tp, ...), custom_call_target="tpu_custom_call" | custom-call | flops 1000000 | bytes 1000 | tf_op jit(solution)/shard_map/pallas_call | solution.py:68
  22.2 2.9 %collective-permute-start.6 = (bf16[512,128]{1,0:T(8,128)(2,1)S(1)}, bf16[512,128]{1,0:T(8,128)(2,1)S(1)}, u32[]{:S(2)}, u32[]{:S(2)}) collective-permute-start(bf16[512,128]{1,0:T(8,128)(2,1)S(1)} %add_convert_fusion.7), channel_id=1, source_target_pairs={{0,64},{32,96},{64,0},{96,32},{1,65},{33,97},{65,1},{97,33},{2,66}... | collective-permute-start | bytes 393224 | tf_op jit(solution)/shard_map/ppermute | solution.py:451
  26.5 2.3 %shard_map.95 = bf16[2048,1024]{1,0:T(8,128)(2,1)S(1)} custom-call(s32[4]{0:T(128)S(1)} %pad_add_fusion.c, bf16[512,2048]{1,0:T(8,128)(2,1)S(1)} %bitcast.75, bf16[512,2048]{1,0:T(8,128)(2,1)S(1)} %collective-permute-done.t.tp), custom_call_target="tpu_custom_call" | custom-call | flops 1000000 | bytes 8388608 | tf_op jit(solution)/shard_map/pallas_call | solution.py:50
  28.9 3.0 %collective-permute-done.5.y3 = bf16[512,128]{1,0:T(8,128)(2,1)S(1)} collective-permute-done((bf16[512,128]{1,0:T(8,128)(2,1)S(1)}, bf16[512,128]{1,0:T(8,128)(2,1)S(1)}, u32[]{:S(2)}, u32[]{:S(2)}) %collective-permute-start.5) | collective-permute-done | bytes 131104 | tf_op jit(solution)/shard_map/ppermute | solution.py:451
  31.9 2.8 %shard_map.96 = (bf16[512,512]{1,0:T(8,128)(2,1)S(1)}, bf16[512,512]{1,0:T(8,128)(2,1)S(1)}, bf16[1024,512]{1,0:T(8,128)(2,1)S(1)}, bf16[512,128]{1,0:T(8,128)(2...) custom-call(s32[4]{0:T(128)S(1)} %pad_add_fusion.c, ...), custom_call_target="tpu_custom_call" | custom-call | flops 1000000 | bytes 1000 | tf_op jit(solution)/shard_map/pallas_call | solution.py:68
  35.9 2.3 %collective-permute-start.10 = (bf16[512,128]{1,0:T(8,128)(2,1)S(1)}, bf16[512,128]{1,0:T(8,128)(2,1)S(1)}, u32[]{:S(2)}, u32[]{:S(2)}) collective-permute-start(bf16[512,128]{1,0:T(8,128)(2,1)S(1)} %get-tuple-element.116), channel_id=1, source_target_pairs={{0,16},{8,24},{16,0},{24,8},{1,17},{9,25},{17,1},{25,9},{2,18},{10... | collective-permute-start | bytes 393224 | tf_op jit(solution)/shard_map/ppermute | solution.py:451
  39.6 3.3 %shard_map.97.g.refs_0_ = bf16[1024,512]{1,0:T(8,128)(2,1)S(1)} custom-call(s32[4]{0:T(128)S(1)} %pad_add_fusion.c, bf16[512,512]{1,0:T(8,128)(2,1)S(1)} %get-tuple-element.96.ko, bf16[512,512]{1,0:T(8,128)(2,1)S(1)} %get-tuple-element.98.kp, bf16[512,512]{1,0:T(8,128)(2,1)S(1)} %get-tuple-element.97.vo, bf16[512,512]{1,0:T(8,128)(2,1)S(1)} %get-tuple-element.99.vp, ...), custom_call_target="tpu_custom_call" | custom-call | flops 1000000 | bytes 1000 | tf_op jit(solution)/shard_map/pallas_call | solution.py:68
  43.0 3.4 %shard_map.98 = bf16[4,4,4,32,512]{4,3,2,1,0:T(8,128)(2,1)S(1)} custom-call(s32[4]{0:T(128)S(1)} %pad_add_fusion.c, bf16[4,4,128,1024]{3,2,1,0:T(8,128)(2,1)S(1)} %bitcast.68, bf16[1024,512]{1,0:T(8,128)(2,1)S(1)} %shard_map.97.g.refs_0_), custom_call_target="tpu_custom_call" | custom-call | flops 1000000 | bytes 1000 | tf_op jit(solution)/shard_map/pallas_call | solution.py:68
  46.6 2.2 %collective-permute-start.16 = (bf16[2,4,32,512]{3,2,1,0:T(8,128)(2,1)S(1)}, bf16[2,4,32,512]{3,2,1,0:T(8,128)(2,1)S(1)}, u32[]{:S(2)}, u32[]{:S(2)}) collective-permute-start(bf16[2,4,32,512]{3,2,1,0:T(8,128)(2,1)S(1)} %get-tuple-element.179), channel_id=1, source_target_pairs={{0,24},{8,0},{16,8},{24,16},{1,25},{9,1},{17,9},{25,17},{2,26},{10... | collective-permute-start | bytes 786440 | tf_op jit(solution)/shard_map/ppermute | solution.py:451
  48.8 2.3 %collective-permute-start.14 = (bf16[512,128]{1,0:T(8,128)(2,1)S(1)}, bf16[512,128]{1,0:T(8,128)(2,1)S(1)}, u32[]{:S(2)}, u32[]{:S(2)}) collective-permute-start(bf16[512,128]{1,0:T(8,128)(2,1)S(1)} %add_convert_fusion.6), channel_id=1, source_target_pairs={{0,64},{32,96},{64,0},{96,32},{1,65},{33,97},{65,1},{97,33},{2,66}... | collective-permute-start | bytes 393224 | tf_op jit(solution)/shard_map/ppermute | solution.py:451
  52.6 5.3 %shard_map.99 = (f32[1024,512]{1,0:T(8,128)S(1)}, f32[1024,512]{1,0:T(8,128)S(1)}) custom-call(s32[4]{0:T(128)S(1)} %pad_add_fusion.c, bf16[512,512]{1,0:T(8,128)(2,1)S(1)} %get-tuple-element.105.qo, bf16[512,512]{1,0:T(8,128)(2,1)S(1)} %get-tuple-element.106.qp, bf16[512,512]{1,0:T(8,128)(2,1)S(1)} %get-tuple-element.96.ko, ...), custom_call_target="tpu_custom_call" | custom-call | flops 1000000 | bytes 1000 | tf_op jit(solution)/shard_map/pallas_call | solution.py:68
  58.6 2.7 %collective-permute-start.21 = (bf16[4,4,32,512]{3,2,1,0:T(8,128)(2,1)S(1)}, bf16[4,4,32,512]{3,2,1,0:T(8,128)(2,1)S(1)}, u32[]{:S(2)}, u32[]{:S(2)}) collective-permute-start(bf16[4,4,32,512]{3,2,1,0:T(8,128)(2,1)S(1)} %pad_maximum_fusion.3), channel_id=1, source_target_pairs={{0,24},{8,0},{16,8},{24,16},{1,25},{9,1},{17,9},{25,17},{2,26},{10... | collective-permute-start | bytes 1572872 | tf_op jit(solution)/shard_map/ppermute | solution.py:451
  62.7 1.8 %shard_map.101 = (bf16[4,4,32,512]{3,2,1,0:T(8,128)(2,1)S(1)}, bf16[4,4,32,512]{3,2,1,0:T(8,128)(2,1)S(1)}) custom-call(s32[4]{0:T(128)S(1)} %pad_add_fusion.c, bf16[4,4,128,1024]{3,2,1,0:T(8,128)(2,1)S(1)} %bitcast.69, bf16[1024,512]{1,0:T(8,128)(2,1)S(1)} %get-tuple-element.153.refs_0_.refs_1_, bf16[1024,512]{1,0:T(8,128)(2,1)S(1)} %get-tuple-element.154.refs_1_.refs_2_.refs_3_), custom_call_target="tpu_custom_call" | custom-call | flops 1000000 | bytes 1000 | tf_op jit(solution)/shard_map/pallas_call | solution.py:68
  66.5 1.8 %shard_map.103 = (bf16[4,4,32,512]{3,2,1,0:T(8,128)(2,1)S(1)}, bf16[4,4,32,512]{3,2,1,0:T(8,128)(2,1)S(1)}) custom-call(s32[4]{0:T(128)S(1)} %pad_add_fusion.c, bf16[4,4,128,1024]{3,2,1,0:T(8,128)(2,1)S(1)} %bitcast.70, bf16[1024,512]{1,0:T(8,128)(2,1)S(1)} %get-tuple-element.153.refs_0_.refs_1_, bf16[1024,512]{1,0:T(8,128)(2,1)S(1)} %get-tuple-element.154.refs_1_.refs_2_.refs_3_), custom_call_target="tpu_custom_call" | custom-call | flops 1000000 | bytes 1000 | tf_op jit(solution)/shard_map/pallas_call | solution.py:68
  68.3 2.9 %shard_map.102 = (bf16[4,4,32,512]{3,2,1,0:T(8,128)(2,1)S(1)}, bf16[4,4,32,512]{3,2,1,0:T(8,128)(2,1)S(1)}, bf16[4,4,32,512]{3,2,1,0:T(8,128)(2,1)S(1)}, bf16[4,4,32,512]{3,2,1,0:T(8,128)(2,1)S(1)}) custom-call(s32[4]{0:T(128)S(1)} %pad_add_fusion.c, bf16[4,4,128,1024]{3,2,1,0:T(8,128)(2,1)S(1)} %bitcast.71, ...), custom_call_target="tpu_custom_call" | custom-call | flops 1000000 | bytes 1000 | tf_op jit(solution)/shard_map/pallas_call | solution.py:68
  71.2 4.6 %shard_map.104 = bf16[512,2048]{1,0:T(8,128)(2,1)S(1)} custom-call(s32[4]{0:T(128)S(1)} %pad_add_fusion.c, bf16[1024,512]{1,0:T(8,128)(2,1)S(1)} %shard_map.97.g.refs_0_, bf16[1024,512]{1,0:T(8,128)(2,1)S(1)} %get-tuple-element.153.refs_0_.refs_1_, bf16[1024,512]{1,0:T(8,128)(2,1)S(1)} %get-tuple-element.154.refs_1_.refs_2_.refs_3_, ...), custom_call_target="tpu_custom_call" | custom-call | flops 1000000 | bytes 1000 | tf_op jit(solution)/shard_map/pallas_call | solution.py:68
  76.8 3.3 %collective-permute-start.22 = (bf16[512,2048]{1,0:T(8,128)(2,1)S(1)}, bf16[512,2048]{1,0:T(8,128)(2,1)S(1)}, u32[]{:S(2)}, u32[]{:S(2)}) collective-permute-start(bf16[512,2048]{1,0:T(8,128)(2,1)S(1)} %shard_map.104), channel_id=1, source_target_pairs={{0,4},{4,0},{1,5},{5,1},{2,6},{6,2},{3,7},{7,3},{8,12},{12,8},{9,1... | collective-permute-start | bytes 6291464 | tf_op jit(solution)/shard_map/ppermute | solution.py:455
  80.3 2.5 %collective-permute-start.24 = (bf16[4,4,32,512]{3,2,1,0:T(8,128)(2,1)S(1)}, bf16[4,4,32,512]{3,2,1,0:T(8,128)(2,1)S(1)}, u32[]{:S(2)}, u32[]{:S(2)}) collective-permute-start(bf16[4,4,32,512]{3,2,1,0:T(8,128)(2,1)S(1)} %pad_maximum_fusion.5), channel_id=1, source_target_pairs={{0,24},{8,0},{16,8},{24,16},{1,25},{9,1},{17,9},{25,17},{2,26},{10... | collective-permute-start | bytes 1572872 | tf_op jit(solution)/shard_map/ppermute | solution.py:451
  83.9 2.4 %collective-permute-start.26 = (bf16[18,32,512]{2,1,0:T(8,128)(2,1)S(1)}, bf16[18,32,512]{2,1,0:T(8,128)(2,1)S(1)}, u32[]{:S(2)}, u32[]{:S(2)}) collective-permute-start(bf16[18,32,512]{2,1,0:T(8,128)(2,1)S(1)} %pad_maximum_fusion.1), channel_id=1, source_target_pairs={{0,96},{32,0},{64,32},{96,64},{1,97},{33,1},{65,33},{97,65},{2,98}... | collective-permute-start | bytes 1769480 | tf_op jit(solution)/shard_map/ppermute | solution.py:451
  86.4 1.5 %shard_map.106 = bf16[512,1024]{1,0:T(8,128)(2,1)} custom-call(s32[4]{0:T(128)S(1)} %pad_add_fusion.c, bf16[512,512]{1,0:T(8,128)(2,1)S(1)} %get-tuple-element.156.o, bf16[512,512]{1,0:T(8,128)(2,1)S(1)} %collective-permute-done.11.r), custom_call_target="tpu_custom_call" | custom-call | flops 1000000 | bytes 1000 | tf_op jit(solution)/shard_map/pallas_call | solution.py:68
  88.0 5.4 %shard_map.105 = bf16[512,2048]{1,0:T(8,128)(2,1)} custom-call(s32[4]{0:T(128)S(1)} %pad_add_fusion.c, bf16[1024,512]{1,0:T(8,128)(2,1)S(1)} %shard_map.97.g.refs_0_, bf16[1024,512]{1,0:T(8,128)(2,1)S(1)} %get-tuple-element.153.refs_0_.refs_1_, bf16[1024,512]{1,0:T(8,128)(2,1)S(1)} %get-tuple-element.154.refs_1_.refs_2_.refs_3_, ...), custom_call_target="tpu_custom_call" | custom-call | flops 1000000 | bytes 1000 | tf_op jit(solution)/shard_map/pallas_call | solution.py:68
  94.2 6.0 %collective-permute-done.23 = bf16[4,4,32,512]{3,2,1,0:T(8,128)(2,1)S(1)} collective-permute-done((bf16[4,4,32,512]{3,2,1,0:T(8,128)(2,1)S(1)}, bf16[4,4,32,512]{3,2,1,0:T(8,128)(2,1)S(1)}, u32[]{:S(2)}, u32[]{:S(2)}) %collective-permute-start.23) | collective-permute-done | bytes 524320 | tf_op jit(solution)/shard_map/ppermute | solution.py:451
  100.9 1.6 %collective-permute-start.28 = (bf16[2,4,32,512]{3,2,1,0:T(8,128)(2,1)S(1)}, bf16[2,4,32,512]{3,2,1,0:T(8,128)(2,1)S(1)}, u32[]{:S(2)}, u32[]{:S(2)}) collective-permute-start(bf16[2,4,32,512]{3,2,1,0:T(8,128)(2,1)S(1)} %pad_maximum_fusion.8), channel_id=1, source_target_pairs={{0,96},{32,0},{64,32},{96,64},{1,97},{33,1},{65,33},{97,65},{2,98}... | collective-permute-start | bytes 786440 | tf_op jit(solution)/shard_map/ppermute | solution.py:451
  104.3 3.7 %collective-permute-done.30 = bf16[4,32,512]{2,1,0:T(8,128)(2,1)S(1)} collective-permute-done((bf16[4,32,512]{2,1,0:T(8,128)(2,1)S(1)}, bf16[4,32,512]{2,1,0:T(8,128)(2,1)S(1)}, u32[]{:S(2)}, u32[]{:S(2)}) %collective-permute-start.30) | collective-permute-done | bytes 131104 | tf_op jit(solution)/shard_map/ppermute | solution.py:451
  108.1 2.2 %collective-permute-done.31 = bf16[4,32,512]{2,1,0:T(8,128)(2,1)S(1)} collective-permute-done((bf16[4,32,512]{2,1,0:T(8,128)(2,1)S(1)}, bf16[4,32,512]{2,1,0:T(8,128)(2,1)S(1)}, u32[]{:S(2)}, u32[]{:S(2)}) %collective-permute-start.31) | collective-permute-done | bytes 131104 | tf_op jit(solution)/shard_map/ppermute | solution.py:451
  111.1 2.8 %collective-permute-done.29 = bf16[4,32,512]{2,1,0:T(8,128)(2,1)S(1)} collective-permute-done((bf16[4,32,512]{2,1,0:T(8,128)(2,1)S(1)}, bf16[4,32,512]{2,1,0:T(8,128)(2,1)S(1)}, u32[]{:S(2)}, u32[]{:S(2)}) %collective-permute-start.29) | collective-permute-done | bytes 131104 | tf_op jit(solution)/shard_map/ppermute | solution.py:451
  114.0 3.7 %collective-permute-start.33 = (bf16[32,1536]{1,0:T(8,128)(2,1)S(1)}, bf16[32,1536]{1,0:T(8,128)(2,1)S(1)}, u32[]{:S(2)}, u32[]{:S(2)}) collective-permute-start(bf16[32,1536]{1,0:T(8,128)(2,1)S(1)} %get-tuple-element.197), channel_id=1, source_target_pairs={{0,2},{1,3},{2,0},{3,1},{4,6},{5,7},{6,4},{7,5},{8,10},{9,11},{10,... | collective-permute-start | bytes 294920 | tf_op jit(solution)/shard_map/ppermute | solution.py:451
  119.7 1.8 %collective-permute-done.35 = bf16[32,1536]{1,0:T(8,128)(2,1)S(1)} collective-permute-done((bf16[32,1536]{1,0:T(8,128)(2,1)S(1)}, bf16[32,1536]{1,0:T(8,128)(2,1)S(1)}, u32[]{:S(2)}, u32[]{:S(2)}) %collective-permute-start.35) | collective-permute-done | bytes 98336 | tf_op jit(solution)/shard_map/ppermute | solution.py:451
  122.9 5.9 %collective-permute-start.36 = (bf16[16,1536]{1,0:T(8,128)(2,1)S(1)}, bf16[16,1536]{1,0:T(8,128)(2,1)S(1)}, u32[]{:S(2)}, u32[]{:S(2)}) collective-permute-start(bf16[16,1536]{1,0:T(8,128)(2,1)S(1)} %slice_select_fusion), channel_id=1, source_target_pairs={{0,4},{4,0},{1,5},{5,1},{2,6},{6,2},{3,7},{7,3},{8,12},{12,8},{9,1... | collective-permute-start | bytes 147464 | tf_op jit(solution)/shard_map/ppermute | solution.py:455
  (96 shorter events, 26.0 us)
Async XLA Ops:
  0.6 7.2 %collective-permute-start = (bf16[512,2048]{1,0:T(8,128)(2,1)}, bf16[512,2048]{1,0:T(8,128)(2,1)S(1)}, u32[]{:S(2)}, u32[]{:S(2)}) collective-permute-start(bf16[512,2048]{1,0:T(8,128)(2,1)} %bitcast.72), channel_id=1, source_target_pairs={{0,4},{4,0},{1,5},{5,1},{2,6},{6,2},{3,7},{7,3},{8,12},{12,8},{9,1... | collective-permute-start | bytes 6291464 | tf_op jit(solution)/shard_map/ppermute | solution.py:455
  11.1 9.9 %collective-permute-start.3 = (bf16[512,128]{1,0:T(8,128)(2,1)S(1)}, bf16[512,128]{1,0:T(8,128)(2,1)S(1)}, u32[]{:S(2)}, u32[]{:S(2)}) collective-permute-start(bf16[512,128]{1,0:T(8,128)(2,1)S(1)} %get-tuple-element.94), channel_id=1, source_target_pairs={{0,16},{8,24},{16,0},{24,8},{1,17},{9,25},{17,1},{25,9},{2,18},{10... | collective-permute-start | bytes 393224 | tf_op jit(solution)/shard_map/ppermute | solution.py:451
  14.0 7.0 %collective-permute-start.2 = (bf16[512,128]{1,0:T(8,128)(2,1)S(1)}, bf16[512,128]{1,0:T(8,128)(2,1)S(1)}, u32[]{:S(2)}, u32[]{:S(2)}) collective-permute-start(bf16[512,128]{1,0:T(8,128)(2,1)S(1)} %get-tuple-element.94), channel_id=1, source_target_pairs={{0,24},{8,0},{16,8},{24,16},{1,25},{9,1},{17,9},{25,17},{2,26},{10... | collective-permute-start | bytes 393224 | tf_op jit(solution)/shard_map/ppermute | solution.py:451
  14.9 6.1 %collective-permute-start.1 = (bf16[512,128]{1,0:T(8,128)(2,1)S(1)}, bf16[512,128]{1,0:T(8,128)(2,1)S(1)}, u32[]{:S(2)}, u32[]{:S(2)}) collective-permute-start(bf16[512,128]{1,0:T(8,128)(2,1)S(1)} %get-tuple-element.94), channel_id=1, source_target_pairs={{0,8},{8,16},{16,24},{24,0},{1,9},{9,17},{17,25},{25,1},{2,10},{10... | collective-permute-start | bytes 393224 | tf_op jit(solution)/shard_map/ppermute | solution.py:451
  21.1 10.8 %collective-permute-start.7 = (bf16[512,512]{1,0:T(8,128)(2,1)S(1)}, bf16[512,512]{1,0:T(8,128)(2,1)S(1)}, u32[]{:S(2)}, u32[]{:S(2)}) collective-permute-start(bf16[512,512]{1,0:T(8,128)(2,1)S(1)} %get-tuple-element.110), channel_id=1, source_target_pairs={{0,4},{4,0},{1,5},{5,1},{2,6},{6,2},{3,7},{7,3},{8,12},{12,8},{9,1... | collective-permute-start | bytes 1572872 | tf_op jit(solution)/shard_map/ppermute | solution.py:455
  22.2 6.7 %collective-permute-start.6 = (bf16[512,128]{1,0:T(8,128)(2,1)S(1)}, bf16[512,128]{1,0:T(8,128)(2,1)S(1)}, u32[]{:S(2)}, u32[]{:S(2)}) collective-permute-start(bf16[512,128]{1,0:T(8,128)(2,1)S(1)} %add_convert_fusion.7), channel_id=1, source_target_pairs={{0,64},{32,96},{64,0},{96,32},{1,65},{33,97},{65,1},{97,33},{2,66}... | collective-permute-start | bytes 393224 | tf_op jit(solution)/shard_map/ppermute | solution.py:451
  25.1 6.8 %collective-permute-start.5 = (bf16[512,128]{1,0:T(8,128)(2,1)S(1)}, bf16[512,128]{1,0:T(8,128)(2,1)S(1)}, u32[]{:S(2)}, u32[]{:S(2)}) collective-permute-start(bf16[512,128]{1,0:T(8,128)(2,1)S(1)} %add_convert_fusion.7), channel_id=1, source_target_pairs={{0,96},{32,0},{64,32},{96,64},{1,97},{33,1},{65,33},{97,65},{2,98}... | collective-permute-start | bytes 393224 | tf_op jit(solution)/shard_map/ppermute | solution.py:451
  25.9 6.0 %collective-permute-start.4 = (bf16[512,128]{1,0:T(8,128)(2,1)S(1)}, bf16[512,128]{1,0:T(8,128)(2,1)S(1)}, u32[]{:S(2)}, u32[]{:S(2)}) collective-permute-start(bf16[512,128]{1,0:T(8,128)(2,1)S(1)} %add_convert_fusion.7), channel_id=1, source_target_pairs={{0,32},{32,64},{64,96},{96,0},{1,33},{33,65},{65,97},{97,1},{2,34}... | collective-permute-start | bytes 393224 | tf_op jit(solution)/shard_map/ppermute | solution.py:451
  34.7 11.7 %collective-permute-start.11 = (bf16[512,512]{1,0:T(8,128)(2,1)S(1)}, bf16[512,512]{1,0:T(8,128)(2,1)S(1)}, u32[]{:S(2)}, u32[]{:S(2)}) collective-permute-start(bf16[512,512]{1,0:T(8,128)(2,1)S(1)} %get-tuple-element.121), channel_id=1, source_target_pairs={{0,4},{4,0},{1,5},{5,1},{2,6},{6,2},{3,7},{7,3},{8,12},{12,8},{9,1... | collective-permute-start | bytes 1572872 | tf_op jit(solution)/shard_map/ppermute | solution.py:455
  35.9 10.5 %collective-permute-start.10 = (bf16[512,128]{1,0:T(8,128)(2,1)S(1)}, bf16[512,128]{1,0:T(8,128)(2,1)S(1)}, u32[]{:S(2)}, u32[]{:S(2)}) collective-permute-start(bf16[512,128]{1,0:T(8,128)(2,1)S(1)} %get-tuple-element.116), channel_id=1, source_target_pairs={{0,16},{8,24},{16,0},{24,8},{1,17},{9,25},{17,1},{25,9},{2,18},{10... | collective-permute-start | bytes 393224 | tf_op jit(solution)/shard_map/ppermute | solution.py:451
  38.2 8.2 %collective-permute-start.9 = (bf16[512,128]{1,0:T(8,128)(2,1)S(1)}, bf16[512,128]{1,0:T(8,128)(2,1)S(1)}, u32[]{:S(2)}, u32[]{:S(2)}) collective-permute-start(bf16[512,128]{1,0:T(8,128)(2,1)S(1)} %get-tuple-element.116), channel_id=1, source_target_pairs={{0,24},{8,0},{16,8},{24,16},{1,25},{9,1},{17,9},{25,17},{2,26},{10... | collective-permute-start | bytes 393224 | tf_op jit(solution)/shard_map/ppermute | solution.py:451
  39.1 7.3 %collective-permute-start.8 = (bf16[512,128]{1,0:T(8,128)(2,1)S(1)}, bf16[512,128]{1,0:T(8,128)(2,1)S(1)}, u32[]{:S(2)}, u32[]{:S(2)}) collective-permute-start(bf16[512,128]{1,0:T(8,128)(2,1)S(1)} %get-tuple-element.116), channel_id=1, source_target_pairs={{0,8},{8,16},{16,24},{24,0},{1,9},{9,17},{17,25},{25,1},{2,10},{10... | collective-permute-start | bytes 393224 | tf_op jit(solution)/shard_map/ppermute | solution.py:451
  46.6 11.6 %collective-permute-start.16 = (bf16[2,4,32,512]{3,2,1,0:T(8,128)(2,1)S(1)}, bf16[2,4,32,512]{3,2,1,0:T(8,128)(2,1)S(1)}, u32[]{:S(2)}, u32[]{:S(2)}) collective-permute-start(bf16[2,4,32,512]{3,2,1,0:T(8,128)(2,1)S(1)} %get-tuple-element.179), channel_id=1, source_target_pairs={{0,24},{8,0},{16,8},{24,16},{1,25},{9,1},{17,9},{25,17},{2,26},{10... | collective-permute-start | bytes 786440 | tf_op jit(solution)/shard_map/ppermute | solution.py:451
  48.8 9.4 %collective-permute-start.15 = (bf16[2,4,32,512]{3,2,1,0:T(8,128)(2,1)S(1)}, bf16[2,4,32,512]{3,2,1,0:T(8,128)(2,1)S(1)}, u32[]{:S(2)}, u32[]{:S(2)}) collective-permute-start(bf16[2,4,32,512]{3,2,1,0:T(8,128)(2,1)S(1)} %get-tuple-element.180), channel_id=1, source_target_pairs={{0,8},{8,16},{16,24},{24,0},{1,9},{9,17},{17,25},{25,1},{2,10},{10... | collective-permute-start | bytes 786440 | tf_op jit(solution)/shard_map/ppermute | solution.py:451
  48.8 9.1 %collective-permute-start.14 = (bf16[512,128]{1,0:T(8,128)(2,1)S(1)}, bf16[512,128]{1,0:T(8,128)(2,1)S(1)}, u32[]{:S(2)}, u32[]{:S(2)}) collective-permute-start(bf16[512,128]{1,0:T(8,128)(2,1)S(1)} %add_convert_fusion.6), channel_id=1, source_target_pairs={{0,64},{32,96},{64,0},{96,32},{1,65},{33,97},{65,1},{97,33},{2,66}... | collective-permute-start | bytes 393224 | tf_op jit(solution)/shard_map/ppermute | solution.py:451
  51.1 6.7 %collective-permute-start.13 = (bf16[512,128]{1,0:T(8,128)(2,1)S(1)}, bf16[512,128]{1,0:T(8,128)(2,1)S(1)}, u32[]{:S(2)}, u32[]{:S(2)}) collective-permute-start(bf16[512,128]{1,0:T(8,128)(2,1)S(1)} %add_convert_fusion.6), channel_id=1, source_target_pairs={{0,96},{32,0},{64,32},{96,64},{1,97},{33,1},{65,33},{97,65},{2,98}... | collective-permute-start | bytes 393224 | tf_op jit(solution)/shard_map/ppermute | solution.py:451
  52.0 6.2 %collective-permute-start.12 = (bf16[512,128]{1,0:T(8,128)(2,1)S(1)}, bf16[512,128]{1,0:T(8,128)(2,1)S(1)}, u32[]{:S(2)}, u32[]{:S(2)}) collective-permute-start(bf16[512,128]{1,0:T(8,128)(2,1)S(1)} %add_convert_fusion.6), channel_id=1, source_target_pairs={{0,32},{32,64},{64,96},{96,0},{1,33},{33,65},{65,97},{97,1},{2,34}... | collective-permute-start | bytes 393224 | tf_op jit(solution)/shard_map/ppermute | solution.py:451
  58.4 18.4 %collective-permute-start.20 = (bf16[4,4,32,512]{3,2,1,0:T(8,128)(2,1)S(1)}, bf16[4,4,32,512]{3,2,1,0:T(8,128)(2,1)S(1)}, u32[]{:S(2)}, u32[]{:S(2)}) collective-permute-start(bf16[4,4,32,512]{3,2,1,0:T(8,128)(2,1)S(1)} %pad_maximum_fusion.2), channel_id=1, source_target_pairs={{0,8},{8,16},{16,24},{24,0},{1,9},{9,17},{17,25},{25,1},{2,10},{10... | collective-permute-start | bytes 1572872 | tf_op jit(solution)/shard_map/ppermute | solution.py:451
  58.6 18.2 %collective-permute-start.21 = (bf16[4,4,32,512]{3,2,1,0:T(8,128)(2,1)S(1)}, bf16[4,4,32,512]{3,2,1,0:T(8,128)(2,1)S(1)}, u32[]{:S(2)}, u32[]{:S(2)}) collective-permute-start(bf16[4,4,32,512]{3,2,1,0:T(8,128)(2,1)S(1)} %pad_maximum_fusion.3), channel_id=1, source_target_pairs={{0,24},{8,0},{16,8},{24,16},{1,25},{9,1},{17,9},{25,17},{2,26},{10... | collective-permute-start | bytes 1572872 | tf_op jit(solution)/shard_map/ppermute | solution.py:451
  64.5 12.3 %collective-permute-start.19 = (bf16[4,4,32,512]{3,2,1,0:T(8,128)(2,1)S(1)}, bf16[4,4,32,512]{3,2,1,0:T(8,128)(2,1)S(1)}, u32[]{:S(2)}, u32[]{:S(2)}) collective-permute-start(bf16[4,4,32,512]{3,2,1,0:T(8,128)(2,1)S(1)} %get-tuple-element.148), channel_id=1, source_target_pairs={{0,32},{32,64},{64,96},{96,0},{1,33},{33,65},{65,97},{97,1},{2,34}... | collective-permute-start | bytes 1572872 | tf_op jit(solution)/shard_map/ppermute | solution.py:451
  65.0 10.9 %collective-permute-start.18 = (bf16[2,4,32,512]{3,2,1,0:T(8,128)(2,1)S(1)}, bf16[2,4,32,512]{3,2,1,0:T(8,128)(2,1)S(1)}, u32[]{:S(2)}, u32[]{:S(2)}) collective-permute-start(bf16[2,4,32,512]{3,2,1,0:T(8,128)(2,1)S(1)} %get-tuple-element.195), channel_id=1, source_target_pairs={{0,24},{8,0},{16,8},{24,16},{1,25},{9,1},{17,9},{25,17},{2,26},{10... | collective-permute-start | bytes 786440 | tf_op jit(solution)/shard_map/ppermute | solution.py:451
  66.2 10.6 %collective-permute-start.17 = (bf16[2,4,32,512]{3,2,1,0:T(8,128)(2,1)S(1)}, bf16[2,4,32,512]{3,2,1,0:T(8,128)(2,1)S(1)}, u32[]{:S(2)}, u32[]{:S(2)}) collective-permute-start(bf16[2,4,32,512]{3,2,1,0:T(8,128)(2,1)S(1)} %get-tuple-element.196), channel_id=1, source_target_pairs={{0,8},{8,16},{16,24},{24,0},{1,9},{9,17},{17,25},{25,1},{2,10},{10... | collective-permute-start | bytes 786440 | tf_op jit(solution)/shard_map/ppermute | solution.py:451
  76.8 11.2 %collective-permute-start.22 = (bf16[512,2048]{1,0:T(8,128)(2,1)S(1)}, bf16[512,2048]{1,0:T(8,128)(2,1)S(1)}, u32[]{:S(2)}, u32[]{:S(2)}) collective-permute-start(bf16[512,2048]{1,0:T(8,128)(2,1)S(1)} %shard_map.104), channel_id=1, source_target_pairs={{0,4},{4,0},{1,5},{5,1},{2,6},{6,2},{3,7},{7,3},{8,12},{12,8},{9,1... | collective-permute-start | bytes 6291464 | tf_op jit(solution)/shard_map/ppermute | solution.py:455
  80.3 13.9 %collective-permute-start.24 = (bf16[4,4,32,512]{3,2,1,0:T(8,128)(2,1)S(1)}, bf16[4,4,32,512]{3,2,1,0:T(8,128)(2,1)S(1)}, u32[]{:S(2)}, u32[]{:S(2)}) collective-permute-start(bf16[4,4,32,512]{3,2,1,0:T(8,128)(2,1)S(1)} %pad_maximum_fusion.5), channel_id=1, source_target_pairs={{0,24},{8,0},{16,8},{24,16},{1,25},{9,1},{17,9},{25,17},{2,26},{10... | collective-permute-start | bytes 1572872 | tf_op jit(solution)/shard_map/ppermute | solution.py:451
  83.4 16.9 %collective-permute-start.25 = (bf16[18,32,512]{2,1,0:T(8,128)(2,1)S(1)}, bf16[18,32,512]{2,1,0:T(8,128)(2,1)S(1)}, u32[]{:S(2)}, u32[]{:S(2)}) collective-permute-start(bf16[18,32,512]{2,1,0:T(8,128)(2,1)S(1)} %pad_maximum_fusion), channel_id=1, source_target_pairs={{0,32},{32,64},{64,96},{96,0},{1,33},{33,65},{65,97},{97,1},{2,34}... | collective-permute-start | bytes 1769480 | tf_op jit(solution)/shard_map/ppermute | solution.py:451
  83.9 16.4 %collective-permute-start.26 = (bf16[18,32,512]{2,1,0:T(8,128)(2,1)S(1)}, bf16[18,32,512]{2,1,0:T(8,128)(2,1)S(1)}, u32[]{:S(2)}, u32[]{:S(2)}) collective-permute-start(bf16[18,32,512]{2,1,0:T(8,128)(2,1)S(1)} %pad_maximum_fusion.1), channel_id=1, source_target_pairs={{0,96},{32,0},{64,32},{96,64},{1,97},{33,1},{65,33},{97,65},{2,98}... | collective-permute-start | bytes 1769480 | tf_op jit(solution)/shard_map/ppermute | solution.py:451
  86.4 13.9 %collective-permute-start.23 = (bf16[4,4,32,512]{3,2,1,0:T(8,128)(2,1)S(1)}, bf16[4,4,32,512]{3,2,1,0:T(8,128)(2,1)S(1)}, u32[]{:S(2)}, u32[]{:S(2)}) collective-permute-start(bf16[4,4,32,512]{3,2,1,0:T(8,128)(2,1)S(1)} %pad_maximum_fusion.4), channel_id=1, source_target_pairs={{0,8},{8,16},{16,24},{24,0},{1,9},{9,17},{17,25},{25,1},{2,10},{10... | collective-permute-start | bytes 1572872 | tf_op jit(solution)/shard_map/ppermute | solution.py:451
  100.9 9.5 %collective-permute-start.28 = (bf16[2,4,32,512]{3,2,1,0:T(8,128)(2,1)S(1)}, bf16[2,4,32,512]{3,2,1,0:T(8,128)(2,1)S(1)}, u32[]{:S(2)}, u32[]{:S(2)}) collective-permute-start(bf16[2,4,32,512]{3,2,1,0:T(8,128)(2,1)S(1)} %pad_maximum_fusion.8), channel_id=1, source_target_pairs={{0,96},{32,0},{64,32},{96,64},{1,97},{33,1},{65,33},{97,65},{2,98}... | collective-permute-start | bytes 786440 | tf_op jit(solution)/shard_map/ppermute | solution.py:451
  104.0 6.3 %collective-permute-start.31 = (bf16[4,32,512]{2,1,0:T(8,128)(2,1)S(1)}, bf16[4,32,512]{2,1,0:T(8,128)(2,1)S(1)}, u32[]{:S(2)}, u32[]{:S(2)}) collective-permute-start(bf16[4,32,512]{2,1,0:T(8,128)(2,1)S(1)} %get-tuple-element.192), channel_id=1, source_target_pairs={{0,8},{8,16},{16,24},{24,0},{1,9},{9,17},{17,25},{25,1},{2,10},{10... | collective-permute-start | bytes 393224 | tf_op jit(solution)/shard_map/ppermute | solution.py:451
  104.2 6.8 %collective-permute-start.27 = (bf16[2,4,32,512]{3,2,1,0:T(8,128)(2,1)S(1)}, bf16[2,4,32,512]{3,2,1,0:T(8,128)(2,1)S(1)}, u32[]{:S(2)}, u32[]{:S(2)}) collective-permute-start(bf16[2,4,32,512]{3,2,1,0:T(8,128)(2,1)S(1)} %pad_maximum_fusion.7), channel_id=1, source_target_pairs={{0,32},{32,64},{64,96},{96,0},{1,33},{33,65},{65,97},{97,1},{2,34}... | collective-permute-start | bytes 786440 | tf_op jit(solution)/shard_map/ppermute | solution.py:451
  108.0 5.9 %collective-permute-start.29 = (bf16[4,32,512]{2,1,0:T(8,128)(2,1)S(1)}, bf16[4,32,512]{2,1,0:T(8,128)(2,1)S(1)}, u32[]{:S(2)}, u32[]{:S(2)}) collective-permute-start(bf16[4,32,512]{2,1,0:T(8,128)(2,1)S(1)} %get-tuple-element.184), channel_id=1, source_target_pairs={{0,64},{32,96},{64,0},{96,32},{1,65},{33,97},{65,1},{97,33},{2,66}... | collective-permute-start | bytes 393224 | tf_op jit(solution)/shard_map/ppermute | solution.py:451
  122.9 6.8 %collective-permute-start.36 = (bf16[16,1536]{1,0:T(8,128)(2,1)S(1)}, bf16[16,1536]{1,0:T(8,128)(2,1)S(1)}, u32[]{:S(2)}, u32[]{:S(2)}) collective-permute-start(bf16[16,1536]{1,0:T(8,128)(2,1)S(1)} %slice_select_fusion), channel_id=1, source_target_pairs={{0,4},{4,0},{1,5},{5,1},{2,6},{6,2},{3,7},{7,3},{8,12},{12,8},{9,1... | collective-permute-start | bytes 147464 | tf_op jit(solution)/shard_map/ppermute | solution.py:455
  (6 other events, 32.7 us)

commit v2 on v1

--- a/solution.py
+++ b/solution.py
@@ -183,34 +183,40 @@
     return total
 
 
-def within(core, tok_o, tok_p, wq, k_o, v_o, k_p, v_p, cot):
-    def kernel(c, to, tp, a, ko, vo, kp, vp, ct, qo, qp, out, mine_ct, other_ct, sems):
-        copies = [
-            pltpu.make_async_copy(ct.at[:, half_of(1 - c[0])], other_ct, sems.at[0]),
-            pltpu.make_async_copy(ct.at[:, half_of(c[0])], mine_ct, sems.at[1]),
-        ]
+def within(core, tok, wq, k, v, cot=None):
+    fetch = cot is not None
+
+    def kernel(c, t, a, ko, vo, *refs):
+        copies = []
+        if fetch:
+            ct, qo, out, mine_ct, other_ct, sems = refs
+            copies = [
+                pltpu.make_async_copy(ct.at[:, half_of(1 - c[0])], other_ct, sems.at[0]),
+                pltpu.make_async_copy(ct.at[:, half_of(c[0])], mine_ct, sems.at[1]),
+            ]
+        else:
+            qo, out = refs
         for copy in copies:
             copy.start()
-        qo[...] = dot(to[...], a[...]).astype(BF)
-        qp[...] = dot(tp[...], a[...]).astype(BF)
-
-        @each_head
+        qo[...] = dot(t[...], a[...]).astype(BF)
+
+        @looped_head
         def _(h):
-            for n, (q, k, v) in enumerate(((qo, ko, vo), (qp, kp, vp))):
-                low, high = forward_pairs(q[:, head(h)], k[:, head(h)], v[:, head(h)])
-                out[n * TOK : n * TOK + 256, head(h)] = low
-                out[n * TOK + 256 : n * TOK + 512, head(h)] = high
+            low, high = forward_pairs(qo[:, head(h)], ko[:, head(h)], vo[:, head(h)])
+            out[:256, head(h)] = low
+            out[256:, head(h)] = high
 
         for copy in copies:
             copy.wait()
 
-    return local(
-        kernel,
-        core,
-        [tok_o, tok_p, wq, k_o, v_o, k_p, v_p, *in_hbm(cot)],
-        [((TOK, 512), BF)] * 2 + [((2 * TOK, 512), F32)] + [((TOK, 512), BF)] * 2,
-        hbm_in=1,
-        scratch=[pltpu.SemaphoreType.DMA((2,))],
+    row = ((TOK, 512), BF)
+    return local(
+        kernel,
+        core,
+        [tok, wq, k, v] + (in_hbm(cot) if fetch else []),
+        [row, ((TOK, 512), F32)] + [row] * (2 if fetch else 0),
+        hbm_in=1 if fetch else 0,
+        scratch=[pltpu.SemaphoreType.DMA((2,))] if fetch else [],
     )
 
 
@@ -230,8 +236,8 @@
     )[0]
 
 
-def normed(core, intra, q_o, q_p, state_o, state_p, along_x, along_y, cot, cot_p):
-    def kernel(c, it, qo, qp, so, sp, x1, x3, x2, y1, y3, y2, co, cp, *outs):
+def normed(core, i_o, i_p, q_o, q_p, state_o, state_p, along_x, along_y, cot, cot_p):
+    def kernel(c, io, ip, qo, qp, so, sp, x1, x3, x2, y1, y3, y2, co, cp, *outs):
         ao, ap, g, po, pp, bo, bp, total = outs
         before = masked_sum((x1, x3, x2), c[2], False) + masked_sum((y1, y3, y2), c[1], False)
         late = c[0].astype(F32)
@@ -241,10 +247,10 @@
         @each_head
         def _(h):
             backs = []
-            for n, (q, p, a, b) in enumerate(((qo, po, ao, bo), (qp, pp, ap, bp))):
+            for n, (it, q, p, a, b) in enumerate(((io, qo, po, ao, bo), (ip, qp, pp, ap, bp))):
                 rows = slice(n * TOK, n * TOK + TOK)
                 qh = q[:, head(h)]
-                mixed = it[rows, head(h)] + dot(qh, p[head(h), :])
+                mixed = it[:, head(h)] + dot(qh, p[head(h), :])
                 inverse = lax.rsqrt(jnp.mean(mixed * mixed, axis=-1, keepdims=True) + EPS)
                 nm = mixed * inverse
                 up = (co if n == 0 else cp)[:, head(h)].astype(F32)
@@ -260,7 +266,7 @@
     return local(
         kernel,
         core,
-        [intra, q_o, q_p, state_o, state_p, *along_x, *along_y, cot, cot_p],
+        [i_o, i_p, q_o, q_p, state_o, state_p, *along_x, *along_y, cot, cot_p],
         [((TOK, 512), BF)] * 2 + [((2 * TOK, 512), BF)] + [state] * 5,
     )
 
@@ -286,7 +292,7 @@
 
 def grads_within(core, q_o, q_p, k_o, k_p, v_o, v_p, g):
     def kernel(c, qo, qp, ko, kp, vo, vp, gr, dk, dv):
-        @looped_head
+        @each_head
         def _(h):
             for n, (q, k, v) in enumerate(((qo, ko, vo), (qp, kp, vp))):
                 qh, kh, vh = q[:, head(h)], k[:, head(h)], v[:, head(h)]
@@ -496,18 +502,17 @@
     k_p, v_p, state_p, total, w_q = project_partner(core, tok_p, w_k, w_v, state_o, w_query)
     weights = (w_q, w_k, w_v)
     along_x = pieces(total, "x")
-    q_o, q_p, intra, cot, cot_s = within(
-        core, tok_o, tok_p, w_q, k_o, v_o, k_p, v_p, cotangent[0]
-    )
-    row, intra, q_o, q_p, tok_t, cot_s = together(
-        f32_sum(total, *along_x), intra, q_o, q_p, tok_o, cot_s
+    q_o, i_o, cot, cot_s = within(core, tok_o, w_q, k_o, v_o, cotangent[0])
+    row, i_o, q_o, tok_t, cot_s, k_p = together(
+        f32_sum(total, *along_x), i_o, q_o, tok_o, cot_s, k_p
     )
     along_y = pieces(row, "y")
     cot_p = swap(cot_s)
+    q_p, i_p = within(core, tok_p, w_q, k_p, v_p)
     tt = turned(core, tok_t, tok_p)
-    *along_y, tt, cot_p = together(*along_y, tt, cot_p)
+    *along_y, tt, cot_p, q_p, i_p = together(*along_y, tt, cot_p, q_p, i_p)
     a_o, a_p, g, p_o, p_p, back_o, back_p, total = normed(
-        core, intra, q_o, q_p, state_o, state_p, along_x, along_y, cot, cot_p
+        core, i_o, i_p, q_o, q_p, state_o, state_p, along_x, along_y, cot, cot_p
     )
     along_x = pieces(total, "x")
     a_r = swap(a_p)
@@ -549,7 +554,9 @@
     down_q = jnp.concatenate([sum_q[3, :2], f32_sum(sum_q[3, 2:], v1[16:])], axis=0)
     up, down = jnp.stack([sum_k[1], up_q]), jnp.stack([sum_k[3], down_q])
     up, down, far = shift(up, "y", 1), shift(down, "y", 3), shift(sum_k[2], "y", 2)
-    sum_v = spread(sum_v, "x")
+    far_v, right = shift(sum_v[2], "x", 2), shift(sum_v[3], "x", 3)
+    right, last_v = together(right, sum_v[1])
+    sum_v = f32_sum(sum_v[0], far_v, right, shift(last_v, "x", 1))
     sum_k = f32_sum(sum_k[0], up[0], down[0], far)
     sum_q = f32_sum(sum_q[0], up[1], down[1])
     summed = spread(jnp.concatenate([sum_q, sum_k, sum_v], axis=-1), "z")

time: 131 us -> 129 us (0.985)
  starting transfers between devices: 50.2 us -> 48 us
    ppermute x5, starting transfers between devices: 13 us -> 10.6 us  [swap(): return lax.ppermute(v, 'c', [(0, 1), (1, 0)])]
    pallas_call x15 -> x16, Pallas kernels: 49.7 us -> 50.8 us  [local(): pl.pallas_call(kernel, out_shape=[jax.ShapeDtypeStruct(s, d) for s, d in...]
  transfers between devices with their start and end apart: 37 -> 37, of which waited for: 14 -> 14; matrix products, arithmetic and copies ran while one was open for 1% -> 1% of each run, Pallas kernels for 34% -> 35%
where the time goes in v2:
time: 129 us
  Pallas kernels  53.1 us (41%)
  starting transfers between devices  48 us (37%)
  waiting for transfers between devices  24.6 us (19%)
  other arithmetic  2.18 us (2%)
    pallas_call x16, Pallas kernels, local(): pl.pallas_call(kernel, out_shape=[jax.ShapeDtypeStruct(s, d) for s, d in...  50.8 us
    ppermute x32, starting transfers between devices, shift(): return lax.ppermute(v, axis, [(i, (i + d) % n) for i in range(n)])  37.4 us
    ppermute x32, waiting for transfers between devices, shift(): return lax.ppermute(v, axis, [(i, (i + d) % n) for i in range(n)])  23.7 us
    ppermute x5, starting transfers between devices, swap(): return lax.ppermute(v, 'c', [(0, 1), (1, 0)])  10.6 us
  transfers between devices with their start and end apart: 37, of which 14 were waited for; matrix products, arithmetic and copies ran while one was open for 1% of the time, Pallas kernels for 35%

profile of v2, /device:TPU:1, one launch (start us, length us, event | category | flops | bytes accessed | tf_op | source)
XLA Modules:
  0.0 129.3 jit_solution(12714152122698286827)
XLA Ops:
  2.2 5.6 %shard_map.92 = (bf16[512,512]{1,0:T(8,128)(2,1)S(1)}, bf16[512,512]{1,0:T(8,128)(2,1)S(1)}, bf16[512,128]{1,0:T(8,128)(2,1)S(1)}, bf16[2048,512]{1,0:T(8,128)(2,1)S(1)}, bf16[2048,512]{1,0:T(8,128)(2,1)S(1)}) custom-call(s32[4]{0:T(128)S(1)} %pad_add_fusion.c, bf16[512,2048]{1,0:T(8,128)(2,1)} %bitcast.73, bf16[2048,1024]{1,0:T(8,128)(2,1)} %b.1, ...), custom_call_target="tpu_custom_call" | custom-call | flops 1000000 | bytes 1000 | tf_op jit(solution)/shard_map/pallas_call | solution.py:68
  7.9 3.2 %shard_map.93 = (bf16[512,512]{1,0:T(8,128)(2,1)S(1)}, bf16[512,512]{1,0:T(8,128)(2,1)S(1)}, bf16[512,128]{1,0:T(8,128)(2,1)S(1)}, bf16[512,128]{1,0:T(8,128)(2,1)S(1)}, bf16[2048,512]{1,0:T(8,128)(2,1)S(1)}) custom-call(s32[4]{0:T(128)S(1)} %pad_add_fusion.c, bf16[512,2048]{1,0:T(8,128)(2,1)S(1)} %collective-permute-done.t.tp, ...), custom_call_target="tpu_custom_call" | custom-call | flops 1000000 | bytes 1000 | tf_op jit(solution)/shard_map/pallas_call | solution.py:68
  11.1 2.9 %collective-permute-start.3 = (bf16[512,128]{1,0:T(8,128)(2,1)S(1)}, bf16[512,128]{1,0:T(8,128)(2,1)S(1)}, u32[]{:S(2)}, u32[]{:S(2)}) collective-permute-start(bf16[512,128]{1,0:T(8,128)(2,1)S(1)} %get-tuple-element.99), channel_id=1, source_target_pairs={{0,16},{8,24},{16,0},{24,8},{1,17},{9,25},{17,1},{25,9},{2,18},{10... | collective-permute-start | bytes 393224 | tf_op jit(solution)/shard_map/ppermute | solution.py:457
  15.5 3.5 %shard_map.94 = (bf16[512,512]{1,0:T(8,128)(2,1)S(1)}, f32[512,512]{1,0:T(8,128)S(1)}, bf16[512,512]{1,0:T(8,128)(2,1)S(1)}, bf16[512,512]{1,0:T(8,128)(2,1)S(1)}) custom-call(s32[4]{0:T(128)S(1)} %pad_add_fusion.c, bf16[512,2048]{1,0:T(8,128)(2,1)S(1)} %bitcast.74, bf16[2048,512]{1,0:T(8,128)(2,1)S(1)} %get-tuple-element.100.a.refs_3_, ...), custom_call_target="tpu_custom_call" | custom-call | flops 1000000 | bytes 1000 | tf_op jit(solution)/shard_map/pallas_call | solution.py:68
  19.0 1.8 %collective-permute-done.2.x3 = bf16[512,128]{1,0:T(8,128)(2,1)S(1)} collective-permute-done((bf16[512,128]{1,0:T(8,128)(2,1)S(1)}, bf16[512,128]{1,0:T(8,128)(2,1)S(1)}, u32[]{:S(2)}, u32[]{:S(2)}) %collective-permute-start.2) | collective-permute-done | bytes 131104 | tf_op jit(solution)/shard_map/ppermute | solution.py:457
  22.2 2.9 %collective-permute-start.6 = (bf16[512,128]{1,0:T(8,128)(2,1)S(1)}, bf16[512,128]{1,0:T(8,128)(2,1)S(1)}, u32[]{:S(2)}, u32[]{:S(2)}) collective-permute-start(bf16[512,128]{1,0:T(8,128)(2,1)S(1)} %add_convert_fusion.7), channel_id=1, source_target_pairs={{0,64},{32,96},{64,0},{96,32},{1,65},{33,97},{65,1},{97,33},{2,66}... | collective-permute-start | bytes 393224 | tf_op jit(solution)/shard_map/ppermute | solution.py:457
  26.5 2.3 %shard_map.95 = bf16[2048,1024]{1,0:T(8,128)(2,1)S(1)} custom-call(s32[4]{0:T(128)S(1)} %pad_add_fusion.c, bf16[512,2048]{1,0:T(8,128)(2,1)S(1)} %bitcast.75, bf16[512,2048]{1,0:T(8,128)(2,1)S(1)} %collective-permute-done.t.tp), custom_call_target="tpu_custom_call" | custom-call | flops 1000000 | bytes 8388608 | tf_op jit(solution)/shard_map/pallas_call | solution.py:50
  28.9 3.5 %shard_map.96 = (bf16[512,512]{1,0:T(8,128)(2,1)S(1)}, f32[512,512]{1,0:T(8,128)S(1)}) custom-call(s32[4]{0:T(128)S(1)} %pad_add_fusion.c, bf16[512,2048]{1,0:T(8,128)(2,1)S(1)} %collective-permute-done.t.tp, bf16[2048,512]{1,0:T(8,128)(2,1)S(1)} %get-tuple-element.100.a.refs_3_, bf16[512,512]{1,0:T(8,128)(2,1)S(1)} %get-tuple-element.111.ko.kp, ...), custom_call_target="tpu_custom_call" | custom-call | flops 1000000 | bytes 1000 | tf_op jit(solution)/shard_map/pallas_call | solution.py:68
  32.4 2.9 %shard_map.97 = (bf16[512,512]{1,0:T(8,128)(2,1)S(1)}, bf16[512,512]{1,0:T(8,128)(2,1)S(1)}, bf16[1024,512]{1,0:T(8,128)(2,1)S(1)}, bf16[512,128]{1,0:T(8,128)(2...) custom-call(s32[4]{0:T(128)S(1)} %pad_add_fusion.c, ...), custom_call_target="tpu_custom_call" | custom-call | flops 1000000 | bytes 1000 | tf_op jit(solution)/shard_map/pallas_call | solution.py:68
  36.3 2.3 %collective-permute-start.10 = (bf16[512,128]{1,0:T(8,128)(2,1)S(1)}, bf16[512,128]{1,0:T(8,128)(2,1)S(1)}, u32[]{:S(2)}, u32[]{:S(2)}) collective-permute-start(bf16[512,128]{1,0:T(8,128)(2,1)S(1)} %get-tuple-element.124), channel_id=1, source_target_pairs={{0,16},{8,24},{16,0},{24,8},{1,17},{9,25},{17,1},{25,9},{2,18},{10... | collective-permute-start | bytes 393224 | tf_op jit(solution)/shard_map/ppermute | solution.py:457
  40.0 3.3 %shard_map.98.g.refs_0_ = bf16[1024,512]{1,0:T(8,128)(2,1)S(1)} custom-call(s32[4]{0:T(128)S(1)} %pad_add_fusion.c, bf16[512,512]{1,0:T(8,128)(2,1)S(1)} %get-tuple-element.101.ko, bf16[512,512]{1,0:T(8,128)(2,1)S(1)} %get-tuple-element.111.ko.kp, bf16[512,512]{1,0:T(8,128)(2,1)S(1)} %get-tuple-element.102.vo, ...), custom_call_target="tpu_custom_call" | custom-call | flops 1000000 | bytes 1000 | tf_op jit(solution)/shard_map/pallas_call | solution.py:68
  43.3 3.4 %shard_map.99 = bf16[4,4,4,32,512]{4,3,2,1,0:T(8,128)(2,1)S(1)} custom-call(s32[4]{0:T(128)S(1)} %pad_add_fusion.c, bf16[4,4,128,1024]{3,2,1,0:T(8,128)(2,1)S(1)} %bitcast.68, bf16[1024,512]{1,0:T(8,128)(2,1)S(1)} %shard_map.98.g.refs_0_), custom_call_target="tpu_custom_call" | custom-call | flops 1000000 | bytes 1000 | tf_op jit(solution)/shard_map/pallas_call | solution.py:68
  46.9 2.2 %collective-permute-start.16 = (bf16[2,4,32,512]{3,2,1,0:T(8,128)(2,1)S(1)}, bf16[2,4,32,512]{3,2,1,0:T(8,128)(2,1)S(1)}, u32[]{:S(2)}, u32[]{:S(2)}) collective-permute-start(bf16[2,4,32,512]{3,2,1,0:T(8,128)(2,1)S(1)} %get-tuple-element.189), channel_id=1, source_target_pairs={{0,24},{8,0},{16,8},{24,16},{1,25},{9,1},{17,9},{25,17},{2,26},{10... | collective-permute-start | bytes 786440 | tf_op jit(solution)/shard_map/ppermute | solution.py:457
  49.1 2.0 %collective-permute-start.14 = (bf16[512,128]{1,0:T(8,128)(2,1)S(1)}, bf16[512,128]{1,0:T(8,128)(2,1)S(1)}, u32[]{:S(2)}, u32[]{:S(2)}) collective-permute-start(bf16[512,128]{1,0:T(8,128)(2,1)S(1)} %add_convert_fusion.6), channel_id=1, source_target_pairs={{0,64},{32,96},{64,0},{96,32},{1,65},{33,97},{65,1},{97,33},{2,66}... | collective-permute-start | bytes 393224 | tf_op jit(solution)/shard_map/ppermute | solution.py:457
  52.6 4.8 %shard_map.100 = (f32[1024,512]{1,0:T(8,128)S(1)}, f32[1024,512]{1,0:T(8,128)S(1)}) custom-call(s32[4]{0:T(128)S(1)} %pad_add_fusion.c, bf16[512,512]{1,0:T(8,128)(2,1)S(1)} %get-tuple-element.116.qo, bf16[512,512]{1,0:T(8,128)(2,1)S(1)} %get-tuple-element.117.qp, bf16[512,512]{1,0:T(8,128)(2,1)S(1)} %get-tuple-element.101.ko, ...), custom_call_target="tpu_custom_call" | custom-call | flops 1000000 | bytes 1000 | tf_op jit(solution)/shard_map/pallas_call | solution.py:68
  58.7 2.7 %collective-permute-start.21 = (bf16[4,4,32,512]{3,2,1,0:T(8,128)(2,1)S(1)}, bf16[4,4,32,512]{3,2,1,0:T(8,128)(2,1)S(1)}, u32[]{:S(2)}, u32[]{:S(2)}) collective-permute-start(bf16[4,4,32,512]{3,2,1,0:T(8,128)(2,1)S(1)} %pad_maximum_fusion.3), channel_id=1, source_target_pairs={{0,24},{8,0},{16,8},{24,16},{1,25},{9,1},{17,9},{25,17},{2,26},{10... | collective-permute-start | bytes 1572872 | tf_op jit(solution)/shard_map/ppermute | solution.py:457
  62.8 1.8 %shard_map.102 = (bf16[4,4,32,512]{3,2,1,0:T(8,128)(2,1)S(1)}, bf16[4,4,32,512]{3,2,1,0:T(8,128)(2,1)S(1)}) custom-call(s32[4]{0:T(128)S(1)} %pad_add_fusion.c, bf16[4,4,128,1024]{3,2,1,0:T(8,128)(2,1)S(1)} %bitcast.69, bf16[1024,512]{1,0:T(8,128)(2,1)S(1)} %get-tuple-element.161.refs_0_.refs_1_, bf16[1024,512]{1,0:T(8,128)(2,1)S(1)} %get-tuple-element.162.refs_1_.refs_2_.refs_3_), custom_call_target="tpu_custom_call" | custom-call | flops 1000000 | bytes 1000 | tf_op jit(solution)/shard_map/pallas_call | solution.py:68
  66.9 1.8 %shard_map.104 = (bf16[4,4,32,512]{3,2,1,0:T(8,128)(2,1)S(1)}, bf16[4,4,32,512]{3,2,1,0:T(8,128)(2,1)S(1)}) custom-call(s32[4]{0:T(128)S(1)} %pad_add_fusion.c, bf16[4,4,128,1024]{3,2,1,0:T(8,128)(2,1)S(1)} %bitcast.70, bf16[1024,512]{1,0:T(8,128)(2,1)S(1)} %get-tuple-element.161.refs_0_.refs_1_, bf16[1024,512]{1,0:T(8,128)(2,1)S(1)} %get-tuple-element.162.refs_1_.refs_2_.refs_3_), custom_call_target="tpu_custom_call" | custom-call | flops 1000000 | bytes 1000 | tf_op jit(solution)/shard_map/pallas_call | solution.py:68
  68.7 2.9 %shard_map.103 = (bf16[4,4,32,512]{3,2,1,0:T(8,128)(2,1)S(1)}, bf16[4,4,32,512]{3,2,1,0:T(8,128)(2,1)S(1)}, bf16[4,4,32,512]{3,2,1,0:T(8,128)(2,1)S(1)}, bf16[4,4,32,512]{3,2,1,0:T(8,128)(2,1)S(1)}) custom-call(s32[4]{0:T(128)S(1)} %pad_add_fusion.c, bf16[4,4,128,1024]{3,2,1,0:T(8,128)(2,1)S(1)} %bitcast.71, ...), custom_call_target="tpu_custom_call" | custom-call | flops 1000000 | bytes 1000 | tf_op jit(solution)/shard_map/pallas_call | solution.py:68
  71.5 4.6 %shard_map.105 = bf16[512,2048]{1,0:T(8,128)(2,1)S(1)} custom-call(s32[4]{0:T(128)S(1)} %pad_add_fusion.c, bf16[1024,512]{1,0:T(8,128)(2,1)S(1)} %shard_map.98.g.refs_0_, bf16[1024,512]{1,0:T(8,128)(2,1)S(1)} %get-tuple-element.161.refs_0_.refs_1_, bf16[1024,512]{1,0:T(8,128)(2,1)S(1)} %get-tuple-element.162.refs_1_.refs_2_.refs_3_, ...), custom_call_target="tpu_custom_call" | custom-call | flops 1000000 | bytes 1000 | tf_op jit(solution)/shard_map/pallas_call | solution.py:68
  77.2 3.2 %collective-permute-start.22 = (bf16[512,2048]{1,0:T(8,128)(2,1)S(1)}, bf16[512,2048]{1,0:T(8,128)(2,1)S(1)}, u32[]{:S(2)}, u32[]{:S(2)}) collective-permute-start(bf16[512,2048]{1,0:T(8,128)(2,1)S(1)} %shard_map.105), channel_id=1, source_target_pairs={{0,4},{4,0},{1,5},{5,1},{2,6},{6,2},{3,7},{7,3},{8,12},{12,8},{9,1... | collective-permute-start | bytes 6291464 | tf_op jit(solution)/shard_map/ppermute | solution.py:461
  80.7 2.3 %collective-permute-start.24 = (bf16[4,4,32,512]{3,2,1,0:T(8,128)(2,1)S(1)}, bf16[4,4,32,512]{3,2,1,0:T(8,128)(2,1)S(1)}, u32[]{:S(2)}, u32[]{:S(2)}) collective-permute-start(bf16[4,4,32,512]{3,2,1,0:T(8,128)(2,1)S(1)} %pad_maximum_fusion.5), channel_id=1, source_target_pairs={{0,24},{8,0},{16,8},{24,16},{1,25},{9,1},{17,9},{25,17},{2,26},{10... | collective-permute-start | bytes 1572872 | tf_op jit(solution)/shard_map/ppermute | solution.py:457
  84.0 2.4 %collective-permute-start.26 = (bf16[18,32,512]{2,1,0:T(8,128)(2,1)S(1)}, bf16[18,32,512]{2,1,0:T(8,128)(2,1)S(1)}, u32[]{:S(2)}, u32[]{:S(2)}) collective-permute-start(bf16[18,32,512]{2,1,0:T(8,128)(2,1)S(1)} %pad_maximum_fusion.1), channel_id=1, source_target_pairs={{0,96},{32,0},{64,32},{96,64},{1,97},{33,1},{65,33},{97,65},{2,98}... | collective-permute-start | bytes 1769480 | tf_op jit(solution)/shard_map/ppermute | solution.py:457
  88.1 5.4 %shard_map.106 = bf16[512,2048]{1,0:T(8,128)(2,1)} custom-call(s32[4]{0:T(128)S(1)} %pad_add_fusion.c, bf16[1024,512]{1,0:T(8,128)(2,1)S(1)} %shard_map.98.g.refs_0_, bf16[1024,512]{1,0:T(8,128)(2,1)S(1)} %get-tuple-element.161.refs_0_.refs_1_, bf16[1024,512]{1,0:T(8,128)(2,1)S(1)} %get-tuple-element.162.refs_1_.refs_2_.refs_3_, ...), custom_call_target="tpu_custom_call" | custom-call | flops 1000000 | bytes 1000 | tf_op jit(solution)/shard_map/pallas_call | solution.py:68
  94.3 6.0 %collective-permute-done.23 = bf16[4,4,32,512]{3,2,1,0:T(8,128)(2,1)S(1)} collective-permute-done((bf16[4,4,32,512]{3,2,1,0:T(8,128)(2,1)S(1)}, bf16[4,4,32,512]{3,2,1,0:T(8,128)(2,1)S(1)}, u32[]{:S(2)}, u32[]{:S(2)}) %collective-permute-start.23) | collective-permute-done | bytes 524320 | tf_op jit(solution)/shard_map/ppermute | solution.py:457
  105.1 1.9 %collective-permute-done.31 = bf16[4,32,512]{2,1,0:T(8,128)(2,1)S(1)} collective-permute-done((bf16[4,32,512]{2,1,0:T(8,128)(2,1)S(1)}, bf16[4,32,512]{2,1,0:T(8,128)(2,1)S(1)}, u32[]{:S(2)}, u32[]{:S(2)}) %collective-permute-start.31) | collective-permute-done | bytes 131104 | tf_op jit(solution)/shard_map/ppermute | solution.py:457
  107.0 4.6 %collective-permute-done.29 = bf16[4,32,512]{2,1,0:T(8,128)(2,1)S(1)} collective-permute-done((bf16[4,32,512]{2,1,0:T(8,128)(2,1)S(1)}, bf16[4,32,512]{2,1,0:T(8,128)(2,1)S(1)}, u32[]{:S(2)}, u32[]{:S(2)}) %collective-permute-start.29) | collective-permute-done | bytes 131104 | tf_op jit(solution)/shard_map/ppermute | solution.py:457
  111.7 2.0 %collective-permute-done.32 = bf16[4,32,512]{2,1,0:T(8,128)(2,1)S(1)} collective-permute-done((bf16[4,32,512]{2,1,0:T(8,128)(2,1)S(1)}, bf16[4,32,512]{2,1,0:T(8,128)(2,1)S(1)}, u32[]{:S(2)}, u32[]{:S(2)}) %collective-permute-start.32) | collective-permute-done | bytes 131104 | tf_op jit(solution)/shard_map/ppermute | solution.py:457
  113.9 3.7 %collective-permute-start.33 = (bf16[32,1536]{1,0:T(8,128)(2,1)S(1)}, bf16[32,1536]{1,0:T(8,128)(2,1)S(1)}, u32[]{:S(2)}, u32[]{:S(2)}) collective-permute-start(bf16[32,1536]{1,0:T(8,128)(2,1)S(1)} %get-tuple-element.207), channel_id=1, source_target_pairs={{0,2},{1,3},{2,0},{3,1},{4,6},{5,7},{6,4},{7,5},{8,10},{9,11},{10,... | collective-permute-start | bytes 294920 | tf_op jit(solution)/shard_map/ppermute | solution.py:457
  119.5 2.1 %collective-permute-done.35 = bf16[32,1536]{1,0:T(8,128)(2,1)S(1)} collective-permute-done((bf16[32,1536]{1,0:T(8,128)(2,1)S(1)}, bf16[32,1536]{1,0:T(8,128)(2,1)S(1)}, u32[]{:S(2)}, u32[]{:S(2)}) %collective-permute-start.35) | collective-permute-done | bytes 98336 | tf_op jit(solution)/shard_map/ppermute | solution.py:457
  121.7 1.9 %collective-permute-done.34 = bf16[32,1536]{1,0:T(8,128)(2,1)S(1)} collective-permute-done((bf16[32,1536]{1,0:T(8,128)(2,1)S(1)}, bf16[32,1536]{1,0:T(8,128)(2,1)S(1)}, u32[]{:S(2)}, u32[]{:S(2)}) %collective-permute-start.34) | collective-permute-done | bytes 98336 | tf_op jit(solution)/shard_map/ppermute | solution.py:457
  123.7 3.6 %collective-permute-start.36 = (bf16[16,1536]{1,0:T(8,128)(2,1)S(1)}, bf16[16,1536]{1,0:T(8,128)(2,1)S(1)}, u32[]{:S(2)}, u32[]{:S(2)}) collective-permute-start(bf16[16,1536]{1,0:T(8,128)(2,1)S(1)} %slice_select_fusion), channel_id=1, source_target_pairs={{0,4},{4,0},{1,5},{5,1},{2,6},{6,2},{3,7},{7,3},{8,12},{12,8},{9,1... | collective-permute-start | bytes 147464 | tf_op jit(solution)/shard_map/ppermute | solution.py:461
  (97 shorter events, 28.7 us)
Async XLA Ops:
  0.6 7.2 %collective-permute-start = (bf16[512,2048]{1,0:T(8,128)(2,1)}, bf16[512,2048]{1,0:T(8,128)(2,1)S(1)}, u32[]{:S(2)}, u32[]{:S(2)}) collective-permute-start(bf16[512,2048]{1,0:T(8,128)(2,1)} %bitcast.72), channel_id=1, source_target_pairs={{0,4},{4,0},{1,5},{5,1},{2,6},{6,2},{3,7},{7,3},{8,12},{12,8},{9,1... | collective-permute-start | bytes 6291464 | tf_op jit(solution)/shard_map/ppermute | solution.py:461
  11.1 7.9 %collective-permute-start.3 = (bf16[512,128]{1,0:T(8,128)(2,1)S(1)}, bf16[512,128]{1,0:T(8,128)(2,1)S(1)}, u32[]{:S(2)}, u32[]{:S(2)}) collective-permute-start(bf16[512,128]{1,0:T(8,128)(2,1)S(1)} %get-tuple-element.99), channel_id=1, source_target_pairs={{0,16},{8,24},{16,0},{24,8},{1,17},{9,25},{17,1},{25,9},{2,18},{10... | collective-permute-start | bytes 393224 | tf_op jit(solution)/shard_map/ppermute | solution.py:457
  14.0 6.8 %collective-permute-start.2 = (bf16[512,128]{1,0:T(8,128)(2,1)S(1)}, bf16[512,128]{1,0:T(8,128)(2,1)S(1)}, u32[]{:S(2)}, u32[]{:S(2)}) collective-permute-start(bf16[512,128]{1,0:T(8,128)(2,1)S(1)} %get-tuple-element.99), channel_id=1, source_target_pairs={{0,24},{8,0},{16,8},{24,16},{1,25},{9,1},{17,9},{25,17},{2,26},{10... | collective-permute-start | bytes 393224 | tf_op jit(solution)/shard_map/ppermute | solution.py:457
  14.9 5.9 %collective-permute-start.1 = (bf16[512,128]{1,0:T(8,128)(2,1)S(1)}, bf16[512,128]{1,0:T(8,128)(2,1)S(1)}, u32[]{:S(2)}, u32[]{:S(2)}) collective-permute-start(bf16[512,128]{1,0:T(8,128)(2,1)S(1)} %get-tuple-element.99), channel_id=1, source_target_pairs={{0,8},{8,16},{16,24},{24,0},{1,9},{9,17},{17,25},{25,1},{2,10},{10... | collective-permute-start | bytes 393224 | tf_op jit(solution)/shard_map/ppermute | solution.py:457
  20.9 11.5 %collective-permute-start.7 = (bf16[512,512]{1,0:T(8,128)(2,1)S(1)}, bf16[512,512]{1,0:T(8,128)(2,1)S(1)}, u32[]{:S(2)}, u32[]{:S(2)}) collective-permute-start(bf16[512,512]{1,0:T(8,128)(2,1)S(1)} %get-tuple-element.110), channel_id=1, source_target_pairs={{0,4},{4,0},{1,5},{5,1},{2,6},{6,2},{3,7},{7,3},{8,12},{12,8},{9,1... | collective-permute-start | bytes 1572872 | tf_op jit(solution)/shard_map/ppermute | solution.py:461
  22.2 10.2 %collective-permute-start.6 = (bf16[512,128]{1,0:T(8,128)(2,1)S(1)}, bf16[512,128]{1,0:T(8,128)(2,1)S(1)}, u32[]{:S(2)}, u32[]{:S(2)}) collective-permute-start(bf16[512,128]{1,0:T(8,128)(2,1)S(1)} %add_convert_fusion.7), channel_id=1, source_target_pairs={{0,64},{32,96},{64,0},{96,32},{1,65},{33,97},{65,1},{97,33},{2,66}... | collective-permute-start | bytes 393224 | tf_op jit(solution)/shard_map/ppermute | solution.py:457
  25.1 7.3 %collective-permute-start.5 = (bf16[512,128]{1,0:T(8,128)(2,1)S(1)}, bf16[512,128]{1,0:T(8,128)(2,1)S(1)}, u32[]{:S(2)}, u32[]{:S(2)}) collective-permute-start(bf16[512,128]{1,0:T(8,128)(2,1)S(1)} %add_convert_fusion.7), channel_id=1, source_target_pairs={{0,96},{32,0},{64,32},{96,64},{1,97},{33,1},{65,33},{97,65},{2,98}... | collective-permute-start | bytes 393224 | tf_op jit(solution)/shard_map/ppermute | solution.py:457
  25.9 6.5 %collective-permute-start.4 = (bf16[512,128]{1,0:T(8,128)(2,1)S(1)}, bf16[512,128]{1,0:T(8,128)(2,1)S(1)}, u32[]{:S(2)}, u32[]{:S(2)}) collective-permute-start(bf16[512,128]{1,0:T(8,128)(2,1)S(1)} %add_convert_fusion.7), channel_id=1, source_target_pairs={{0,32},{32,64},{64,96},{96,0},{1,33},{33,65},{65,97},{97,1},{2,34}... | collective-permute-start | bytes 393224 | tf_op jit(solution)/shard_map/ppermute | solution.py:457
  35.3 11.6 %collective-permute-start.11 = (bf16[512,512]{1,0:T(8,128)(2,1)S(1)}, bf16[512,512]{1,0:T(8,128)(2,1)S(1)}, u32[]{:S(2)}, u32[]{:S(2)}) collective-permute-start(bf16[512,512]{1,0:T(8,128)(2,1)S(1)} %get-tuple-element.129), channel_id=1, source_target_pairs={{0,4},{4,0},{1,5},{5,1},{2,6},{6,2},{3,7},{7,3},{8,12},{12,8},{9,1... | collective-permute-start | bytes 1572872 | tf_op jit(solution)/shard_map/ppermute | solution.py:461
  36.3 10.5 %collective-permute-start.10 = (bf16[512,128]{1,0:T(8,128)(2,1)S(1)}, bf16[512,128]{1,0:T(8,128)(2,1)S(1)}, u32[]{:S(2)}, u32[]{:S(2)}) collective-permute-start(bf16[512,128]{1,0:T(8,128)(2,1)S(1)} %get-tuple-element.124), channel_id=1, source_target_pairs={{0,16},{8,24},{16,0},{24,8},{1,17},{9,25},{17,1},{25,9},{2,18},{10... | collective-permute-start | bytes 393224 | tf_op jit(solution)/shard_map/ppermute | solution.py:457
  38.5 8.2 %collective-permute-start.9 = (bf16[512,128]{1,0:T(8,128)(2,1)S(1)}, bf16[512,128]{1,0:T(8,128)(2,1)S(1)}, u32[]{:S(2)}, u32[]{:S(2)}) collective-permute-start(bf16[512,128]{1,0:T(8,128)(2,1)S(1)} %get-tuple-element.124), channel_id=1, source_target_pairs={{0,24},{8,0},{16,8},{24,16},{1,25},{9,1},{17,9},{25,17},{2,26},{10... | collective-permute-start | bytes 393224 | tf_op jit(solution)/shard_map/ppermute | solution.py:457
  39.4 7.3 %collective-permute-start.8 = (bf16[512,128]{1,0:T(8,128)(2,1)S(1)}, bf16[512,128]{1,0:T(8,128)(2,1)S(1)}, u32[]{:S(2)}, u32[]{:S(2)}) collective-permute-start(bf16[512,128]{1,0:T(8,128)(2,1)S(1)} %get-tuple-element.124), channel_id=1, source_target_pairs={{0,8},{8,16},{16,24},{24,0},{1,9},{9,17},{17,25},{25,1},{2,10},{10... | collective-permute-start | bytes 393224 | tf_op jit(solution)/shard_map/ppermute | solution.py:457
  46.9 11.4 %collective-permute-start.16 = (bf16[2,4,32,512]{3,2,1,0:T(8,128)(2,1)S(1)}, bf16[2,4,32,512]{3,2,1,0:T(8,128)(2,1)S(1)}, u32[]{:S(2)}, u32[]{:S(2)}) collective-permute-start(bf16[2,4,32,512]{3,2,1,0:T(8,128)(2,1)S(1)} %get-tuple-element.189), channel_id=1, source_target_pairs={{0,24},{8,0},{16,8},{24,16},{1,25},{9,1},{17,9},{25,17},{2,26},{10... | collective-permute-start | bytes 786440 | tf_op jit(solution)/shard_map/ppermute | solution.py:457
  49.1 9.2 %collective-permute-start.15 = (bf16[2,4,32,512]{3,2,1,0:T(8,128)(2,1)S(1)}, bf16[2,4,32,512]{3,2,1,0:T(8,128)(2,1)S(1)}, u32[]{:S(2)}, u32[]{:S(2)}) collective-permute-start(bf16[2,4,32,512]{3,2,1,0:T(8,128)(2,1)S(1)} %get-tuple-element.190), channel_id=1, source_target_pairs={{0,8},{8,16},{16,24},{24,0},{1,9},{9,17},{17,25},{25,1},{2,10},{10... | collective-permute-start | bytes 786440 | tf_op jit(solution)/shard_map/ppermute | solution.py:457
  49.1 8.3 %collective-permute-start.14 = (bf16[512,128]{1,0:T(8,128)(2,1)S(1)}, bf16[512,128]{1,0:T(8,128)(2,1)S(1)}, u32[]{:S(2)}, u32[]{:S(2)}) collective-permute-start(bf16[512,128]{1,0:T(8,128)(2,1)S(1)} %add_convert_fusion.6), channel_id=1, source_target_pairs={{0,64},{32,96},{64,0},{96,32},{1,65},{33,97},{65,1},{97,33},{2,66}... | collective-permute-start | bytes 393224 | tf_op jit(solution)/shard_map/ppermute | solution.py:457
  51.1 6.3 %collective-permute-start.13 = (bf16[512,128]{1,0:T(8,128)(2,1)S(1)}, bf16[512,128]{1,0:T(8,128)(2,1)S(1)}, u32[]{:S(2)}, u32[]{:S(2)}) collective-permute-start(bf16[512,128]{1,0:T(8,128)(2,1)S(1)} %add_convert_fusion.6), channel_id=1, source_target_pairs={{0,96},{32,0},{64,32},{96,64},{1,97},{33,1},{65,33},{97,65},{2,98}... | collective-permute-start | bytes 393224 | tf_op jit(solution)/shard_map/ppermute | solution.py:457
  52.0 6.3 %collective-permute-start.12 = (bf16[512,128]{1,0:T(8,128)(2,1)S(1)}, bf16[512,128]{1,0:T(8,128)(2,1)S(1)}, u32[]{:S(2)}, u32[]{:S(2)}) collective-permute-start(bf16[512,128]{1,0:T(8,128)(2,1)S(1)} %add_convert_fusion.6), channel_id=1, source_target_pairs={{0,32},{32,64},{64,96},{96,0},{1,33},{33,65},{65,97},{97,1},{2,34}... | collective-permute-start | bytes 393224 | tf_op jit(solution)/shard_map/ppermute | solution.py:457
  58.6 18.6 %collective-permute-start.20 = (bf16[4,4,32,512]{3,2,1,0:T(8,128)(2,1)S(1)}, bf16[4,4,32,512]{3,2,1,0:T(8,128)(2,1)S(1)}, u32[]{:S(2)}, u32[]{:S(2)}) collective-permute-start(bf16[4,4,32,512]{3,2,1,0:T(8,128)(2,1)S(1)} %pad_maximum_fusion.2), channel_id=1, source_target_pairs={{0,8},{8,16},{16,24},{24,0},{1,9},{9,17},{17,25},{25,1},{2,10},{10... | collective-permute-start | bytes 1572872 | tf_op jit(solution)/shard_map/ppermute | solution.py:457
  58.7 18.4 %collective-permute-start.21 = (bf16[4,4,32,512]{3,2,1,0:T(8,128)(2,1)S(1)}, bf16[4,4,32,512]{3,2,1,0:T(8,128)(2,1)S(1)}, u32[]{:S(2)}, u32[]{:S(2)}) collective-permute-start(bf16[4,4,32,512]{3,2,1,0:T(8,128)(2,1)S(1)} %pad_maximum_fusion.3), channel_id=1, source_target_pairs={{0,24},{8,0},{16,8},{24,16},{1,25},{9,1},{17,9},{25,17},{2,26},{10... | collective-permute-start | bytes 1572872 | tf_op jit(solution)/shard_map/ppermute | solution.py:457
  64.6 12.6 %collective-permute-start.19 = (bf16[4,4,32,512]{3,2,1,0:T(8,128)(2,1)S(1)}, bf16[4,4,32,512]{3,2,1,0:T(8,128)(2,1)S(1)}, u32[]{:S(2)}, u32[]{:S(2)}) collective-permute-start(bf16[4,4,32,512]{3,2,1,0:T(8,128)(2,1)S(1)} %get-tuple-element.156), channel_id=1, source_target_pairs={{0,32},{32,64},{64,96},{96,0},{1,33},{33,65},{65,97},{97,1},{2,34}... | collective-permute-start | bytes 1572872 | tf_op jit(solution)/shard_map/ppermute | solution.py:457
  65.3 10.9 %collective-permute-start.18 = (bf16[2,4,32,512]{3,2,1,0:T(8,128)(2,1)S(1)}, bf16[2,4,32,512]{3,2,1,0:T(8,128)(2,1)S(1)}, u32[]{:S(2)}, u32[]{:S(2)}) collective-permute-start(bf16[2,4,32,512]{3,2,1,0:T(8,128)(2,1)S(1)} %get-tuple-element.205), channel_id=1, source_target_pairs={{0,24},{8,0},{16,8},{24,16},{1,25},{9,1},{17,9},{25,17},{2,26},{10... | collective-permute-start | bytes 786440 | tf_op jit(solution)/shard_map/ppermute | solution.py:457
  66.6 10.6 %collective-permute-start.17 = (bf16[2,4,32,512]{3,2,1,0:T(8,128)(2,1)S(1)}, bf16[2,4,32,512]{3,2,1,0:T(8,128)(2,1)S(1)}, u32[]{:S(2)}, u32[]{:S(2)}) collective-permute-start(bf16[2,4,32,512]{3,2,1,0:T(8,128)(2,1)S(1)} %get-tuple-element.206), channel_id=1, source_target_pairs={{0,8},{8,16},{16,24},{24,0},{1,9},{9,17},{17,25},{25,1},{2,10},{10... | collective-permute-start | bytes 786440 | tf_op jit(solution)/shard_map/ppermute | solution.py:457
  77.2 10.9 %collective-permute-start.22 = (bf16[512,2048]{1,0:T(8,128)(2,1)S(1)}, bf16[512,2048]{1,0:T(8,128)(2,1)S(1)}, u32[]{:S(2)}, u32[]{:S(2)}) collective-permute-start(bf16[512,2048]{1,0:T(8,128)(2,1)S(1)} %shard_map.105), channel_id=1, source_target_pairs={{0,4},{4,0},{1,5},{5,1},{2,6},{6,2},{3,7},{7,3},{8,12},{12,8},{9,1... | collective-permute-start | bytes 6291464 | tf_op jit(solution)/shard_map/ppermute | solution.py:461
  80.7 13.7 %collective-permute-start.24 = (bf16[4,4,32,512]{3,2,1,0:T(8,128)(2,1)S(1)}, bf16[4,4,32,512]{3,2,1,0:T(8,128)(2,1)S(1)}, u32[]{:S(2)}, u32[]{:S(2)}) collective-permute-start(bf16[4,4,32,512]{3,2,1,0:T(8,128)(2,1)S(1)} %pad_maximum_fusion.5), channel_id=1, source_target_pairs={{0,24},{8,0},{16,8},{24,16},{1,25},{9,1},{17,9},{25,17},{2,26},{10... | collective-permute-start | bytes 1572872 | tf_op jit(solution)/shard_map/ppermute | solution.py:457
  83.5 16.9 %collective-permute-start.25 = (bf16[18,32,512]{2,1,0:T(8,128)(2,1)S(1)}, bf16[18,32,512]{2,1,0:T(8,128)(2,1)S(1)}, u32[]{:S(2)}, u32[]{:S(2)}) collective-permute-start(bf16[18,32,512]{2,1,0:T(8,128)(2,1)S(1)} %pad_maximum_fusion), channel_id=1, source_target_pairs={{0,32},{32,64},{64,96},{96,0},{1,33},{33,65},{65,97},{97,1},{2,34}... | collective-permute-start | bytes 1769480 | tf_op jit(solution)/shard_map/ppermute | solution.py:457
  84.0 16.4 %collective-permute-start.26 = (bf16[18,32,512]{2,1,0:T(8,128)(2,1)S(1)}, bf16[18,32,512]{2,1,0:T(8,128)(2,1)S(1)}, u32[]{:S(2)}, u32[]{:S(2)}) collective-permute-start(bf16[18,32,512]{2,1,0:T(8,128)(2,1)S(1)} %pad_maximum_fusion.1), channel_id=1, source_target_pairs={{0,96},{32,0},{64,32},{96,64},{1,97},{33,1},{65,33},{97,65},{2,98}... | collective-permute-start | bytes 1769480 | tf_op jit(solution)/shard_map/ppermute | solution.py:457
  86.5 13.9 %collective-permute-start.23 = (bf16[4,4,32,512]{3,2,1,0:T(8,128)(2,1)S(1)}, bf16[4,4,32,512]{3,2,1,0:T(8,128)(2,1)S(1)}, u32[]{:S(2)}, u32[]{:S(2)}) collective-permute-start(bf16[4,4,32,512]{3,2,1,0:T(8,128)(2,1)S(1)} %pad_maximum_fusion.4), channel_id=1, source_target_pairs={{0,8},{8,16},{16,24},{24,0},{1,9},{9,17},{17,25},{25,1},{2,10},{10... | collective-permute-start | bytes 1572872 | tf_op jit(solution)/shard_map/ppermute | solution.py:457
  101.1 10.5 %collective-permute-start.28 = (bf16[2,4,32,512]{3,2,1,0:T(8,128)(2,1)S(1)}, bf16[2,4,32,512]{3,2,1,0:T(8,128)(2,1)S(1)}, u32[]{:S(2)}, u32[]{:S(2)}) collective-permute-start(bf16[2,4,32,512]{3,2,1,0:T(8,128)(2,1)S(1)} %pad_maximum_fusion.8), channel_id=1, source_target_pairs={{0,96},{32,0},{64,32},{96,64},{1,97},{33,1},{65,33},{97,65},{2,98}... | collective-permute-start | bytes 786440 | tf_op jit(solution)/shard_map/ppermute | solution.py:457
  102.7 8.9 %collective-permute-start.27 = (bf16[2,4,32,512]{3,2,1,0:T(8,128)(2,1)S(1)}, bf16[2,4,32,512]{3,2,1,0:T(8,128)(2,1)S(1)}, u32[]{:S(2)}, u32[]{:S(2)}) collective-permute-start(bf16[2,4,32,512]{3,2,1,0:T(8,128)(2,1)S(1)} %pad_maximum_fusion.7), channel_id=1, source_target_pairs={{0,32},{32,64},{64,96},{96,0},{1,33},{33,65},{65,97},{97,1},{2,34}... | collective-permute-start | bytes 786440 | tf_op jit(solution)/shard_map/ppermute | solution.py:457
  102.9 8.7 %collective-permute-start.29 = (bf16[4,32,512]{2,1,0:T(8,128)(2,1)S(1)}, bf16[4,32,512]{2,1,0:T(8,128)(2,1)S(1)}, u32[]{:S(2)}, u32[]{:S(2)}) collective-permute-start(bf16[4,32,512]{2,1,0:T(8,128)(2,1)S(1)} %get-tuple-element.194), channel_id=1, source_target_pairs={{0,64},{32,96},{64,0},{96,32},{1,65},{33,97},{65,1},{97,33},{2,66}... | collective-permute-start | bytes 393224 | tf_op jit(solution)/shard_map/ppermute | solution.py:457
  104.2 7.6 %collective-permute-start.30 = (bf16[4,32,512]{2,1,0:T(8,128)(2,1)S(1)}, bf16[4,32,512]{2,1,0:T(8,128)(2,1)S(1)}, u32[]{:S(2)}, u32[]{:S(2)}) collective-permute-start(bf16[4,32,512]{2,1,0:T(8,128)(2,1)S(1)} %get-tuple-element.200), channel_id=1, source_target_pairs={{0,16},{8,24},{16,0},{24,8},{1,17},{9,25},{17,1},{25,9},{2,18},{10... | collective-permute-start | bytes 393224 | tf_op jit(solution)/shard_map/ppermute | solution.py:457
  107.0 6.7 %collective-permute-start.32 = (bf16[4,32,512]{2,1,0:T(8,128)(2,1)S(1)}, bf16[4,32,512]{2,1,0:T(8,128)(2,1)S(1)}, u32[]{:S(2)}, u32[]{:S(2)}) collective-permute-start(bf16[4,32,512]{2,1,0:T(8,128)(2,1)S(1)} %get-tuple-element.183), channel_id=1, source_target_pairs={{0,8},{8,16},{16,24},{24,0},{1,9},{9,17},{17,25},{25,1},{2,10},{10... | collective-permute-start | bytes 393224 | tf_op jit(solution)/shard_map/ppermute | solution.py:457
  (6 other events, 31.7 us)

commit v3 on v2

--- a/solution.py
+++ b/solution.py
@@ -14,6 +14,8 @@
 BF = jnp.bfloat16
 F32 = jnp.float32
 MB = 1 << 20
+LOW = slice(0, 256)
+HIGH = slice(256, 512)
 
 
 def dot(a, b, ca=1, cb=0):
@@ -103,7 +105,7 @@
 
 
 def project_own(core, tok, wk, wv):
-    def kernel(c, t, b, d, k, v, s, bh, dh, tv, sems):
+    def kernel(c, t, b, d, k, v, s, low, bh, dh, tv, sems):
         copies = [[], [], []]
         for i in range(4):
             rows, part = pl.ds(i * 512, 512), pl.ds(i * 128, 128)
@@ -120,27 +122,31 @@
                 copy.wait()
             out[...] = dot(tv[...], w[...]).astype(BF)
         for h in range(4):
-            s[head(h), :] = dot(k[:, head(h)], v[:, head(h)], 0, 0).astype(BF)
+            first = dot(k[LOW, head(h)], v[LOW, head(h)], 0, 0)
+            low[head(h), :] = first.astype(BF)
+            s[head(h), :] = (first + dot(k[HIGH, head(h)], v[HIGH, head(h)], 0, 0)).astype(BF)
 
     row, weight = ((TOK, 512), BF), ((2048, 512), BF)
     return local(
         kernel,
         core,
         in_hbm(tok, wk, wv),
-        [row] * 2 + [((512, DH), BF)] + [weight] * 2,
+        [row] * 2 + [((512, DH), BF)] * 2 + [weight] * 2,
         hbm_in=3,
         scratch=[pltpu.VMEM((TOK, 2048), BF), pltpu.SemaphoreType.DMA((3, 4))],
     )
 
 
 def project_partner(core, tok, wk, wv, state, wq):
-    def kernel(c, t, b, d, so, a, k, v, s, total, ah, sem):
+    def kernel(c, t, b, d, so, a, k, v, s, low, total, ah, sem):
         copy = pltpu.make_async_copy(a.at[:, half_of(c[0])], ah, sem)
         copy.start()
         k[...] = dot(t[...], b[...]).astype(BF)
         v[...] = dot(t[...], d[...]).astype(BF)
         for h in range(4):
-            st = dot(k[:, head(h)], v[:, head(h)], 0, 0).astype(BF)
+            first = dot(k[LOW, head(h)], v[LOW, head(h)], 0, 0)
+            low[head(h), :] = first.astype(BF)
+            st = (first + dot(k[HIGH, head(h)], v[HIGH, head(h)], 0, 0)).astype(BF)
             s[head(h), :] = st
             total[head(h), :] = (st.astype(F32) + so[head(h), :].astype(F32)).astype(BF)
         copy.wait()
@@ -150,28 +156,21 @@
         kernel,
         core,
         [tok, wk, wv, state, *in_hbm(wq)],
-        [row] * 2 + [((512, DH), BF)] * 2 + [((2048, 512), BF)],
+        [row] * 2 + [((512, DH), BF)] * 3 + [((2048, 512), BF)],
         hbm_in=1,
         scratch=[pltpu.SemaphoreType.DMA],
     )
 
 
-LOW = slice(0, 256)
-HIGH = slice(256, 512)
-
-
-def forward_pairs(q, k, v):
-    s00 = causal(dot(q[LOW], k[LOW], 1, 1))
-    s10 = dot(q[HIGH], k[LOW], 1, 1).astype(BF)
-    s11 = causal(dot(q[HIGH], k[HIGH], 1, 1))
-    return dot(s00, v[LOW]), dot(s10, v[LOW]) + dot(s11, v[HIGH])
-
-
-def backward_pairs(q, k, x):
-    s00 = causal(dot(k[LOW], q[LOW], 1, 1), True)
-    s01 = dot(k[LOW], q[HIGH], 1, 1).astype(BF)
-    s11 = causal(dot(k[HIGH], q[HIGH], 1, 1), True)
-    return dot(s00, x[LOW]) + dot(s01, x[HIGH]), dot(s11, x[HIGH])
+HALVES = (LOW, HIGH)
+
+
+def diagonal(q, k, x):
+    return [dot(causal(dot(q[r], k[r], 1, 1)), x[r]) for r in HALVES]
+
+
+def diagonal_turned(q, k, x):
+    return [dot(causal(dot(k[r], q[r], 1, 1), True), x[r]) for r in HALVES]
 
 
 def masked_sum(refs, at, reverse):
@@ -200,9 +199,9 @@
             copy.start()
         qo[...] = dot(t[...], a[...]).astype(BF)
 
-        @looped_head
+        @each_head
         def _(h):
-            low, high = forward_pairs(qo[:, head(h)], ko[:, head(h)], vo[:, head(h)])
+            low, high = diagonal(qo[:, head(h)], ko[:, head(h)], vo[:, head(h)])
             out[:256, head(h)] = low
             out[256:, head(h)] = high
 
@@ -236,56 +235,68 @@
     )[0]
 
 
-def normed(core, i_o, i_p, q_o, q_p, state_o, state_p, along_x, along_y, cot, cot_p):
-    def kernel(c, io, ip, qo, qp, so, sp, x1, x3, x2, y1, y3, y2, co, cp, *outs):
-        ao, ap, g, po, pp, bo, bp, total = outs
+def normed(core, i_o, i_p, q_o, q_p, states, lows, along_x, along_y, cot, cot_p):
+    def kernel(c, io, ip, qo, qp, so, sp, lo, lp, x1, x3, x2, y1, y3, y2, co, cp, *outs):
+        ao, ap, g, po, pp, ho, hp, bo, bp, eo, ep, total = outs
         before = masked_sum((x1, x3, x2), c[2], False) + masked_sum((y1, y3, y2), c[1], False)
         late = c[0].astype(F32)
-        po[...] = (before + sp[...].astype(F32) * late).astype(BF)
-        pp[...] = (before + so[...].astype(F32) * (1.0 - late)).astype(BF)
+        base_o = before + sp[...].astype(F32) * late
+        base_p = before + so[...].astype(F32) * (1.0 - late)
+        po[...] = base_o.astype(BF)
+        pp[...] = base_p.astype(BF)
+        ho[...] = (base_o + lo[...].astype(F32)).astype(BF)
+        hp[...] = (base_p + lp[...].astype(F32)).astype(BF)
 
         @each_head
         def _(h):
-            backs = []
-            for n, (it, q, p, a, b) in enumerate(((io, qo, po, ao, bo), (ip, qp, pp, ap, bp))):
-                rows = slice(n * TOK, n * TOK + TOK)
-                qh = q[:, head(h)]
-                mixed = it[:, head(h)] + dot(qh, p[head(h), :])
-                inverse = lax.rsqrt(jnp.mean(mixed * mixed, axis=-1, keepdims=True) + EPS)
-                nm = mixed * inverse
-                up = (co if n == 0 else cp)[:, head(h)].astype(F32)
-                a[:, head(h)] = nm.astype(BF)
-                gm = ((up - nm * jnp.mean(up * nm, axis=-1, keepdims=True)) * inverse).astype(BF)
-                g[rows, head(h)] = gm
-                back = dot(qh, gm, 0, 0).astype(BF)
+            both = None
+            for n, (it, q, p, up_h, a, ct, b, e) in enumerate(
+                ((io, qo, po, ho, ao, co, bo, eo), (ip, qp, pp, hp, ap, cp, bp, ep))
+            ):
+                back = None
+                for r, prefix in zip(HALVES, (p, up_h)):
+                    qh = q[r, head(h)]
+                    mixed = it[r, head(h)] + dot(qh, prefix[head(h), :])
+                    inverse = lax.rsqrt(jnp.mean(mixed * mixed, axis=-1, keepdims=True) + EPS)
+                    nm = mixed * inverse
+                    up = ct[r, head(h)].astype(F32)
+                    a[r, head(h)] = nm.astype(BF)
+                    mean = jnp.mean(up * nm, axis=-1, keepdims=True)
+                    gm = ((up - nm * mean) * inverse).astype(BF)
+                    g[n * TOK + r.start : n * TOK + r.stop, head(h)] = gm
+                    part = dot(qh, gm, 0, 0)
+                    if r is HIGH:
+                        e[head(h), :] = part.astype(BF)
+                    back = part if back is None else back + part
+                back = back.astype(BF)
                 b[head(h), :] = back
-                backs.append(back.astype(F32))
-            total[head(h), :] = (backs[0] + backs[1]).astype(BF)
+                both = back.astype(F32) if both is None else both + back.astype(F32)
+            total[head(h), :] = both.astype(BF)
 
     state = ((512, DH), BF)
     return local(
         kernel,
         core,
-        [i_o, i_p, q_o, q_p, state_o, state_p, *along_x, *along_y, cot, cot_p],
-        [((TOK, 512), BF)] * 2 + [((2 * TOK, 512), BF)] + [state] * 5,
-    )
-
-
-def grad_q_of(core, k_o, k_p, v_o, v_p, g, p_o, p_p):
-    def kernel(c, ko, kp, vo, vp, gr, po, pp, dq):
+        [i_o, i_p, q_o, q_p, *states, *lows, *along_x, *along_y, cot, cot_p],
+        [((TOK, 512), BF)] * 2 + [((2 * TOK, 512), BF)] + [state] * 9,
+    )
+
+
+def grad_q_of(core, k_o, k_p, v_o, v_p, g, p_o, p_p, h_o, h_p):
+    def kernel(c, ko, kp, vo, vp, gr, po, pp, ho, hp, dq):
         @each_head
         def _(h):
-            for n, (k, v, p) in enumerate(((ko, vo, po), (kp, vp, pp))):
+            for n, (k, v, p, up) in enumerate(((ko, vo, po, ho), (kp, vp, pp, hp))):
                 gh = gr[n * TOK : n * TOK + TOK, head(h)]
-                past = dot(gh, p[head(h), :], 1, 1)
-                low, high = forward_pairs(gh, v[:, head(h)], k[:, head(h)])
-                dq[n * TOK : n * TOK + 256, head(h)] = (low + past[LOW]).astype(BF)
-                dq[n * TOK + 256 : n * TOK + 512, head(h)] = (high + past[HIGH]).astype(BF)
-
-    return local(
-        kernel,
-        core,
-        [k_o, k_p, v_o, v_p, g, p_o, p_p],
+                parts = diagonal(gh, v[:, head(h)], k[:, head(h)])
+                for r, part, prefix in zip(HALVES, parts, (p, up)):
+                    past = dot(gh[r], prefix[head(h), :], 1, 1)
+                    dq[n * TOK + r.start : n * TOK + r.stop, head(h)] = (part + past).astype(BF)
+
+    return local(
+        kernel,
+        core,
+        [k_o, k_p, v_o, v_p, g, p_o, p_p, h_o, h_p],
         [((2 * TOK, 512), BF)],
     )[0]
 
@@ -298,7 +309,7 @@
                 qh, kh, vh = q[:, head(h)], k[:, head(h)], v[:, head(h)]
                 gh = gr[n * TOK : n * TOK + TOK, head(h)]
                 for left, right, x, out in ((gh, vh, qh, dk), (qh, kh, gh, dv)):
-                    low, high = backward_pairs(left, right, x)
+                    low, high = diagonal_turned(left, right, x)
                     out[n * TOK : n * TOK + 256, head(h)] = low
                     out[n * TOK + 256 : n * TOK + 512, head(h)] = high
 
@@ -310,23 +321,26 @@
     )
 
 
-def grads_after(core, k_o, k_p, v_o, v_p, dk, dv, back_o, back_p, along_x, along_y):
-    def kernel(c, ko, kp, vo, vp, ak, av, bo, bp, x1, x3, x2, y1, y3, y2, ok, ov):
+def grads_after(core, k_o, k_p, v_o, v_p, dk, dv, backs, ends, along_x, along_y):
+    def kernel(c, ko, kp, vo, vp, ak, av, bo, bp, eo, ep, x1, x3, x2, y1, y3, y2, ok, ov):
         after = masked_sum((x1, x3, x2), c[2], True) + masked_sum((y1, y3, y2), c[1], True)
         late = c[0].astype(F32)
-        s_o = (after + bp[...].astype(F32) * (1.0 - late)).astype(BF)
-        s_p = (after + bo[...].astype(F32) * late).astype(BF)
-        for n, (k, v, s) in enumerate(((ko, vo, s_o), (kp, vp, s_p))):
-            rows = slice(n * TOK, n * TOK + TOK)
-            for h in range(4):
-                sh = s[head(h), :]
-                ok[rows, head(h)] = (ak[rows, head(h)] + dot(v[:, head(h)], sh, 1, 1)).astype(BF)
-                ov[rows, head(h)] = (av[rows, head(h)] + dot(k[:, head(h)], sh)).astype(BF)
-
-    return local(
-        kernel,
-        core,
-        [k_o, k_p, v_o, v_p, dk, dv, back_o, back_p, *along_x, *along_y],
+        s_o = after + bp[...].astype(F32) * (1.0 - late)
+        s_p = after + bo[...].astype(F32) * late
+        for n, (k, v, s, e) in enumerate(((ko, vo, s_o, eo), (kp, vp, s_p, ep))):
+            low = (s + e[...].astype(F32)).astype(BF)
+            for r, suffix in zip(HALVES, (low, s.astype(BF))):
+                rows = slice(n * TOK + r.start, n * TOK + r.stop)
+                for h in range(4):
+                    sh = suffix[head(h), :]
+                    kh, vh = k[r, head(h)], v[r, head(h)]
+                    ok[rows, head(h)] = (ak[rows, head(h)] + dot(vh, sh, 1, 1)).astype(BF)
+                    ov[rows, head(h)] = (av[rows, head(h)] + dot(kh, sh)).astype(BF)
+
+    return local(
+        kernel,
+        core,
+        [k_o, k_p, v_o, v_p, dk, dv, *backs, *ends, *along_x, *along_y],
         [((2 * TOK, 512), BF)] * 2,
     )
 
@@ -372,7 +386,8 @@
                         out[dx, dy, (z - c[3] + 4) % 4, here, :] = part[row : row + 16, :]
             return carry
 
-        lax.fori_loop(0, 4, at_y, 0)
+        for y in range(4):
+            at_y(y, 0)
 
     return local(
         kernel,
@@ -498,8 +513,10 @@
     tok_p = swap(tok_o)
     late = c == 1
 
-    k_o, v_o, state_o, w_k, w_v = project_own(core, tok_o, w_key, w_value)
-    k_p, v_p, state_p, total, w_q = project_partner(core, tok_p, w_k, w_v, state_o, w_query)
+    k_o, v_o, state_o, low_o, w_k, w_v = project_own(core, tok_o, w_key, w_value)
+    k_p, v_p, state_p, low_p, total, w_q = project_partner(
+        core, tok_p, w_k, w_v, state_o, w_query
+    )
     weights = (w_q, w_k, w_v)
     along_x = pieces(total, "x")
     q_o, i_o, cot, cot_s = within(core, tok_o, w_q, k_o, v_o, cotangent[0])
@@ -511,12 +528,13 @@
     q_p, i_p = within(core, tok_p, w_q, k_p, v_p)
     tt = turned(core, tok_t, tok_p)
     *along_y, tt, cot_p, q_p, i_p = together(*along_y, tt, cot_p, q_p, i_p)
-    a_o, a_p, g, p_o, p_p, back_o, back_p, total = normed(
-        core, i_o, i_p, q_o, q_p, state_o, state_p, along_x, along_y, cot, cot_p
+    states, lows = (state_o, state_p), (low_o, low_p)
+    a_o, a_p, g, p_o, p_p, h_o, h_p, back_o, back_p, end_o, end_p, total = normed(
+        core, i_o, i_p, q_o, q_p, states, lows, along_x, along_y, cot, cot_p
     )
     along_x = pieces(total, "x")
     a_r = swap(a_p)
-    dq = grad_q_of(core, k_o, k_p, v_o, v_p, g, p_o, p_p)
+    dq = grad_q_of(core, k_o, k_p, v_o, v_p, g, p_o, p_p, h_o, h_p)
     part_q = weight_grad_all(core, tt, dq)
     row, part_q, g, a_r = together(f32_sum(total, *along_x), part_q, g, a_r)
     along_y = pieces(row, "y")
@@ -525,7 +543,7 @@
     *along_y, dk, dv, c0, c1 = together(*along_y, dk, dv, *came_q)
     last_q = ring_near(part_q[1], part_q[3], (c0, c1), "x")
     dk, dv = grads_after(
-        core, k_o, k_p, v_o, v_p, dk, dv, back_o, back_p, along_x, along_y
+        core, k_o, k_p, v_o, v_p, dk, dv, (back_o, back_p), (end_o, end_p), along_x, along_y
     )
     far_k, far_v = weight_grad(core, tt, [(dk, "x", 2), (dv, "y", 2)])
     far_k, far_v, dk, dv = together(far_k, far_v, dk, dv)

time: 129 us -> 131 us (1.016)
  Pallas kernels: 53.1 us -> 51.1 us
  waiting for transfers between devices: 24.6 us -> 26.6 us
  starting transfers between devices: 48 us -> 49.6 us
    pallas_call x16, Pallas kernels: 50.8 us -> 48.8 us  [local(): pl.pallas_call(kernel, out_shape=[jax.ShapeDtypeStruct(s, d) for s, d in...]
    ppermute x32, waiting for transfers between devices: 23.7 us -> 25.7 us  [shift(): return lax.ppermute(v, axis, [(i, (i + d) % n) for i in range(n)])]
    ppermute x32, starting transfers between devices: 37.4 us -> 38.8 us  [shift(): return lax.ppermute(v, axis, [(i, (i + d) % n) for i in range(n)])]
  transfers between devices with their start and end apart: 37 -> 37, of which waited for: 14 -> 16; matrix products, arithmetic and copies ran while one was open for 1% -> 1% of each run, Pallas kernels for 35% -> 31%
where the time goes in v3:
time: 131 us
  Pallas kernels  51.1 us (39%)
  starting transfers between devices  49.6 us (38%)
  waiting for transfers between devices  26.6 us (20%)
  other arithmetic  2.19 us (2%)
    pallas_call x16, Pallas kernels, local(): pl.pallas_call(kernel, out_shape=[jax.ShapeDtypeStruct(s, d) for s, d in...  48.8 us
    ppermute x32, starting transfers between devices, shift(): return lax.ppermute(v, axis, [(i, (i + d) % n) for i in range(n)])  38.8 us
    ppermute x32, waiting for transfers between devices, shift(): return lax.ppermute(v, axis, [(i, (i + d) % n) for i in range(n)])  25.7 us
    ppermute x5, starting transfers between devices, swap(): return lax.ppermute(v, 'c', [(0, 1), (1, 0)])  10.8 us
  transfers between devices with their start and end apart: 37, of which 16 were waited for; matrix products, arithmetic and copies ran while one was open for 1% of the time, Pallas kernels for 31%

profile of v3, /device:TPU:1, one launch (start us, length us, event | category | flops | bytes accessed | tf_op | source)
XLA Modules:
  0.0 130.8 jit_solution(16777959176657001458)
XLA Ops:
  2.2 5.6 %shard_map.92 = (bf16[512,512]{1,0:T(8,128)(2,1)S(1)}, bf16[512,512]{1,0:T(8,128)(2,1)S(1)}, bf16[512,128]{1,0:T(8,128)(2,1)S(1)}, bf16[512,128]{1,0:T(8,128)(2,...) custom-call(s32[4]{0:T(128)S(1)} %pad_add_fusion.c, bf16[512,2048]{1,0:T(8,128)(2,1)} %bitcast.73, ...), custom_call_target="tpu_custom_call" | custom-call | flops 1000000 | bytes 1000 | tf_op jit(solution)/shard_map/pallas_call | solution.py:70
  7.9 4.8 %shard_map.93 = (bf16[512,512]{1,0:T(8,128)(2,1)S(1)}, bf16[512,512]{1,0:T(8,128)(2,1)S(1)}, bf16[512,128]{1,0:T(8,128)(2,1)S(1)}, bf16[512,128]{1,0:T(8,128)(2,...) custom-call(s32[4]{0:T(128)S(1)} %pad_add_fusion.c, ...), custom_call_target="tpu_custom_call" | custom-call | flops 1000000 | bytes 1000 | tf_op jit(solution)/shard_map/pallas_call | solution.py:70
  12.6 2.9 %collective-permute-start.3 = (bf16[512,128]{1,0:T(8,128)(2,1)S(1)}, bf16[512,128]{1,0:T(8,128)(2,1)S(1)}, u32[]{:S(2)}, u32[]{:S(2)}) collective-permute-start(bf16[512,128]{1,0:T(8,128)(2,1)S(1)} %get-tuple-element.105), channel_id=1, source_target_pairs={{0,16},{8,24},{16,0},{24,8},{1,17},{9,25},{17,1},{25,9},{2,18},{10... | collective-permute-start | bytes 393224 | tf_op jit(solution)/shard_map/ppermute | solution.py:472
  17.0 2.8 %shard_map.94 = (bf16[512,512]{1,0:T(8,128)(2,1)S(1)}, f32[512,512]{1,0:T(8,128)S(1)}, bf16[512,512]{1,0:T(8,128)(2,1)S(1)}, bf16[512,512]{1,0:T(8,128)(2,1)S(1)}) custom-call(s32[4]{0:T(128)S(1)} %pad_add_fusion.c, bf16[512,2048]{1,0:T(8,128)(2,1)S(1)} %bitcast.74, bf16[2048,512]{1,0:T(8,128)(2,1)S(1)} %get-tuple-element.106.a.refs_3_, ...), custom_call_target="tpu_custom_call" | custom-call | flops 1000000 | bytes 1000 | tf_op jit(solution)/shard_map/pallas_call | solution.py:70
  19.9 2.5 %collective-permute-done.2.x3 = bf16[512,128]{1,0:T(8,128)(2,1)S(1)} collective-permute-done((bf16[512,128]{1,0:T(8,128)(2,1)S(1)}, bf16[512,128]{1,0:T(8,128)(2,1)S(1)}, u32[]{:S(2)}, u32[]{:S(2)}) %collective-permute-start.2) | collective-permute-done | bytes 131104 | tf_op jit(solution)/shard_map/ppermute | solution.py:472
  23.7 2.9 %collective-permute-start.6 = (bf16[512,128]{1,0:T(8,128)(2,1)S(1)}, bf16[512,128]{1,0:T(8,128)(2,1)S(1)}, u32[]{:S(2)}, u32[]{:S(2)}) collective-permute-start(bf16[512,128]{1,0:T(8,128)(2,1)S(1)} %add_convert_fusion.7), channel_id=1, source_target_pairs={{0,64},{32,96},{64,0},{96,32},{1,65},{33,97},{65,1},{97,33},{2,66}... | collective-permute-start | bytes 393224 | tf_op jit(solution)/shard_map/ppermute | solution.py:472
  28.1 2.3 %shard_map.95 = bf16[2048,1024]{1,0:T(8,128)(2,1)S(1)} custom-call(s32[4]{0:T(128)S(1)} %pad_add_fusion.c, bf16[512,2048]{1,0:T(8,128)(2,1)S(1)} %bitcast.75, bf16[512,2048]{1,0:T(8,128)(2,1)S(1)} %collective-permute-done.t.tp), custom_call_target="tpu_custom_call" | custom-call | flops 1000000 | bytes 8388608 | tf_op jit(solution)/shard_map/pallas_call | solution.py:52
  30.4 2.5 %shard_map.96 = (bf16[512,512]{1,0:T(8,128)(2,1)S(1)}, f32[512,512]{1,0:T(8,128)S(1)}) custom-call(s32[4]{0:T(128)S(1)} %pad_add_fusion.c, bf16[512,2048]{1,0:T(8,128)(2,1)S(1)} %collective-permute-done.t.tp, bf16[2048,512]{1,0:T(8,128)(2,1)S(1)} %get-tuple-element.106.a.refs_3_, bf16[512,512]{1,0:T(8,128)(2,1)S(1)} %get-tuple-element.117.ko.kp, ...), custom_call_target="tpu_custom_call" | custom-call | flops 1000000 | bytes 1000 | tf_op jit(solution)/shard_map/pallas_call | solution.py:70
  33.4 4.1 %shard_map.97 = (bf16[512,512]{1,0:T(8,128)(2,1)S(1)}, bf16[512,512]{1,0:T(8,128)(2,1)S(1)}, bf16[1024,512]{1,0:T(8,128)(2,1)S(1)}, bf16[512,128]{1,0:T(8,128)(2...) custom-call(s32[4]{0:T(128)S(1)} %pad_add_fusion.c, ...), custom_call_target="tpu_custom_call" | custom-call | flops 1000000 | bytes 1000 | tf_op jit(solution)/shard_map/pallas_call | solution.py:70
  38.7 2.3 %collective-permute-start.10 = (bf16[512,128]{1,0:T(8,128)(2,1)S(1)}, bf16[512,128]{1,0:T(8,128)(2,1)S(1)}, u32[]{:S(2)}, u32[]{:S(2)}) collective-permute-start(bf16[512,128]{1,0:T(8,128)(2,1)S(1)} %get-tuple-element.132), channel_id=1, source_target_pairs={{0,16},{8,24},{16,0},{24,8},{1,17},{9,25},{17,1},{25,9},{2,18},{10... | collective-permute-start | bytes 393224 | tf_op jit(solution)/shard_map/ppermute | solution.py:472
  42.4 2.3 %shard_map.98.g.refs_0_ = bf16[1024,512]{1,0:T(8,128)(2,1)S(1)} custom-call(s32[4]{0:T(128)S(1)} %pad_add_fusion.c, bf16[512,512]{1,0:T(8,128)(2,1)S(1)} %get-tuple-element.107.ko, bf16[512,512]{1,0:T(8,128)(2,1)S(1)} %get-tuple-element.117.ko.kp, bf16[512,512]{1,0:T(8,128)(2,1)S(1)} %get-tuple-element.108.vo, ...), custom_call_target="tpu_custom_call" | custom-call | flops 1000000 | bytes 1000 | tf_op jit(solution)/shard_map/pallas_call | solution.py:70
  44.7 2.9 %shard_map.99 = bf16[4,4,4,32,512]{4,3,2,1,0:T(8,128)(2,1)S(1)} custom-call(s32[4]{0:T(128)S(1)} %pad_add_fusion.c, bf16[4,4,128,1024]{3,2,1,0:T(8,128)(2,1)S(1)} %bitcast.68, bf16[1024,512]{1,0:T(8,128)(2,1)S(1)} %shard_map.98.g.refs_0_), custom_call_target="tpu_custom_call" | custom-call | flops 1000000 | bytes 1000 | tf_op jit(solution)/shard_map/pallas_call | solution.py:70
  48.1 2.6 %collective-permute-start.16 = (bf16[2,4,32,512]{3,2,1,0:T(8,128)(2,1)S(1)}, bf16[2,4,32,512]{3,2,1,0:T(8,128)(2,1)S(1)}, u32[]{:S(2)}, u32[]{:S(2)}) collective-permute-start(bf16[2,4,32,512]{3,2,1,0:T(8,128)(2,1)S(1)} %get-tuple-element.201), channel_id=1, source_target_pairs={{0,24},{8,0},{16,8},{24,16},{1,25},{9,1},{17,9},{25,17},{2,26},{10... | collective-permute-start | bytes 786440 | tf_op jit(solution)/shard_map/ppermute | solution.py:472
  50.7 2.3 %collective-permute-start.14 = (bf16[512,128]{1,0:T(8,128)(2,1)S(1)}, bf16[512,128]{1,0:T(8,128)(2,1)S(1)}, u32[]{:S(2)}, u32[]{:S(2)}) collective-permute-start(bf16[512,128]{1,0:T(8,128)(2,1)S(1)} %add_convert_fusion.6), channel_id=1, source_target_pairs={{0,64},{32,96},{64,0},{96,32},{1,65},{33,97},{65,1},{97,33},{2,66}... | collective-permute-start | bytes 393224 | tf_op jit(solution)/shard_map/ppermute | solution.py:472
  54.5 3.1 %shard_map.100 = (f32[1024,512]{1,0:T(8,128)S(1)}, f32[1024,512]{1,0:T(8,128)S(1)}) custom-call(s32[4]{0:T(128)S(1)} %pad_add_fusion.c, bf16[512,512]{1,0:T(8,128)(2,1)S(1)} %get-tuple-element.122.qo, bf16[512,512]{1,0:T(8,128)(2,1)S(1)} %get-tuple-element.123.qp, bf16[512,512]{1,0:T(8,128)(2,1)S(1)} %get-tuple-element.107.ko, ...), custom_call_target="tpu_custom_call" | custom-call | flops 1000000 | bytes 1000 | tf_op jit(solution)/shard_map/pallas_call | solution.py:70
  60.2 2.7 %collective-permute-start.21 = (bf16[4,4,32,512]{3,2,1,0:T(8,128)(2,1)S(1)}, bf16[4,4,32,512]{3,2,1,0:T(8,128)(2,1)S(1)}, u32[]{:S(2)}, u32[]{:S(2)}) collective-permute-start(bf16[4,4,32,512]{3,2,1,0:T(8,128)(2,1)S(1)} %pad_maximum_fusion.3), channel_id=1, source_target_pairs={{0,24},{8,0},{16,8},{24,16},{1,25},{9,1},{17,9},{25,17},{2,26},{10... | collective-permute-start | bytes 1572872 | tf_op jit(solution)/shard_map/ppermute | solution.py:472
  64.4 1.8 %shard_map.102 = (bf16[4,4,32,512]{3,2,1,0:T(8,128)(2,1)S(1)}, bf16[4,4,32,512]{3,2,1,0:T(8,128)(2,1)S(1)}) custom-call(s32[4]{0:T(128)S(1)} %pad_add_fusion.c, bf16[4,4,128,1024]{3,2,1,0:T(8,128)(2,1)S(1)} %bitcast.69, bf16[1024,512]{1,0:T(8,128)(2,1)S(1)} %get-tuple-element.173.refs_0_.refs_1_, bf16[1024,512]{1,0:T(8,128)(2,1)S(1)} %get-tuple-element.174.refs_1_.refs_2_.refs_3_), custom_call_target="tpu_custom_call" | custom-call | flops 1000000 | bytes 1000 | tf_op jit(solution)/shard_map/pallas_call | solution.py:70
  69.1 1.8 %shard_map.104 = (bf16[4,4,32,512]{3,2,1,0:T(8,128)(2,1)S(1)}, bf16[4,4,32,512]{3,2,1,0:T(8,128)(2,1)S(1)}) custom-call(s32[4]{0:T(128)S(1)} %pad_add_fusion.c, bf16[4,4,128,1024]{3,2,1,0:T(8,128)(2,1)S(1)} %bitcast.70, bf16[1024,512]{1,0:T(8,128)(2,1)S(1)} %get-tuple-element.173.refs_0_.refs_1_, bf16[1024,512]{1,0:T(8,128)(2,1)S(1)} %get-tuple-element.174.refs_1_.refs_2_.refs_3_), custom_call_target="tpu_custom_call" | custom-call | flops 1000000 | bytes 1000 | tf_op jit(solution)/shard_map/pallas_call | solution.py:70
  70.9 2.9 %shard_map.103 = (bf16[4,4,32,512]{3,2,1,0:T(8,128)(2,1)S(1)}, bf16[4,4,32,512]{3,2,1,0:T(8,128)(2,1)S(1)}, bf16[4,4,32,512]{3,2,1,0:T(8,128)(2,1)S(1)}, bf16[4,4,32,512]{3,2,1,0:T(8,128)(2,1)S(1)}) custom-call(s32[4]{0:T(128)S(1)} %pad_add_fusion.c, bf16[4,4,128,1024]{3,2,1,0:T(8,128)(2,1)S(1)} %bitcast.71, ...), custom_call_target="tpu_custom_call" | custom-call | flops 1000000 | bytes 1000 | tf_op jit(solution)/shard_map/pallas_call | solution.py:70
  73.7 4.6 %shard_map.105 = bf16[512,2048]{1,0:T(8,128)(2,1)S(1)} custom-call(s32[4]{0:T(128)S(1)} %pad_add_fusion.c, bf16[1024,512]{1,0:T(8,128)(2,1)S(1)} %shard_map.98.g.refs_0_, bf16[1024,512]{1,0:T(8,128)(2,1)S(1)} %get-tuple-element.173.refs_0_.refs_1_, bf16[1024,512]{1,0:T(8,128)(2,1)S(1)} %get-tuple-element.174.refs_1_.refs_2_.refs_3_, ...), custom_call_target="tpu_custom_call" | custom-call | flops 1000000 | bytes 1000 | tf_op jit(solution)/shard_map/pallas_call | solution.py:70
  78.6 3.2 %collective-permute-start.22 = (bf16[512,2048]{1,0:T(8,128)(2,1)S(1)}, bf16[512,2048]{1,0:T(8,128)(2,1)S(1)}, u32[]{:S(2)}, u32[]{:S(2)}) collective-permute-start(bf16[512,2048]{1,0:T(8,128)(2,1)S(1)} %shard_map.105), channel_id=1, source_target_pairs={{0,4},{4,0},{1,5},{5,1},{2,6},{6,2},{3,7},{7,3},{8,12},{12,8},{9,1... | collective-permute-start | bytes 6291464 | tf_op jit(solution)/shard_map/ppermute | solution.py:476
  82.0 2.4 %collective-permute-start.24 = (bf16[4,4,32,512]{3,2,1,0:T(8,128)(2,1)S(1)}, bf16[4,4,32,512]{3,2,1,0:T(8,128)(2,1)S(1)}, u32[]{:S(2)}, u32[]{:S(2)}) collective-permute-start(bf16[4,4,32,512]{3,2,1,0:T(8,128)(2,1)S(1)} %pad_maximum_fusion.5), channel_id=1, source_target_pairs={{0,24},{8,0},{16,8},{24,16},{1,25},{9,1},{17,9},{25,17},{2,26},{10... | collective-permute-start | bytes 1572872 | tf_op jit(solution)/shard_map/ppermute | solution.py:472
  89.6 5.4 %shard_map.106 = bf16[512,2048]{1,0:T(8,128)(2,1)} custom-call(s32[4]{0:T(128)S(1)} %pad_add_fusion.c, bf16[1024,512]{1,0:T(8,128)(2,1)S(1)} %shard_map.98.g.refs_0_, bf16[1024,512]{1,0:T(8,128)(2,1)S(1)} %get-tuple-element.173.refs_0_.refs_1_, bf16[1024,512]{1,0:T(8,128)(2,1)S(1)} %get-tuple-element.174.refs_1_.refs_2_.refs_3_, ...), custom_call_target="tpu_custom_call" | custom-call | flops 1000000 | bytes 1000 | tf_op jit(solution)/shard_map/pallas_call | solution.py:70
  95.8 6.0 %collective-permute-done.23 = bf16[4,4,32,512]{3,2,1,0:T(8,128)(2,1)S(1)} collective-permute-done((bf16[4,4,32,512]{3,2,1,0:T(8,128)(2,1)S(1)}, bf16[4,4,32,512]{3,2,1,0:T(8,128)(2,1)S(1)}, u32[]{:S(2)}, u32[]{:S(2)}) %collective-permute-start.23) | collective-permute-done | bytes 524320 | tf_op jit(solution)/shard_map/ppermute | solution.py:472
  102.5 1.6 %collective-permute-start.28 = (bf16[2,4,32,512]{3,2,1,0:T(8,128)(2,1)S(1)}, bf16[2,4,32,512]{3,2,1,0:T(8,128)(2,1)S(1)}, u32[]{:S(2)}, u32[]{:S(2)}) collective-permute-start(bf16[2,4,32,512]{3,2,1,0:T(8,128)(2,1)S(1)} %pad_maximum_fusion.8), channel_id=1, source_target_pairs={{0,96},{32,0},{64,32},{96,64},{1,97},{33,1},{65,33},{97,65},{2,98}... | collective-permute-start | bytes 786440 | tf_op jit(solution)/shard_map/ppermute | solution.py:472
  106.4 2.0 %collective-permute-done.31 = bf16[4,32,512]{2,1,0:T(8,128)(2,1)S(1)} collective-permute-done((bf16[4,32,512]{2,1,0:T(8,128)(2,1)S(1)}, bf16[4,32,512]{2,1,0:T(8,128)(2,1)S(1)}, u32[]{:S(2)}, u32[]{:S(2)}) %collective-permute-start.31) | collective-permute-done | bytes 131104 | tf_op jit(solution)/shard_map/ppermute | solution.py:472
  108.5 3.9 %collective-permute-done.29 = bf16[4,32,512]{2,1,0:T(8,128)(2,1)S(1)} collective-permute-done((bf16[4,32,512]{2,1,0:T(8,128)(2,1)S(1)}, bf16[4,32,512]{2,1,0:T(8,128)(2,1)S(1)}, u32[]{:S(2)}, u32[]{:S(2)}) %collective-permute-start.29) | collective-permute-done | bytes 131104 | tf_op jit(solution)/shard_map/ppermute | solution.py:472
  113.3 1.9 %collective-permute-done.32 = bf16[4,32,512]{2,1,0:T(8,128)(2,1)S(1)} collective-permute-done((bf16[4,32,512]{2,1,0:T(8,128)(2,1)S(1)}, bf16[4,32,512]{2,1,0:T(8,128)(2,1)S(1)}, u32[]{:S(2)}, u32[]{:S(2)}) %collective-permute-start.32) | collective-permute-done | bytes 131104 | tf_op jit(solution)/shard_map/ppermute | solution.py:472
  115.3 3.7 %collective-permute-start.33 = (bf16[32,1536]{1,0:T(8,128)(2,1)S(1)}, bf16[32,1536]{1,0:T(8,128)(2,1)S(1)}, u32[]{:S(2)}, u32[]{:S(2)}) collective-permute-start(bf16[32,1536]{1,0:T(8,128)(2,1)S(1)} %get-tuple-element.219), channel_id=1, source_target_pairs={{0,2},{1,3},{2,0},{3,1},{4,6},{5,7},{6,4},{7,5},{8,10},{9,11},{10,... | collective-permute-start | bytes 294920 | tf_op jit(solution)/shard_map/ppermute | solution.py:472
  121.0 1.8 %collective-permute-done.35 = bf16[32,1536]{1,0:T(8,128)(2,1)S(1)} collective-permute-done((bf16[32,1536]{1,0:T(8,128)(2,1)S(1)}, bf16[32,1536]{1,0:T(8,128)(2,1)S(1)}, u32[]{:S(2)}, u32[]{:S(2)}) %collective-permute-start.35) | collective-permute-done | bytes 98336 | tf_op jit(solution)/shard_map/ppermute | solution.py:472
  122.8 2.2 %collective-permute-done.34 = bf16[32,1536]{1,0:T(8,128)(2,1)S(1)} collective-permute-done((bf16[32,1536]{1,0:T(8,128)(2,1)S(1)}, bf16[32,1536]{1,0:T(8,128)(2,1)S(1)}, u32[]{:S(2)}, u32[]{:S(2)}) %collective-permute-start.34) | collective-permute-done | bytes 98336 | tf_op jit(solution)/shard_map/ppermute | solution.py:472
  125.1 3.6 %collective-permute-start.36 = (bf16[16,1536]{1,0:T(8,128)(2,1)S(1)}, bf16[16,1536]{1,0:T(8,128)(2,1)S(1)}, u32[]{:S(2)}, u32[]{:S(2)}) collective-permute-start(bf16[16,1536]{1,0:T(8,128)(2,1)S(1)} %slice_select_fusion), channel_id=1, source_target_pairs={{0,4},{4,0},{1,5},{5,1},{2,6},{6,2},{3,7},{7,3},{8,12},{12,8},{9,1... | collective-permute-start | bytes 147464 | tf_op jit(solution)/shard_map/ppermute | solution.py:476
  (97 shorter events, 32.4 us)
Async XLA Ops:
  0.6 7.2 %collective-permute-start = (bf16[512,2048]{1,0:T(8,128)(2,1)}, bf16[512,2048]{1,0:T(8,128)(2,1)S(1)}, u32[]{:S(2)}, u32[]{:S(2)}) collective-permute-start(bf16[512,2048]{1,0:T(8,128)(2,1)} %bitcast.72), channel_id=1, source_target_pairs={{0,4},{4,0},{1,5},{5,1},{2,6},{6,2},{3,7},{7,3},{8,12},{12,8},{9,1... | collective-permute-start | bytes 6291464 | tf_op jit(solution)/shard_map/ppermute | solution.py:476
  12.6 7.2 %collective-permute-start.3 = (bf16[512,128]{1,0:T(8,128)(2,1)S(1)}, bf16[512,128]{1,0:T(8,128)(2,1)S(1)}, u32[]{:S(2)}, u32[]{:S(2)}) collective-permute-start(bf16[512,128]{1,0:T(8,128)(2,1)S(1)} %get-tuple-element.105), channel_id=1, source_target_pairs={{0,16},{8,24},{16,0},{24,8},{1,17},{9,25},{17,1},{25,9},{2,18},{10... | collective-permute-start | bytes 393224 | tf_op jit(solution)/shard_map/ppermute | solution.py:472
  15.5 6.8 %collective-permute-start.2 = (bf16[512,128]{1,0:T(8,128)(2,1)S(1)}, bf16[512,128]{1,0:T(8,128)(2,1)S(1)}, u32[]{:S(2)}, u32[]{:S(2)}) collective-permute-start(bf16[512,128]{1,0:T(8,128)(2,1)S(1)} %get-tuple-element.105), channel_id=1, source_target_pairs={{0,24},{8,0},{16,8},{24,16},{1,25},{9,1},{17,9},{25,17},{2,26},{10... | collective-permute-start | bytes 393224 | tf_op jit(solution)/shard_map/ppermute | solution.py:472
  16.4 5.9 %collective-permute-start.1 = (bf16[512,128]{1,0:T(8,128)(2,1)S(1)}, bf16[512,128]{1,0:T(8,128)(2,1)S(1)}, u32[]{:S(2)}, u32[]{:S(2)}) collective-permute-start(bf16[512,128]{1,0:T(8,128)(2,1)S(1)} %get-tuple-element.105), channel_id=1, source_target_pairs={{0,8},{8,16},{16,24},{24,0},{1,9},{9,17},{17,25},{25,1},{2,10},{10... | collective-permute-start | bytes 393224 | tf_op jit(solution)/shard_map/ppermute | solution.py:472
  22.4 11.0 %collective-permute-start.7 = (bf16[512,512]{1,0:T(8,128)(2,1)S(1)}, bf16[512,512]{1,0:T(8,128)(2,1)S(1)}, u32[]{:S(2)}, u32[]{:S(2)}) collective-permute-start(bf16[512,512]{1,0:T(8,128)(2,1)S(1)} %get-tuple-element.116), channel_id=1, source_target_pairs={{0,4},{4,0},{1,5},{5,1},{2,6},{6,2},{3,7},{7,3},{8,12},{12,8},{9,1... | collective-permute-start | bytes 1572872 | tf_op jit(solution)/shard_map/ppermute | solution.py:476
  23.7 9.2 %collective-permute-start.6 = (bf16[512,128]{1,0:T(8,128)(2,1)S(1)}, bf16[512,128]{1,0:T(8,128)(2,1)S(1)}, u32[]{:S(2)}, u32[]{:S(2)}) collective-permute-start(bf16[512,128]{1,0:T(8,128)(2,1)S(1)} %add_convert_fusion.7), channel_id=1, source_target_pairs={{0,64},{32,96},{64,0},{96,32},{1,65},{33,97},{65,1},{97,33},{2,66}... | collective-permute-start | bytes 393224 | tf_op jit(solution)/shard_map/ppermute | solution.py:472
  26.6 6.8 %collective-permute-start.5 = (bf16[512,128]{1,0:T(8,128)(2,1)S(1)}, bf16[512,128]{1,0:T(8,128)(2,1)S(1)}, u32[]{:S(2)}, u32[]{:S(2)}) collective-permute-start(bf16[512,128]{1,0:T(8,128)(2,1)S(1)} %add_convert_fusion.7), channel_id=1, source_target_pairs={{0,96},{32,0},{64,32},{96,64},{1,97},{33,1},{65,33},{97,65},{2,98}... | collective-permute-start | bytes 393224 | tf_op jit(solution)/shard_map/ppermute | solution.py:472
  27.4 6.0 %collective-permute-start.4 = (bf16[512,128]{1,0:T(8,128)(2,1)S(1)}, bf16[512,128]{1,0:T(8,128)(2,1)S(1)}, u32[]{:S(2)}, u32[]{:S(2)}) collective-permute-start(bf16[512,128]{1,0:T(8,128)(2,1)S(1)} %add_convert_fusion.7), channel_id=1, source_target_pairs={{0,32},{32,64},{64,96},{96,0},{1,33},{33,65},{65,97},{97,1},{2,34}... | collective-permute-start | bytes 393224 | tf_op jit(solution)/shard_map/ppermute | solution.py:472
  37.5 10.4 %collective-permute-start.11 = (bf16[512,512]{1,0:T(8,128)(2,1)S(1)}, bf16[512,512]{1,0:T(8,128)(2,1)S(1)}, u32[]{:S(2)}, u32[]{:S(2)}) collective-permute-start(bf16[512,512]{1,0:T(8,128)(2,1)S(1)} %get-tuple-element.139), channel_id=1, source_target_pairs={{0,4},{4,0},{1,5},{5,1},{2,6},{6,2},{3,7},{7,3},{8,12},{12,8},{9,1... | collective-permute-start | bytes 1572872 | tf_op jit(solution)/shard_map/ppermute | solution.py:476
  38.7 8.9 %collective-permute-start.10 = (bf16[512,128]{1,0:T(8,128)(2,1)S(1)}, bf16[512,128]{1,0:T(8,128)(2,1)S(1)}, u32[]{:S(2)}, u32[]{:S(2)}) collective-permute-start(bf16[512,128]{1,0:T(8,128)(2,1)S(1)} %get-tuple-element.132), channel_id=1, source_target_pairs={{0,16},{8,24},{16,0},{24,8},{1,17},{9,25},{17,1},{25,9},{2,18},{10... | collective-permute-start | bytes 393224 | tf_op jit(solution)/shard_map/ppermute | solution.py:472
  40.9 6.7 %collective-permute-start.9 = (bf16[512,128]{1,0:T(8,128)(2,1)S(1)}, bf16[512,128]{1,0:T(8,128)(2,1)S(1)}, u32[]{:S(2)}, u32[]{:S(2)}) collective-permute-start(bf16[512,128]{1,0:T(8,128)(2,1)S(1)} %get-tuple-element.132), channel_id=1, source_target_pairs={{0,24},{8,0},{16,8},{24,16},{1,25},{9,1},{17,9},{25,17},{2,26},{10... | collective-permute-start | bytes 393224 | tf_op jit(solution)/shard_map/ppermute | solution.py:472
  41.9 6.0 %collective-permute-start.8 = (bf16[512,128]{1,0:T(8,128)(2,1)S(1)}, bf16[512,128]{1,0:T(8,128)(2,1)S(1)}, u32[]{:S(2)}, u32[]{:S(2)}) collective-permute-start(bf16[512,128]{1,0:T(8,128)(2,1)S(1)} %get-tuple-element.132), channel_id=1, source_target_pairs={{0,8},{8,16},{16,24},{24,0},{1,9},{9,17},{17,25},{25,1},{2,10},{10... | collective-permute-start | bytes 393224 | tf_op jit(solution)/shard_map/ppermute | solution.py:472
  48.1 11.7 %collective-permute-start.16 = (bf16[2,4,32,512]{3,2,1,0:T(8,128)(2,1)S(1)}, bf16[2,4,32,512]{3,2,1,0:T(8,128)(2,1)S(1)}, u32[]{:S(2)}, u32[]{:S(2)}) collective-permute-start(bf16[2,4,32,512]{3,2,1,0:T(8,128)(2,1)S(1)} %get-tuple-element.201), channel_id=1, source_target_pairs={{0,24},{8,0},{16,8},{24,16},{1,25},{9,1},{17,9},{25,17},{2,26},{10... | collective-permute-start | bytes 786440 | tf_op jit(solution)/shard_map/ppermute | solution.py:472
  50.7 9.1 %collective-permute-start.15 = (bf16[2,4,32,512]{3,2,1,0:T(8,128)(2,1)S(1)}, bf16[2,4,32,512]{3,2,1,0:T(8,128)(2,1)S(1)}, u32[]{:S(2)}, u32[]{:S(2)}) collective-permute-start(bf16[2,4,32,512]{3,2,1,0:T(8,128)(2,1)S(1)} %get-tuple-element.202), channel_id=1, source_target_pairs={{0,8},{8,16},{16,24},{24,0},{1,9},{9,17},{17,25},{25,1},{2,10},{10... | collective-permute-start | bytes 786440 | tf_op jit(solution)/shard_map/ppermute | solution.py:472
  50.7 6.9 %collective-permute-start.14 = (bf16[512,128]{1,0:T(8,128)(2,1)S(1)}, bf16[512,128]{1,0:T(8,128)(2,1)S(1)}, u32[]{:S(2)}, u32[]{:S(2)}) collective-permute-start(bf16[512,128]{1,0:T(8,128)(2,1)S(1)} %add_convert_fusion.6), channel_id=1, source_target_pairs={{0,64},{32,96},{64,0},{96,32},{1,65},{33,97},{65,1},{97,33},{2,66}... | collective-permute-start | bytes 393224 | tf_op jit(solution)/shard_map/ppermute | solution.py:472
  53.0 5.8 %collective-permute-start.13 = (bf16[512,128]{1,0:T(8,128)(2,1)S(1)}, bf16[512,128]{1,0:T(8,128)(2,1)S(1)}, u32[]{:S(2)}, u32[]{:S(2)}) collective-permute-start(bf16[512,128]{1,0:T(8,128)(2,1)S(1)} %add_convert_fusion.6), channel_id=1, source_target_pairs={{0,96},{32,0},{64,32},{96,64},{1,97},{33,1},{65,33},{97,65},{2,98}... | collective-permute-start | bytes 393224 | tf_op jit(solution)/shard_map/ppermute | solution.py:472
  53.9 5.9 %collective-permute-start.12 = (bf16[512,128]{1,0:T(8,128)(2,1)S(1)}, bf16[512,128]{1,0:T(8,128)(2,1)S(1)}, u32[]{:S(2)}, u32[]{:S(2)}) collective-permute-start(bf16[512,128]{1,0:T(8,128)(2,1)S(1)} %add_convert_fusion.6), channel_id=1, source_target_pairs={{0,32},{32,64},{64,96},{96,0},{1,33},{33,65},{65,97},{97,1},{2,34}... | collective-permute-start | bytes 393224 | tf_op jit(solution)/shard_map/ppermute | solution.py:472
  60.0 18.5 %collective-permute-start.20 = (bf16[4,4,32,512]{3,2,1,0:T(8,128)(2,1)S(1)}, bf16[4,4,32,512]{3,2,1,0:T(8,128)(2,1)S(1)}, u32[]{:S(2)}, u32[]{:S(2)}) collective-permute-start(bf16[4,4,32,512]{3,2,1,0:T(8,128)(2,1)S(1)} %pad_maximum_fusion.2), channel_id=1, source_target_pairs={{0,8},{8,16},{16,24},{24,0},{1,9},{9,17},{17,25},{25,1},{2,10},{10... | collective-permute-start | bytes 1572872 | tf_op jit(solution)/shard_map/ppermute | solution.py:472
  60.2 18.3 %collective-permute-start.21 = (bf16[4,4,32,512]{3,2,1,0:T(8,128)(2,1)S(1)}, bf16[4,4,32,512]{3,2,1,0:T(8,128)(2,1)S(1)}, u32[]{:S(2)}, u32[]{:S(2)}) collective-permute-start(bf16[4,4,32,512]{3,2,1,0:T(8,128)(2,1)S(1)} %pad_maximum_fusion.3), channel_id=1, source_target_pairs={{0,24},{8,0},{16,8},{24,16},{1,25},{9,1},{17,9},{25,17},{2,26},{10... | collective-permute-start | bytes 1572872 | tf_op jit(solution)/shard_map/ppermute | solution.py:472
  66.2 12.4 %collective-permute-start.19 = (bf16[4,4,32,512]{3,2,1,0:T(8,128)(2,1)S(1)}, bf16[4,4,32,512]{3,2,1,0:T(8,128)(2,1)S(1)}, u32[]{:S(2)}, u32[]{:S(2)}) collective-permute-start(bf16[4,4,32,512]{3,2,1,0:T(8,128)(2,1)S(1)} %get-tuple-element.168), channel_id=1, source_target_pairs={{0,32},{32,64},{64,96},{96,0},{1,33},{33,65},{65,97},{97,1},{2,34}... | collective-permute-start | bytes 1572872 | tf_op jit(solution)/shard_map/ppermute | solution.py:472
  67.5 10.8 %collective-permute-start.18 = (bf16[2,4,32,512]{3,2,1,0:T(8,128)(2,1)S(1)}, bf16[2,4,32,512]{3,2,1,0:T(8,128)(2,1)S(1)}, u32[]{:S(2)}, u32[]{:S(2)}) collective-permute-start(bf16[2,4,32,512]{3,2,1,0:T(8,128)(2,1)S(1)} %get-tuple-element.217), channel_id=1, source_target_pairs={{0,24},{8,0},{16,8},{24,16},{1,25},{9,1},{17,9},{25,17},{2,26},{10... | collective-permute-start | bytes 786440 | tf_op jit(solution)/shard_map/ppermute | solution.py:472
  68.8 9.7 %collective-permute-start.17 = (bf16[2,4,32,512]{3,2,1,0:T(8,128)(2,1)S(1)}, bf16[2,4,32,512]{3,2,1,0:T(8,128)(2,1)S(1)}, u32[]{:S(2)}, u32[]{:S(2)}) collective-permute-start(bf16[2,4,32,512]{3,2,1,0:T(8,128)(2,1)S(1)} %get-tuple-element.218), channel_id=1, source_target_pairs={{0,8},{8,16},{16,24},{24,0},{1,9},{9,17},{17,25},{25,1},{2,10},{10... | collective-permute-start | bytes 786440 | tf_op jit(solution)/shard_map/ppermute | solution.py:472
  78.6 11.0 %collective-permute-start.22 = (bf16[512,2048]{1,0:T(8,128)(2,1)S(1)}, bf16[512,2048]{1,0:T(8,128)(2,1)S(1)}, u32[]{:S(2)}, u32[]{:S(2)}) collective-permute-start(bf16[512,2048]{1,0:T(8,128)(2,1)S(1)} %shard_map.105), channel_id=1, source_target_pairs={{0,4},{4,0},{1,5},{5,1},{2,6},{6,2},{3,7},{7,3},{8,12},{12,8},{9,1... | collective-permute-start | bytes 6291464 | tf_op jit(solution)/shard_map/ppermute | solution.py:476
  82.0 13.8 %collective-permute-start.24 = (bf16[4,4,32,512]{3,2,1,0:T(8,128)(2,1)S(1)}, bf16[4,4,32,512]{3,2,1,0:T(8,128)(2,1)S(1)}, u32[]{:S(2)}, u32[]{:S(2)}) collective-permute-start(bf16[4,4,32,512]{3,2,1,0:T(8,128)(2,1)S(1)} %pad_maximum_fusion.5), channel_id=1, source_target_pairs={{0,24},{8,0},{16,8},{24,16},{1,25},{9,1},{17,9},{25,17},{2,26},{10... | collective-permute-start | bytes 1572872 | tf_op jit(solution)/shard_map/ppermute | solution.py:472
  85.0 16.9 %collective-permute-start.25 = (bf16[18,32,512]{2,1,0:T(8,128)(2,1)S(1)}, bf16[18,32,512]{2,1,0:T(8,128)(2,1)S(1)}, u32[]{:S(2)}, u32[]{:S(2)}) collective-permute-start(bf16[18,32,512]{2,1,0:T(8,128)(2,1)S(1)} %pad_maximum_fusion), channel_id=1, source_target_pairs={{0,32},{32,64},{64,96},{96,0},{1,33},{33,65},{65,97},{97,1},{2,34}... | collective-permute-start | bytes 1769480 | tf_op jit(solution)/shard_map/ppermute | solution.py:472
  86.3 15.5 %collective-permute-start.26 = (bf16[18,32,512]{2,1,0:T(8,128)(2,1)S(1)}, bf16[18,32,512]{2,1,0:T(8,128)(2,1)S(1)}, u32[]{:S(2)}, u32[]{:S(2)}) collective-permute-start(bf16[18,32,512]{2,1,0:T(8,128)(2,1)S(1)} %pad_maximum_fusion.1), channel_id=1, source_target_pairs={{0,96},{32,0},{64,32},{96,64},{1,97},{33,1},{65,33},{97,65},{2,98}... | collective-permute-start | bytes 1769480 | tf_op jit(solution)/shard_map/ppermute | solution.py:472
  88.0 13.9 %collective-permute-start.23 = (bf16[4,4,32,512]{3,2,1,0:T(8,128)(2,1)S(1)}, bf16[4,4,32,512]{3,2,1,0:T(8,128)(2,1)S(1)}, u32[]{:S(2)}, u32[]{:S(2)}) collective-permute-start(bf16[4,4,32,512]{3,2,1,0:T(8,128)(2,1)S(1)} %pad_maximum_fusion.4), channel_id=1, source_target_pairs={{0,8},{8,16},{16,24},{24,0},{1,9},{9,17},{17,25},{25,1},{2,10},{10... | collective-permute-start | bytes 1572872 | tf_op jit(solution)/shard_map/ppermute | solution.py:472
  102.5 9.8 %collective-permute-start.28 = (bf16[2,4,32,512]{3,2,1,0:T(8,128)(2,1)S(1)}, bf16[2,4,32,512]{3,2,1,0:T(8,128)(2,1)S(1)}, u32[]{:S(2)}, u32[]{:S(2)}) collective-permute-start(bf16[2,4,32,512]{3,2,1,0:T(8,128)(2,1)S(1)} %pad_maximum_fusion.8), channel_id=1, source_target_pairs={{0,96},{32,0},{64,32},{96,64},{1,97},{33,1},{65,33},{97,65},{2,98}... | collective-permute-start | bytes 786440 | tf_op jit(solution)/shard_map/ppermute | solution.py:472
  104.2 9.0 %collective-permute-start.27 = (bf16[2,4,32,512]{3,2,1,0:T(8,128)(2,1)S(1)}, bf16[2,4,32,512]{3,2,1,0:T(8,128)(2,1)S(1)}, u32[]{:S(2)}, u32[]{:S(2)}) collective-permute-start(bf16[2,4,32,512]{3,2,1,0:T(8,128)(2,1)S(1)} %pad_maximum_fusion.7), channel_id=1, source_target_pairs={{0,32},{32,64},{64,96},{96,0},{1,33},{33,65},{65,97},{97,1},{2,34}... | collective-permute-start | bytes 786440 | tf_op jit(solution)/shard_map/ppermute | solution.py:472
  104.4 7.9 %collective-permute-start.29 = (bf16[4,32,512]{2,1,0:T(8,128)(2,1)S(1)}, bf16[4,32,512]{2,1,0:T(8,128)(2,1)S(1)}, u32[]{:S(2)}, u32[]{:S(2)}) collective-permute-start(bf16[4,32,512]{2,1,0:T(8,128)(2,1)S(1)} %get-tuple-element.206), channel_id=1, source_target_pairs={{0,64},{32,96},{64,0},{96,32},{1,65},{33,97},{65,1},{97,33},{2,66}... | collective-permute-start | bytes 393224 | tf_op jit(solution)/shard_map/ppermute | solution.py:472
  105.6 7.7 %collective-permute-start.30 = (bf16[4,32,512]{2,1,0:T(8,128)(2,1)S(1)}, bf16[4,32,512]{2,1,0:T(8,128)(2,1)S(1)}, u32[]{:S(2)}, u32[]{:S(2)}) collective-permute-start(bf16[4,32,512]{2,1,0:T(8,128)(2,1)S(1)} %get-tuple-element.212), channel_id=1, source_target_pairs={{0,16},{8,24},{16,0},{24,8},{1,17},{9,25},{17,1},{25,9},{2,18},{10... | collective-permute-start | bytes 393224 | tf_op jit(solution)/shard_map/ppermute | solution.py:472
  108.5 6.7 %collective-permute-start.32 = (bf16[4,32,512]{2,1,0:T(8,128)(2,1)S(1)}, bf16[4,32,512]{2,1,0:T(8,128)(2,1)S(1)}, u32[]{:S(2)}, u32[]{:S(2)}) collective-permute-start(bf16[4,32,512]{2,1,0:T(8,128)(2,1)S(1)} %get-tuple-element.195), channel_id=1, source_target_pairs={{0,8},{8,16},{16,24},{24,0},{1,9},{9,17},{17,25},{25,1},{2,10},{10... | collective-permute-start | bytes 393224 | tf_op jit(solution)/shard_map/ppermute | solution.py:472
  (6 other events, 32.9 us)

commit v4 on v2

--- a/solution.py
+++ b/solution.py
@@ -160,18 +160,19 @@
 HIGH = slice(256, 512)
 
 
-def forward_pairs(q, k, v):
-    s00 = causal(dot(q[LOW], k[LOW], 1, 1))
-    s10 = dot(q[HIGH], k[LOW], 1, 1).astype(BF)
-    s11 = causal(dot(q[HIGH], k[HIGH], 1, 1))
-    return dot(s00, v[LOW]), dot(s10, v[LOW]) + dot(s11, v[HIGH])
-
-
-def backward_pairs(q, k, x):
-    s00 = causal(dot(k[LOW], q[LOW], 1, 1), True)
-    s01 = dot(k[LOW], q[HIGH], 1, 1).astype(BF)
-    s11 = causal(dot(k[HIGH], q[HIGH], 1, 1), True)
-    return dot(s00, x[LOW]) + dot(s01, x[HIGH]), dot(s11, x[HIGH])
+HALVES = (LOW, HIGH)
+
+
+def diagonal(q, k, x):
+    return [dot(causal(dot(q[r], k[r], 1, 1)), x[r]) for r in HALVES]
+
+
+def diagonal_turned(q, k, x):
+    return [dot(causal(dot(k[r], q[r], 1, 1), True), x[r]) for r in HALVES]
+
+
+def outer(a, b, r):
+    return dot(a[r], b[r], 0, 0)
 
 
 def masked_sum(refs, at, reverse):
@@ -189,22 +190,25 @@
     def kernel(c, t, a, ko, vo, *refs):
         copies = []
         if fetch:
-            ct, qo, out, mine_ct, other_ct, sems = refs
+            ct, qo, out, first, mine_ct, other_ct, sems = refs
             copies = [
                 pltpu.make_async_copy(ct.at[:, half_of(1 - c[0])], other_ct, sems.at[0]),
                 pltpu.make_async_copy(ct.at[:, half_of(c[0])], mine_ct, sems.at[1]),
             ]
         else:
-            qo, out = refs
+            qo, out, first = refs
         for copy in copies:
             copy.start()
         qo[...] = dot(t[...], a[...]).astype(BF)
 
-        @looped_head
+        @each_head
         def _(h):
-            low, high = forward_pairs(qo[:, head(h)], ko[:, head(h)], vo[:, head(h)])
+            qh, kh, vh = qo[:, head(h)], ko[:, head(h)], vo[:, head(h)]
+            low, high = diagonal(qh, kh, vh)
+            state = outer(kh, vh, LOW).astype(BF)
+            first[head(h), :] = state
             out[:256, head(h)] = low
-            out[256:, head(h)] = high
+            out[256:, head(h)] = high + dot(qh[HIGH], state)
 
         for copy in copies:
             copy.wait()
@@ -214,7 +218,7 @@
         kernel,
         core,
         [tok, wq, k, v] + (in_hbm(cot) if fetch else []),
-        [row, ((TOK, 512), F32)] + [row] * (2 if fetch else 0),
+        [row, ((TOK, 512), F32), ((512, DH), BF)] + [row] * (2 if fetch else 0),
         hbm_in=1 if fetch else 0,
         scratch=[pltpu.SemaphoreType.DMA((2,))] if fetch else [],
     )
@@ -271,21 +275,23 @@
     )
 
 
-def grad_q_of(core, k_o, k_p, v_o, v_p, g, p_o, p_p):
-    def kernel(c, ko, kp, vo, vp, gr, po, pp, dq):
+def grad_q_of(core, k_o, k_p, v_o, v_p, g, p_o, p_p, low_o, low_p):
+    def kernel(c, ko, kp, vo, vp, gr, po, pp, lo, lp, dq):
         @each_head
         def _(h):
-            for n, (k, v, p) in enumerate(((ko, vo, po), (kp, vp, pp))):
+            for n, (k, v, p, low) in enumerate(((ko, vo, po, lo), (kp, vp, pp, lp))):
                 gh = gr[n * TOK : n * TOK + TOK, head(h)]
-                past = dot(gh, p[head(h), :], 1, 1)
-                low, high = forward_pairs(gh, v[:, head(h)], k[:, head(h)])
-                dq[n * TOK : n * TOK + 256, head(h)] = (low + past[LOW]).astype(BF)
-                dq[n * TOK + 256 : n * TOK + 512, head(h)] = (high + past[HIGH]).astype(BF)
-
-    return local(
-        kernel,
-        core,
-        [k_o, k_p, v_o, v_p, g, p_o, p_p],
+                prefix = p[head(h), :]
+                later = (prefix.astype(F32) + low[head(h), :].astype(F32)).astype(BF)
+                parts = diagonal(gh, v[:, head(h)], k[:, head(h)])
+                for r, part, before in zip(HALVES, parts, (prefix, later)):
+                    past = dot(gh[r], before, 1, 1)
+                    dq[n * TOK + r.start : n * TOK + r.stop, head(h)] = (part + past).astype(BF)
+
+    return local(
+        kernel,
+        core,
+        [k_o, k_p, v_o, v_p, g, p_o, p_p, low_o, low_p],
         [((2 * TOK, 512), BF)],
     )[0]
 
@@ -297,10 +303,13 @@
             for n, (q, k, v) in enumerate(((qo, ko, vo), (qp, kp, vp))):
                 qh, kh, vh = q[:, head(h)], k[:, head(h)], v[:, head(h)]
                 gh = gr[n * TOK : n * TOK + TOK, head(h)]
-                for left, right, x, out in ((gh, vh, qh, dk), (qh, kh, gh, dv)):
-                    low, high = backward_pairs(left, right, x)
-                    out[n * TOK : n * TOK + 256, head(h)] = low
-                    out[n * TOK + 256 : n * TOK + 512, head(h)] = high
+                back = outer(qh, gh, HIGH).astype(BF)
+                low, high = diagonal_turned(gh, vh, qh)
+                dk[n * TOK : n * TOK + 256, head(h)] = low + dot(vh[LOW], back, 1, 1)
+                dk[n * TOK + 256 : n * TOK + 512, head(h)] = high
+                low, high = diagonal_turned(qh, kh, gh)
+                dv[n * TOK : n * TOK + 256, head(h)] = low + dot(kh[LOW], back)
+                dv[n * TOK + 256 : n * TOK + 512, head(h)] = high
 
     return local(
         kernel,
@@ -502,13 +511,13 @@
     k_p, v_p, state_p, total, w_q = project_partner(core, tok_p, w_k, w_v, state_o, w_query)
     weights = (w_q, w_k, w_v)
     along_x = pieces(total, "x")
-    q_o, i_o, cot, cot_s = within(core, tok_o, w_q, k_o, v_o, cotangent[0])
+    q_o, i_o, low_o, cot, cot_s = within(core, tok_o, w_q, k_o, v_o, cotangent[0])
     row, i_o, q_o, tok_t, cot_s, k_p = together(
         f32_sum(total, *along_x), i_o, q_o, tok_o, cot_s, k_p
     )
     along_y = pieces(row, "y")
     cot_p = swap(cot_s)
-    q_p, i_p = within(core, tok_p, w_q, k_p, v_p)
+    q_p, i_p, low_p = within(core, tok_p, w_q, k_p, v_p)
     tt = turned(core, tok_t, tok_p)
     *along_y, tt, cot_p, q_p, i_p = together(*along_y, tt, cot_p, q_p, i_p)
     a_o, a_p, g, p_o, p_p, back_o, back_p, total = normed(
@@ -516,7 +525,7 @@
     )
     along_x = pieces(total, "x")
     a_r = swap(a_p)
-    dq = grad_q_of(core, k_o, k_p, v_o, v_p, g, p_o, p_p)
+    dq = grad_q_of(core, k_o, k_p, v_o, v_p, g, p_o, p_p, low_o, low_p)
     part_q = weight_grad_all(core, tt, dq)
     row, part_q, g, a_r = together(f32_sum(total, *along_x), part_q, g, a_r)
     along_y = pieces(row, "y")

time: 129 us -> 129 us (level)
  transfers between devices with their start and end apart: 37 -> 37, of which waited for: 14 -> 12; matrix products, arithmetic and copies ran while one was open for 1% -> 1% of each run, Pallas kernels for 35% -> 35%
where the time goes in v4:
time: 129 us
  Pallas kernels  52.2 us (40%)
  starting transfers between devices  48.7 us (38%)
  waiting for transfers between devices  24.1 us (19%)
  other arithmetic  2.17 us (2%)
    pallas_call x16, Pallas kernels, local(): pl.pallas_call(kernel, out_shape=[jax.ShapeDtypeStruct(s, d) for s, d in...  49.9 us
    ppermute x32, starting transfers between devices, shift(): return lax.ppermute(v, axis, [(i, (i + d) % n) for i in range(n)])  38.3 us
    ppermute x32, waiting for transfers between devices, shift(): return lax.ppermute(v, axis, [(i, (i + d) % n) for i in range(n)])  23.2 us
    ppermute x5, starting transfers between devices, swap(): return lax.ppermute(v, 'c', [(0, 1), (1, 0)])  10.4 us
  transfers between devices with their start and end apart: 37, of which 12 were waited for; matrix products, arithmetic and copies ran while one was open for 1% of the time, Pallas kernels for 35%

profile of v4, /device:TPU:1, one launch (start us, length us, event | category | flops | bytes accessed | tf_op | source)
XLA Modules:
  0.0 128.5 jit_solution(3220937815232658262)
XLA Ops:
  2.2 5.6 %shard_map.92 = (bf16[512,512]{1,0:T(8,128)(2,1)S(1)}, bf16[512,512]{1,0:T(8,128)(2,1)S(1)}, bf16[512,128]{1,0:T(8,128)(2,1)S(1)}, bf16[2048,512]{1,0:T(8,128)(2,1)S(1)}, bf16[2048,512]{1,0:T(8,128)(2,1)S(1)}) custom-call(s32[4]{0:T(128)S(1)} %pad_add_fusion.c, bf16[512,2048]{1,0:T(8,128)(2,1)} %bitcast.73, bf16[2048,1024]{1,0:T(8,128)(2,1)} %b.1, ...), custom_call_target="tpu_custom_call" | custom-call | flops 1000000 | bytes 1000 | tf_op jit(solution)/shard_map/pallas_call | solution.py:68
  7.9 3.2 %shard_map.93 = (bf16[512,512]{1,0:T(8,128)(2,1)S(1)}, bf16[512,512]{1,0:T(8,128)(2,1)S(1)}, bf16[512,128]{1,0:T(8,128)(2,1)S(1)}, bf16[512,128]{1,0:T(8,128)(2,1)S(1)}, bf16[2048,512]{1,0:T(8,128)(2,1)S(1)}) custom-call(s32[4]{0:T(128)S(1)} %pad_add_fusion.c, bf16[512,2048]{1,0:T(8,128)(2,1)S(1)} %collective-permute-done.t.tp, ...), custom_call_target="tpu_custom_call" | custom-call | flops 1000000 | bytes 1000 | tf_op jit(solution)/shard_map/pallas_call | solution.py:68
  11.1 2.9 %collective-permute-start.3 = (bf16[512,128]{1,0:T(8,128)(2,1)S(1)}, bf16[512,128]{1,0:T(8,128)(2,1)S(1)}, u32[]{:S(2)}, u32[]{:S(2)}) collective-permute-start(bf16[512,128]{1,0:T(8,128)(2,1)S(1)} %get-tuple-element.101), channel_id=1, source_target_pairs={{0,16},{8,24},{16,0},{24,8},{1,17},{9,25},{17,1},{25,9},{2,18},{10... | collective-permute-start | bytes 393224 | tf_op jit(solution)/shard_map/ppermute | solution.py:466
  15.5 4.3 %shard_map.94 = (bf16[512,512]{1,0:T(8,128)(2,1)S(1)}, f32[512,512]{1,0:T(8,128)S(1)}, bf16[512,128]{1,0:T(8,128)(2,1)S(1)}, bf16[512,512]{1,0:T(8,128)(2,1)S(1)}, bf16[512,512]{1,0:T(8,128)(2,1)S(1)}) custom-call(s32[4]{0:T(128)S(1)} %pad_add_fusion.c, bf16[512,2048]{1,0:T(8,128)(2,1)S(1)} %bitcast.74, bf16[2048,512]{1,0:T(8,128)(2,1)S(1)} %get-tuple-element.102.a.refs_3_, ...), custom_call_target="tpu_custom_call" | custom-call | flops 1000000 | bytes 1000 | tf_op jit(solution)/shard_map/pallas_call | solution.py:68
  22.2 2.9 %collective-permute-start.6 = (bf16[512,128]{1,0:T(8,128)(2,1)S(1)}, bf16[512,128]{1,0:T(8,128)(2,1)S(1)}, u32[]{:S(2)}, u32[]{:S(2)}) collective-permute-start(bf16[512,128]{1,0:T(8,128)(2,1)S(1)} %add_convert_fusion.7), channel_id=1, source_target_pairs={{0,64},{32,96},{64,0},{96,32},{1,65},{33,97},{65,1},{97,33},{2,66}... | collective-permute-start | bytes 393224 | tf_op jit(solution)/shard_map/ppermute | solution.py:466
  26.5 2.3 %shard_map.95 = bf16[2048,1024]{1,0:T(8,128)(2,1)S(1)} custom-call(s32[4]{0:T(128)S(1)} %pad_add_fusion.c, bf16[512,2048]{1,0:T(8,128)(2,1)S(1)} %bitcast.75, bf16[512,2048]{1,0:T(8,128)(2,1)S(1)} %collective-permute-done.t.tp), custom_call_target="tpu_custom_call" | custom-call | flops 1000000 | bytes 8388608 | tf_op jit(solution)/shard_map/pallas_call | solution.py:50
  28.9 3.3 %shard_map.96 = (bf16[512,512]{1,0:T(8,128)(2,1)S(1)}, f32[512,512]{1,0:T(8,128)S(1)}, bf16[512,128]{1,0:T(8,128)(2,1)S(1)}) custom-call(s32[4]{0:T(128)S(1)} %pad_add_fusion.c, bf16[512,2048]{1,0:T(8,128)(2,1)S(1)} %collective-permute-done.t.tp, bf16[2048,512]{1,0:T(8,128)(2,1)S(1)} %get-tuple-element.102.a.refs_3_, ...), custom_call_target="tpu_custom_call" | custom-call | flops 1000000 | bytes 1000 | tf_op jit(solution)/shard_map/pallas_call | solution.py:68
  32.2 2.9 %shard_map.97 = (bf16[512,512]{1,0:T(8,128)(2,1)S(1)}, bf16[512,512]{1,0:T(8,128)(2,1)S(1)}, bf16[1024,512]{1,0:T(8,128)(2,1)S(1)}, bf16[512,128]{1,0:T(8,128)(2...) custom-call(s32[4]{0:T(128)S(1)} %pad_add_fusion.c, ...), custom_call_target="tpu_custom_call" | custom-call | flops 1000000 | bytes 1000 | tf_op jit(solution)/shard_map/pallas_call | solution.py:68
  36.1 2.3 %collective-permute-start.10 = (bf16[512,128]{1,0:T(8,128)(2,1)S(1)}, bf16[512,128]{1,0:T(8,128)(2,1)S(1)}, u32[]{:S(2)}, u32[]{:S(2)}) collective-permute-start(bf16[512,128]{1,0:T(8,128)(2,1)S(1)} %get-tuple-element.126), channel_id=1, source_target_pairs={{0,16},{8,24},{16,0},{24,8},{1,17},{9,25},{17,1},{25,9},{2,18},{10... | collective-permute-start | bytes 393224 | tf_op jit(solution)/shard_map/ppermute | solution.py:466
  39.8 2.3 %shard_map.98.g.refs_0_ = bf16[1024,512]{1,0:T(8,128)(2,1)S(1)} custom-call(s32[4]{0:T(128)S(1)} %pad_add_fusion.c, bf16[512,512]{1,0:T(8,128)(2,1)S(1)} %get-tuple-element.103.ko, bf16[512,512]{1,0:T(8,128)(2,1)S(1)} %get-tuple-element.113.ko.kp, bf16[512,512]{1,0:T(8,128)(2,1)S(1)} %get-tuple-element.104.vo, ...), custom_call_target="tpu_custom_call" | custom-call | flops 1000000 | bytes 1000 | tf_op jit(solution)/shard_map/pallas_call | solution.py:68
  42.1 3.4 %shard_map.99 = bf16[4,4,4,32,512]{4,3,2,1,0:T(8,128)(2,1)S(1)} custom-call(s32[4]{0:T(128)S(1)} %pad_add_fusion.c, bf16[4,4,128,1024]{3,2,1,0:T(8,128)(2,1)S(1)} %bitcast.68, bf16[1024,512]{1,0:T(8,128)(2,1)S(1)} %shard_map.98.g.refs_0_), custom_call_target="tpu_custom_call" | custom-call | flops 1000000 | bytes 1000 | tf_op jit(solution)/shard_map/pallas_call | solution.py:68
  45.7 2.4 %collective-permute-start.16 = (bf16[2,4,32,512]{3,2,1,0:T(8,128)(2,1)S(1)}, bf16[2,4,32,512]{3,2,1,0:T(8,128)(2,1)S(1)}, u32[]{:S(2)}, u32[]{:S(2)}) collective-permute-start(bf16[2,4,32,512]{3,2,1,0:T(8,128)(2,1)S(1)} %get-tuple-element.193), channel_id=1, source_target_pairs={{0,24},{8,0},{16,8},{24,16},{1,25},{9,1},{17,9},{25,17},{2,26},{10... | collective-permute-start | bytes 786440 | tf_op jit(solution)/shard_map/ppermute | solution.py:466
  48.1 2.2 %collective-permute-start.14 = (bf16[512,128]{1,0:T(8,128)(2,1)S(1)}, bf16[512,128]{1,0:T(8,128)(2,1)S(1)}, u32[]{:S(2)}, u32[]{:S(2)}) collective-permute-start(bf16[512,128]{1,0:T(8,128)(2,1)S(1)} %add_convert_fusion.6), channel_id=1, source_target_pairs={{0,64},{32,96},{64,0},{96,32},{1,65},{33,97},{65,1},{97,33},{2,66}... | collective-permute-start | bytes 393224 | tf_op jit(solution)/shard_map/ppermute | solution.py:466
  51.7 4.3 %shard_map.100 = (f32[1024,512]{1,0:T(8,128)S(1)}, f32[1024,512]{1,0:T(8,128)S(1)}) custom-call(s32[4]{0:T(128)S(1)} %pad_add_fusion.c, bf16[512,512]{1,0:T(8,128)(2,1)S(1)} %get-tuple-element.118.qo, bf16[512,512]{1,0:T(8,128)(2,1)S(1)} %get-tuple-element.119.qp, bf16[512,512]{1,0:T(8,128)(2,1)S(1)} %get-tuple-element.103.ko, ...), custom_call_target="tpu_custom_call" | custom-call | flops 1000000 | bytes 1000 | tf_op jit(solution)/shard_map/pallas_call | solution.py:68
  57.9 2.5 %collective-permute-start.21 = (bf16[4,4,32,512]{3,2,1,0:T(8,128)(2,1)S(1)}, bf16[4,4,32,512]{3,2,1,0:T(8,128)(2,1)S(1)}, u32[]{:S(2)}, u32[]{:S(2)}) collective-permute-start(bf16[4,4,32,512]{3,2,1,0:T(8,128)(2,1)S(1)} %pad_maximum_fusion.3), channel_id=1, source_target_pairs={{0,24},{8,0},{16,8},{24,16},{1,25},{9,1},{17,9},{25,17},{2,26},{10... | collective-permute-start | bytes 1572872 | tf_op jit(solution)/shard_map/ppermute | solution.py:466
  61.8 1.8 %shard_map.102 = (bf16[4,4,32,512]{3,2,1,0:T(8,128)(2,1)S(1)}, bf16[4,4,32,512]{3,2,1,0:T(8,128)(2,1)S(1)}) custom-call(s32[4]{0:T(128)S(1)} %pad_add_fusion.c, bf16[4,4,128,1024]{3,2,1,0:T(8,128)(2,1)S(1)} %bitcast.69, bf16[1024,512]{1,0:T(8,128)(2,1)S(1)} %get-tuple-element.165.refs_0_.refs_1_, bf16[1024,512]{1,0:T(8,128)(2,1)S(1)} %get-tuple-element.166.refs_1_.refs_2_.refs_3_), custom_call_target="tpu_custom_call" | custom-call | flops 1000000 | bytes 1000 | tf_op jit(solution)/shard_map/pallas_call | solution.py:68
  66.0 1.8 %shard_map.104 = (bf16[4,4,32,512]{3,2,1,0:T(8,128)(2,1)S(1)}, bf16[4,4,32,512]{3,2,1,0:T(8,128)(2,1)S(1)}) custom-call(s32[4]{0:T(128)S(1)} %pad_add_fusion.c, bf16[4,4,128,1024]{3,2,1,0:T(8,128)(2,1)S(1)} %bitcast.70, bf16[1024,512]{1,0:T(8,128)(2,1)S(1)} %get-tuple-element.165.refs_0_.refs_1_, bf16[1024,512]{1,0:T(8,128)(2,1)S(1)} %get-tuple-element.166.refs_1_.refs_2_.refs_3_), custom_call_target="tpu_custom_call" | custom-call | flops 1000000 | bytes 1000 | tf_op jit(solution)/shard_map/pallas_call | solution.py:68
  67.8 2.9 %shard_map.103 = (bf16[4,4,32,512]{3,2,1,0:T(8,128)(2,1)S(1)}, bf16[4,4,32,512]{3,2,1,0:T(8,128)(2,1)S(1)}, bf16[4,4,32,512]{3,2,1,0:T(8,128)(2,1)S(1)}, bf16[4,4,32,512]{3,2,1,0:T(8,128)(2,1)S(1)}) custom-call(s32[4]{0:T(128)S(1)} %pad_add_fusion.c, bf16[4,4,128,1024]{3,2,1,0:T(8,128)(2,1)S(1)} %bitcast.71, ...), custom_call_target="tpu_custom_call" | custom-call | flops 1000000 | bytes 1000 | tf_op jit(solution)/shard_map/pallas_call | solution.py:68
  70.7 4.6 %shard_map.105 = bf16[512,2048]{1,0:T(8,128)(2,1)S(1)} custom-call(s32[4]{0:T(128)S(1)} %pad_add_fusion.c, bf16[1024,512]{1,0:T(8,128)(2,1)S(1)} %shard_map.98.g.refs_0_, bf16[1024,512]{1,0:T(8,128)(2,1)S(1)} %get-tuple-element.165.refs_0_.refs_1_, bf16[1024,512]{1,0:T(8,128)(2,1)S(1)} %get-tuple-element.166.refs_1_.refs_2_.refs_3_, ...), custom_call_target="tpu_custom_call" | custom-call | flops 1000000 | bytes 1000 | tf_op jit(solution)/shard_map/pallas_call | solution.py:68
  76.1 3.1 %collective-permute-start.22 = (bf16[512,2048]{1,0:T(8,128)(2,1)S(1)}, bf16[512,2048]{1,0:T(8,128)(2,1)S(1)}, u32[]{:S(2)}, u32[]{:S(2)}) collective-permute-start(bf16[512,2048]{1,0:T(8,128)(2,1)S(1)} %shard_map.105), channel_id=1, source_target_pairs={{0,4},{4,0},{1,5},{5,1},{2,6},{6,2},{3,7},{7,3},{8,12},{12,8},{9,1... | collective-permute-start | bytes 6291464 | tf_op jit(solution)/shard_map/ppermute | solution.py:470
  79.4 2.5 %collective-permute-start.24 = (bf16[4,4,32,512]{3,2,1,0:T(8,128)(2,1)S(1)}, bf16[4,4,32,512]{3,2,1,0:T(8,128)(2,1)S(1)}, u32[]{:S(2)}, u32[]{:S(2)}) collective-permute-start(bf16[4,4,32,512]{3,2,1,0:T(8,128)(2,1)S(1)} %pad_maximum_fusion.5), channel_id=1, source_target_pairs={{0,24},{8,0},{16,8},{24,16},{1,25},{9,1},{17,9},{25,17},{2,26},{10... | collective-permute-start | bytes 1572872 | tf_op jit(solution)/shard_map/ppermute | solution.py:466
  83.3 2.2 %collective-permute-start.26 = (bf16[18,32,512]{2,1,0:T(8,128)(2,1)S(1)}, bf16[18,32,512]{2,1,0:T(8,128)(2,1)S(1)}, u32[]{:S(2)}, u32[]{:S(2)}) collective-permute-start(bf16[18,32,512]{2,1,0:T(8,128)(2,1)S(1)} %pad_maximum_fusion.1), channel_id=1, source_target_pairs={{0,96},{32,0},{64,32},{96,64},{1,97},{33,1},{65,33},{97,65},{2,98}... | collective-permute-start | bytes 1769480 | tf_op jit(solution)/shard_map/ppermute | solution.py:466
  87.3 5.4 %shard_map.106 = bf16[512,2048]{1,0:T(8,128)(2,1)} custom-call(s32[4]{0:T(128)S(1)} %pad_add_fusion.c, bf16[1024,512]{1,0:T(8,128)(2,1)S(1)} %shard_map.98.g.refs_0_, bf16[1024,512]{1,0:T(8,128)(2,1)S(1)} %get-tuple-element.165.refs_0_.refs_1_, bf16[1024,512]{1,0:T(8,128)(2,1)S(1)} %get-tuple-element.166.refs_1_.refs_2_.refs_3_, ...), custom_call_target="tpu_custom_call" | custom-call | flops 1000000 | bytes 1000 | tf_op jit(solution)/shard_map/pallas_call | solution.py:68
  93.3 6.3 %collective-permute-done.23 = bf16[4,4,32,512]{3,2,1,0:T(8,128)(2,1)S(1)} collective-permute-done((bf16[4,4,32,512]{3,2,1,0:T(8,128)(2,1)S(1)}, bf16[4,4,32,512]{3,2,1,0:T(8,128)(2,1)S(1)}, u32[]{:S(2)}, u32[]{:S(2)}) %collective-permute-start.23) | collective-permute-done | bytes 524320 | tf_op jit(solution)/shard_map/ppermute | solution.py:466
  100.3 1.6 %collective-permute-start.28 = (bf16[2,4,32,512]{3,2,1,0:T(8,128)(2,1)S(1)}, bf16[2,4,32,512]{3,2,1,0:T(8,128)(2,1)S(1)}, u32[]{:S(2)}, u32[]{:S(2)}) collective-permute-start(bf16[2,4,32,512]{3,2,1,0:T(8,128)(2,1)S(1)} %pad_maximum_fusion.8), channel_id=1, source_target_pairs={{0,96},{32,0},{64,32},{96,64},{1,97},{33,1},{65,33},{97,65},{2,98}... | collective-permute-start | bytes 786440 | tf_op jit(solution)/shard_map/ppermute | solution.py:466
  104.1 2.1 %collective-permute-done.31 = bf16[4,32,512]{2,1,0:T(8,128)(2,1)S(1)} collective-permute-done((bf16[4,32,512]{2,1,0:T(8,128)(2,1)S(1)}, bf16[4,32,512]{2,1,0:T(8,128)(2,1)S(1)}, u32[]{:S(2)}, u32[]{:S(2)}) %collective-permute-start.31) | collective-permute-done | bytes 131104 | tf_op jit(solution)/shard_map/ppermute | solution.py:466
  106.2 4.5 %collective-permute-done.29 = bf16[4,32,512]{2,1,0:T(8,128)(2,1)S(1)} collective-permute-done((bf16[4,32,512]{2,1,0:T(8,128)(2,1)S(1)}, bf16[4,32,512]{2,1,0:T(8,128)(2,1)S(1)}, u32[]{:S(2)}, u32[]{:S(2)}) %collective-permute-start.29) | collective-permute-done | bytes 131104 | tf_op jit(solution)/shard_map/ppermute | solution.py:466
  110.9 2.0 %collective-permute-done.32 = bf16[4,32,512]{2,1,0:T(8,128)(2,1)S(1)} collective-permute-done((bf16[4,32,512]{2,1,0:T(8,128)(2,1)S(1)}, bf16[4,32,512]{2,1,0:T(8,128)(2,1)S(1)}, u32[]{:S(2)}, u32[]{:S(2)}) %collective-permute-start.32) | collective-permute-done | bytes 131104 | tf_op jit(solution)/shard_map/ppermute | solution.py:466
  113.1 3.7 %collective-permute-start.33 = (bf16[32,1536]{1,0:T(8,128)(2,1)S(1)}, bf16[32,1536]{1,0:T(8,128)(2,1)S(1)}, u32[]{:S(2)}, u32[]{:S(2)}) collective-permute-start(bf16[32,1536]{1,0:T(8,128)(2,1)S(1)} %get-tuple-element.211), channel_id=1, source_target_pairs={{0,2},{1,3},{2,0},{3,1},{4,6},{5,7},{6,4},{7,5},{8,10},{9,11},{10,... | collective-permute-start | bytes 294920 | tf_op jit(solution)/shard_map/ppermute | solution.py:466
  118.8 2.1 %collective-permute-done.35 = bf16[32,1536]{1,0:T(8,128)(2,1)S(1)} collective-permute-done((bf16[32,1536]{1,0:T(8,128)(2,1)S(1)}, bf16[32,1536]{1,0:T(8,128)(2,1)S(1)}, u32[]{:S(2)}, u32[]{:S(2)}) %collective-permute-start.35) | collective-permute-done | bytes 98336 | tf_op jit(solution)/shard_map/ppermute | solution.py:466
  120.9 1.9 %collective-permute-done.34 = bf16[32,1536]{1,0:T(8,128)(2,1)S(1)} collective-permute-done((bf16[32,1536]{1,0:T(8,128)(2,1)S(1)}, bf16[32,1536]{1,0:T(8,128)(2,1)S(1)}, u32[]{:S(2)}, u32[]{:S(2)}) %collective-permute-start.34) | collective-permute-done | bytes 98336 | tf_op jit(solution)/shard_map/ppermute | solution.py:466
  122.9 3.5 %collective-permute-start.36 = (bf16[16,1536]{1,0:T(8,128)(2,1)S(1)}, bf16[16,1536]{1,0:T(8,128)(2,1)S(1)}, u32[]{:S(2)}, u32[]{:S(2)}) collective-permute-start(bf16[16,1536]{1,0:T(8,128)(2,1)S(1)} %slice_select_fusion), channel_id=1, source_target_pairs={{0,4},{4,0},{1,5},{5,1},{2,6},{6,2},{3,7},{7,3},{8,12},{12,8},{9,1... | collective-permute-start | bytes 147464 | tf_op jit(solution)/shard_map/ppermute | solution.py:470
  (97 shorter events, 28.5 us)
Async XLA Ops:
  0.6 7.2 %collective-permute-start = (bf16[512,2048]{1,0:T(8,128)(2,1)}, bf16[512,2048]{1,0:T(8,128)(2,1)S(1)}, u32[]{:S(2)}, u32[]{:S(2)}) collective-permute-start(bf16[512,2048]{1,0:T(8,128)(2,1)} %bitcast.72), channel_id=1, source_target_pairs={{0,4},{4,0},{1,5},{5,1},{2,6},{6,2},{3,7},{7,3},{8,12},{12,8},{9,1... | collective-permute-start | bytes 6291464 | tf_op jit(solution)/shard_map/ppermute | solution.py:470
  11.1 8.7 %collective-permute-start.3 = (bf16[512,128]{1,0:T(8,128)(2,1)S(1)}, bf16[512,128]{1,0:T(8,128)(2,1)S(1)}, u32[]{:S(2)}, u32[]{:S(2)}) collective-permute-start(bf16[512,128]{1,0:T(8,128)(2,1)S(1)} %get-tuple-element.101), channel_id=1, source_target_pairs={{0,16},{8,24},{16,0},{24,8},{1,17},{9,25},{17,1},{25,9},{2,18},{10... | collective-permute-start | bytes 393224 | tf_op jit(solution)/shard_map/ppermute | solution.py:466
  14.0 6.8 %collective-permute-start.2 = (bf16[512,128]{1,0:T(8,128)(2,1)S(1)}, bf16[512,128]{1,0:T(8,128)(2,1)S(1)}, u32[]{:S(2)}, u32[]{:S(2)}) collective-permute-start(bf16[512,128]{1,0:T(8,128)(2,1)S(1)} %get-tuple-element.101), channel_id=1, source_target_pairs={{0,24},{8,0},{16,8},{24,16},{1,25},{9,1},{17,9},{25,17},{2,26},{10... | collective-permute-start | bytes 393224 | tf_op jit(solution)/shard_map/ppermute | solution.py:466
  14.9 5.9 %collective-permute-start.1 = (bf16[512,128]{1,0:T(8,128)(2,1)S(1)}, bf16[512,128]{1,0:T(8,128)(2,1)S(1)}, u32[]{:S(2)}, u32[]{:S(2)}) collective-permute-start(bf16[512,128]{1,0:T(8,128)(2,1)S(1)} %get-tuple-element.101), channel_id=1, source_target_pairs={{0,8},{8,16},{16,24},{24,0},{1,9},{9,17},{17,25},{25,1},{2,10},{10... | collective-permute-start | bytes 393224 | tf_op jit(solution)/shard_map/ppermute | solution.py:466
  20.9 11.3 %collective-permute-start.7 = (bf16[512,512]{1,0:T(8,128)(2,1)S(1)}, bf16[512,512]{1,0:T(8,128)(2,1)S(1)}, u32[]{:S(2)}, u32[]{:S(2)}) collective-permute-start(bf16[512,512]{1,0:T(8,128)(2,1)S(1)} %get-tuple-element.112), channel_id=1, source_target_pairs={{0,4},{4,0},{1,5},{5,1},{2,6},{6,2},{3,7},{7,3},{8,12},{12,8},{9,1... | collective-permute-start | bytes 1572872 | tf_op jit(solution)/shard_map/ppermute | solution.py:470
  22.2 10.0 %collective-permute-start.6 = (bf16[512,128]{1,0:T(8,128)(2,1)S(1)}, bf16[512,128]{1,0:T(8,128)(2,1)S(1)}, u32[]{:S(2)}, u32[]{:S(2)}) collective-permute-start(bf16[512,128]{1,0:T(8,128)(2,1)S(1)} %add_convert_fusion.7), channel_id=1, source_target_pairs={{0,64},{32,96},{64,0},{96,32},{1,65},{33,97},{65,1},{97,33},{2,66}... | collective-permute-start | bytes 393224 | tf_op jit(solution)/shard_map/ppermute | solution.py:466
  25.1 7.1 %collective-permute-start.5 = (bf16[512,128]{1,0:T(8,128)(2,1)S(1)}, bf16[512,128]{1,0:T(8,128)(2,1)S(1)}, u32[]{:S(2)}, u32[]{:S(2)}) collective-permute-start(bf16[512,128]{1,0:T(8,128)(2,1)S(1)} %add_convert_fusion.7), channel_id=1, source_target_pairs={{0,96},{32,0},{64,32},{96,64},{1,97},{33,1},{65,33},{97,65},{2,98}... | collective-permute-start | bytes 393224 | tf_op jit(solution)/shard_map/ppermute | solution.py:466
  25.9 6.3 %collective-permute-start.4 = (bf16[512,128]{1,0:T(8,128)(2,1)S(1)}, bf16[512,128]{1,0:T(8,128)(2,1)S(1)}, u32[]{:S(2)}, u32[]{:S(2)}) collective-permute-start(bf16[512,128]{1,0:T(8,128)(2,1)S(1)} %add_convert_fusion.7), channel_id=1, source_target_pairs={{0,32},{32,64},{64,96},{96,0},{1,33},{33,65},{65,97},{97,1},{2,34}... | collective-permute-start | bytes 393224 | tf_op jit(solution)/shard_map/ppermute | solution.py:466
  35.1 10.5 %collective-permute-start.11 = (bf16[512,512]{1,0:T(8,128)(2,1)S(1)}, bf16[512,512]{1,0:T(8,128)(2,1)S(1)}, u32[]{:S(2)}, u32[]{:S(2)}) collective-permute-start(bf16[512,512]{1,0:T(8,128)(2,1)S(1)} %get-tuple-element.133), channel_id=1, source_target_pairs={{0,4},{4,0},{1,5},{5,1},{2,6},{6,2},{3,7},{7,3},{8,12},{12,8},{9,1... | collective-permute-start | bytes 1572872 | tf_op jit(solution)/shard_map/ppermute | solution.py:470
  36.1 9.4 %collective-permute-start.10 = (bf16[512,128]{1,0:T(8,128)(2,1)S(1)}, bf16[512,128]{1,0:T(8,128)(2,1)S(1)}, u32[]{:S(2)}, u32[]{:S(2)}) collective-permute-start(bf16[512,128]{1,0:T(8,128)(2,1)S(1)} %get-tuple-element.126), channel_id=1, source_target_pairs={{0,16},{8,24},{16,0},{24,8},{1,17},{9,25},{17,1},{25,9},{2,18},{10... | collective-permute-start | bytes 393224 | tf_op jit(solution)/shard_map/ppermute | solution.py:466
  38.3 7.2 %collective-permute-start.9 = (bf16[512,128]{1,0:T(8,128)(2,1)S(1)}, bf16[512,128]{1,0:T(8,128)(2,1)S(1)}, u32[]{:S(2)}, u32[]{:S(2)}) collective-permute-start(bf16[512,128]{1,0:T(8,128)(2,1)S(1)} %get-tuple-element.126), channel_id=1, source_target_pairs={{0,24},{8,0},{16,8},{24,16},{1,25},{9,1},{17,9},{25,17},{2,26},{10... | collective-permute-start | bytes 393224 | tf_op jit(solution)/shard_map/ppermute | solution.py:466
  39.3 6.3 %collective-permute-start.8 = (bf16[512,128]{1,0:T(8,128)(2,1)S(1)}, bf16[512,128]{1,0:T(8,128)(2,1)S(1)}, u32[]{:S(2)}, u32[]{:S(2)}) collective-permute-start(bf16[512,128]{1,0:T(8,128)(2,1)S(1)} %get-tuple-element.126), channel_id=1, source_target_pairs={{0,8},{8,16},{16,24},{24,0},{1,9},{9,17},{17,25},{25,1},{2,10},{10... | collective-permute-start | bytes 393224 | tf_op jit(solution)/shard_map/ppermute | solution.py:466
  45.7 11.6 %collective-permute-start.16 = (bf16[2,4,32,512]{3,2,1,0:T(8,128)(2,1)S(1)}, bf16[2,4,32,512]{3,2,1,0:T(8,128)(2,1)S(1)}, u32[]{:S(2)}, u32[]{:S(2)}) collective-permute-start(bf16[2,4,32,512]{3,2,1,0:T(8,128)(2,1)S(1)} %get-tuple-element.193), channel_id=1, source_target_pairs={{0,24},{8,0},{16,8},{24,16},{1,25},{9,1},{17,9},{25,17},{2,26},{10... | collective-permute-start | bytes 786440 | tf_op jit(solution)/shard_map/ppermute | solution.py:466
  48.1 9.2 %collective-permute-start.15 = (bf16[2,4,32,512]{3,2,1,0:T(8,128)(2,1)S(1)}, bf16[2,4,32,512]{3,2,1,0:T(8,128)(2,1)S(1)}, u32[]{:S(2)}, u32[]{:S(2)}) collective-permute-start(bf16[2,4,32,512]{3,2,1,0:T(8,128)(2,1)S(1)} %get-tuple-element.194), channel_id=1, source_target_pairs={{0,8},{8,16},{16,24},{24,0},{1,9},{9,17},{17,25},{25,1},{2,10},{10... | collective-permute-start | bytes 786440 | tf_op jit(solution)/shard_map/ppermute | solution.py:466
  48.1 7.9 %collective-permute-start.14 = (bf16[512,128]{1,0:T(8,128)(2,1)S(1)}, bf16[512,128]{1,0:T(8,128)(2,1)S(1)}, u32[]{:S(2)}, u32[]{:S(2)}) collective-permute-start(bf16[512,128]{1,0:T(8,128)(2,1)S(1)} %add_convert_fusion.6), channel_id=1, source_target_pairs={{0,64},{32,96},{64,0},{96,32},{1,65},{33,97},{65,1},{97,33},{2,66}... | collective-permute-start | bytes 393224 | tf_op jit(solution)/shard_map/ppermute | solution.py:466
  50.3 5.8 %collective-permute-start.13 = (bf16[512,128]{1,0:T(8,128)(2,1)S(1)}, bf16[512,128]{1,0:T(8,128)(2,1)S(1)}, u32[]{:S(2)}, u32[]{:S(2)}) collective-permute-start(bf16[512,128]{1,0:T(8,128)(2,1)S(1)} %add_convert_fusion.6), channel_id=1, source_target_pairs={{0,96},{32,0},{64,32},{96,64},{1,97},{33,1},{65,33},{97,65},{2,98}... | collective-permute-start | bytes 393224 | tf_op jit(solution)/shard_map/ppermute | solution.py:466
  51.2 6.1 %collective-permute-start.12 = (bf16[512,128]{1,0:T(8,128)(2,1)S(1)}, bf16[512,128]{1,0:T(8,128)(2,1)S(1)}, u32[]{:S(2)}, u32[]{:S(2)}) collective-permute-start(bf16[512,128]{1,0:T(8,128)(2,1)S(1)} %add_convert_fusion.6), channel_id=1, source_target_pairs={{0,32},{32,64},{64,96},{96,0},{1,33},{33,65},{65,97},{97,1},{2,34}... | collective-permute-start | bytes 393224 | tf_op jit(solution)/shard_map/ppermute | solution.py:466
  57.5 18.6 %collective-permute-start.20 = (bf16[4,4,32,512]{3,2,1,0:T(8,128)(2,1)S(1)}, bf16[4,4,32,512]{3,2,1,0:T(8,128)(2,1)S(1)}, u32[]{:S(2)}, u32[]{:S(2)}) collective-permute-start(bf16[4,4,32,512]{3,2,1,0:T(8,128)(2,1)S(1)} %pad_maximum_fusion.2), channel_id=1, source_target_pairs={{0,8},{8,16},{16,24},{24,0},{1,9},{9,17},{17,25},{25,1},{2,10},{10... | collective-permute-start | bytes 1572872 | tf_op jit(solution)/shard_map/ppermute | solution.py:466
  57.9 18.2 %collective-permute-start.21 = (bf16[4,4,32,512]{3,2,1,0:T(8,128)(2,1)S(1)}, bf16[4,4,32,512]{3,2,1,0:T(8,128)(2,1)S(1)}, u32[]{:S(2)}, u32[]{:S(2)}) collective-permute-start(bf16[4,4,32,512]{3,2,1,0:T(8,128)(2,1)S(1)} %pad_maximum_fusion.3), channel_id=1, source_target_pairs={{0,24},{8,0},{16,8},{24,16},{1,25},{9,1},{17,9},{25,17},{2,26},{10... | collective-permute-start | bytes 1572872 | tf_op jit(solution)/shard_map/ppermute | solution.py:466
  63.6 12.5 %collective-permute-start.19 = (bf16[4,4,32,512]{3,2,1,0:T(8,128)(2,1)S(1)}, bf16[4,4,32,512]{3,2,1,0:T(8,128)(2,1)S(1)}, u32[]{:S(2)}, u32[]{:S(2)}) collective-permute-start(bf16[4,4,32,512]{3,2,1,0:T(8,128)(2,1)S(1)} %get-tuple-element.160), channel_id=1, source_target_pairs={{0,32},{32,64},{64,96},{96,0},{1,33},{33,65},{65,97},{97,1},{2,34}... | collective-permute-start | bytes 1572872 | tf_op jit(solution)/shard_map/ppermute | solution.py:466
  64.5 10.8 %collective-permute-start.18 = (bf16[2,4,32,512]{3,2,1,0:T(8,128)(2,1)S(1)}, bf16[2,4,32,512]{3,2,1,0:T(8,128)(2,1)S(1)}, u32[]{:S(2)}, u32[]{:S(2)}) collective-permute-start(bf16[2,4,32,512]{3,2,1,0:T(8,128)(2,1)S(1)} %get-tuple-element.209), channel_id=1, source_target_pairs={{0,24},{8,0},{16,8},{24,16},{1,25},{9,1},{17,9},{25,17},{2,26},{10... | collective-permute-start | bytes 786440 | tf_op jit(solution)/shard_map/ppermute | solution.py:466
  65.7 10.4 %collective-permute-start.17 = (bf16[2,4,32,512]{3,2,1,0:T(8,128)(2,1)S(1)}, bf16[2,4,32,512]{3,2,1,0:T(8,128)(2,1)S(1)}, u32[]{:S(2)}, u32[]{:S(2)}) collective-permute-start(bf16[2,4,32,512]{3,2,1,0:T(8,128)(2,1)S(1)} %get-tuple-element.210), channel_id=1, source_target_pairs={{0,8},{8,16},{16,24},{24,0},{1,9},{9,17},{17,25},{25,1},{2,10},{10... | collective-permute-start | bytes 786440 | tf_op jit(solution)/shard_map/ppermute | solution.py:466
  76.1 11.2 %collective-permute-start.22 = (bf16[512,2048]{1,0:T(8,128)(2,1)S(1)}, bf16[512,2048]{1,0:T(8,128)(2,1)S(1)}, u32[]{:S(2)}, u32[]{:S(2)}) collective-permute-start(bf16[512,2048]{1,0:T(8,128)(2,1)S(1)} %shard_map.105), channel_id=1, source_target_pairs={{0,4},{4,0},{1,5},{5,1},{2,6},{6,2},{3,7},{7,3},{8,12},{12,8},{9,1... | collective-permute-start | bytes 6291464 | tf_op jit(solution)/shard_map/ppermute | solution.py:470
  79.4 13.9 %collective-permute-start.24 = (bf16[4,4,32,512]{3,2,1,0:T(8,128)(2,1)S(1)}, bf16[4,4,32,512]{3,2,1,0:T(8,128)(2,1)S(1)}, u32[]{:S(2)}, u32[]{:S(2)}) collective-permute-start(bf16[4,4,32,512]{3,2,1,0:T(8,128)(2,1)S(1)} %pad_maximum_fusion.5), channel_id=1, source_target_pairs={{0,24},{8,0},{16,8},{24,16},{1,25},{9,1},{17,9},{25,17},{2,26},{10... | collective-permute-start | bytes 1572872 | tf_op jit(solution)/shard_map/ppermute | solution.py:466
  82.4 17.1 %collective-permute-start.25 = (bf16[18,32,512]{2,1,0:T(8,128)(2,1)S(1)}, bf16[18,32,512]{2,1,0:T(8,128)(2,1)S(1)}, u32[]{:S(2)}, u32[]{:S(2)}) collective-permute-start(bf16[18,32,512]{2,1,0:T(8,128)(2,1)S(1)} %pad_maximum_fusion), channel_id=1, source_target_pairs={{0,32},{32,64},{64,96},{96,0},{1,33},{33,65},{65,97},{97,1},{2,34}... | collective-permute-start | bytes 1769480 | tf_op jit(solution)/shard_map/ppermute | solution.py:466
  83.3 16.2 %collective-permute-start.26 = (bf16[18,32,512]{2,1,0:T(8,128)(2,1)S(1)}, bf16[18,32,512]{2,1,0:T(8,128)(2,1)S(1)}, u32[]{:S(2)}, u32[]{:S(2)}) collective-permute-start(bf16[18,32,512]{2,1,0:T(8,128)(2,1)S(1)} %pad_maximum_fusion.1), channel_id=1, source_target_pairs={{0,96},{32,0},{64,32},{96,64},{1,97},{33,1},{65,33},{97,65},{2,98}... | collective-permute-start | bytes 1769480 | tf_op jit(solution)/shard_map/ppermute | solution.py:466
  85.7 13.9 %collective-permute-start.23 = (bf16[4,4,32,512]{3,2,1,0:T(8,128)(2,1)S(1)}, bf16[4,4,32,512]{3,2,1,0:T(8,128)(2,1)S(1)}, u32[]{:S(2)}, u32[]{:S(2)}) collective-permute-start(bf16[4,4,32,512]{3,2,1,0:T(8,128)(2,1)S(1)} %pad_maximum_fusion.4), channel_id=1, source_target_pairs={{0,8},{8,16},{16,24},{24,0},{1,9},{9,17},{17,25},{25,1},{2,10},{10... | collective-permute-start | bytes 1572872 | tf_op jit(solution)/shard_map/ppermute | solution.py:466
  100.3 10.5 %collective-permute-start.28 = (bf16[2,4,32,512]{3,2,1,0:T(8,128)(2,1)S(1)}, bf16[2,4,32,512]{3,2,1,0:T(8,128)(2,1)S(1)}, u32[]{:S(2)}, u32[]{:S(2)}) collective-permute-start(bf16[2,4,32,512]{3,2,1,0:T(8,128)(2,1)S(1)} %pad_maximum_fusion.8), channel_id=1, source_target_pairs={{0,96},{32,0},{64,32},{96,64},{1,97},{33,1},{65,33},{97,65},{2,98}... | collective-permute-start | bytes 786440 | tf_op jit(solution)/shard_map/ppermute | solution.py:466
  101.9 8.8 %collective-permute-start.27 = (bf16[2,4,32,512]{3,2,1,0:T(8,128)(2,1)S(1)}, bf16[2,4,32,512]{3,2,1,0:T(8,128)(2,1)S(1)}, u32[]{:S(2)}, u32[]{:S(2)}) collective-permute-start(bf16[2,4,32,512]{3,2,1,0:T(8,128)(2,1)S(1)} %pad_maximum_fusion.7), channel_id=1, source_target_pairs={{0,32},{32,64},{64,96},{96,0},{1,33},{33,65},{65,97},{97,1},{2,34}... | collective-permute-start | bytes 786440 | tf_op jit(solution)/shard_map/ppermute | solution.py:466
  102.2 8.6 %collective-permute-start.29 = (bf16[4,32,512]{2,1,0:T(8,128)(2,1)S(1)}, bf16[4,32,512]{2,1,0:T(8,128)(2,1)S(1)}, u32[]{:S(2)}, u32[]{:S(2)}) collective-permute-start(bf16[4,32,512]{2,1,0:T(8,128)(2,1)S(1)} %get-tuple-element.198), channel_id=1, source_target_pairs={{0,64},{32,96},{64,0},{96,32},{1,65},{33,97},{65,1},{97,33},{2,66}... | collective-permute-start | bytes 393224 | tf_op jit(solution)/shard_map/ppermute | solution.py:466
  103.4 7.5 %collective-permute-start.30 = (bf16[4,32,512]{2,1,0:T(8,128)(2,1)S(1)}, bf16[4,32,512]{2,1,0:T(8,128)(2,1)S(1)}, u32[]{:S(2)}, u32[]{:S(2)}) collective-permute-start(bf16[4,32,512]{2,1,0:T(8,128)(2,1)S(1)} %get-tuple-element.204), channel_id=1, source_target_pairs={{0,16},{8,24},{16,0},{24,8},{1,17},{9,25},{17,1},{25,9},{2,18},{10... | collective-permute-start | bytes 393224 | tf_op jit(solution)/shard_map/ppermute | solution.py:466
  106.2 6.7 %collective-permute-start.32 = (bf16[4,32,512]{2,1,0:T(8,128)(2,1)S(1)}, bf16[4,32,512]{2,1,0:T(8,128)(2,1)S(1)}, u32[]{:S(2)}, u32[]{:S(2)}) collective-permute-start(bf16[4,32,512]{2,1,0:T(8,128)(2,1)S(1)} %get-tuple-element.187), channel_id=1, source_target_pairs={{0,8},{8,16},{16,24},{24,0},{1,9},{9,17},{17,25},{25,1},{2,10},{10... | collective-permute-start | bytes 393224 | tf_op jit(solution)/shard_map/ppermute | solution.py:466
  (6 other events, 31.7 us)

commit v5 on v4

--- a/solution.py
+++ b/solution.py
@@ -540,10 +540,9 @@
     far_k, far_v, dk, dv = together(far_k, far_v, dk, dv)
     came_k, came_v = ring_out(far_k, "x"), shift(far_v, "y", 1)
     near = weight_grad(core, tt, [(dk, "x", 1), (dk, "x", 3), (dv, "y", 1), (dv, "y", 3)])
-    here_k, here_v = weight_grad(core, tt, [(dk, "x", 0), (dv, "y", 0)])
     ig_p = input_part(core, 1, (dq, dk, dv), weights)
-    *near, dk, dv, here_k, here_v, ig_p, a_o, k0, k1, came_v, q0, q1 = together(
-        *near, dk, dv, here_k, here_v, ig_p, a_o, *came_k, came_v, *last_q
+    *near, dk, dv, ig_p, a_o, k0, k1, came_v, q0, q1 = together(
+        *near, dk, dv, ig_p, a_o, *came_k, came_v, *last_q
     )
     last_k = ring_near(near[0], near[1], (k0, k1), "x")
     sum_q = f32_sum(part_q[0], q0, q1)
@@ -552,10 +551,11 @@
     down = jnp.concatenate([near[3].reshape(flat), sum_q[2, 2:]], axis=0)
     last_v = [shift(up, "y", 1), shift(down, "y", 3)]
     ig_r = swap(ig_p)
+    here_k, here_v = weight_grad(core, tt, [(dk, "x", 0), (dv, "y", 0)])
     attn_out = joined_heads(core, a_o, a_r)
     input_grad = input_part(core, 0, (dq, dk, dv), weights, ig_r)
-    sum_q, input_grad, attn_out, k0, k1, v0, v1 = together(
-        sum_q, input_grad, attn_out, *last_k, *last_v
+    sum_q, here_k, here_v, input_grad, attn_out, k0, k1, v0, v1 = together(
+        sum_q, here_k, here_v, input_grad, attn_out, *last_k, *last_v
     )
     sum_k = f32_sum(here_k, k0, k1)
     sum_v = f32_sum(here_v.reshape(flat), v0[:16], v1[:16]).reshape(4, 4, 32, 512)

time: 129 us -> 129 us (level)
  transfers between devices with their start and end apart: 37 -> 37, of which waited for: 12 -> 13; matrix products, arithmetic and copies ran while one was open for 1% -> 1% of each run, Pallas kernels for 35% -> 35%
where the time goes in v5:
time: 129 us; the launch traced here: 128 us
  Pallas kernels  52.2 us (40%)
  starting transfers between devices  48.4 us (38%)
  waiting for transfers between devices  24.2 us (19%)
  other arithmetic  2.19 us (2%)
    pallas_call x16, Pallas kernels, local(): pl.pallas_call(kernel, out_shape=[jax.ShapeDtypeStruct(s, d) for s, d in...  49.9 us
    ppermute x32, starting transfers between devices, shift(): return lax.ppermute(v, axis, [(i, (i + d) % n) for i in range(n)])  38 us
    ppermute x32, waiting for transfers between devices, shift(): return lax.ppermute(v, axis, [(i, (i + d) % n) for i in range(n)])  23.4 us
    ppermute x5, starting transfers between devices, swap(): return lax.ppermute(v, 'c', [(0, 1), (1, 0)])  10.4 us
  transfers between devices with their start and end apart: 37, of which 13 were waited for; matrix products, arithmetic and copies ran while one was open for 1% of the time, Pallas kernels for 35%

profile of v5, /device:TPU:1, one launch (start us, length us, event | category | flops | bytes accessed | tf_op | source)
XLA Modules:
  0.0 128.5 jit_solution(8292801081670226141)
XLA Ops:
  2.2 5.6 %shard_map.92 = (bf16[512,512]{1,0:T(8,128)(2,1)S(1)}, bf16[512,512]{1,0:T(8,128)(2,1)S(1)}, bf16[512,128]{1,0:T(8,128)(2,1)S(1)}, bf16[2048,512]{1,0:T(8,128)(2,1)S(1)}, bf16[2048,512]{1,0:T(8,128)(2,1)S(1)}) custom-call(s32[4]{0:T(128)S(1)} %pad_add_fusion.c, bf16[512,2048]{1,0:T(8,128)(2,1)} %bitcast.73, bf16[2048,1024]{1,0:T(8,128)(2,1)} %b.1, ...), custom_call_target="tpu_custom_call" | custom-call | flops 1000000 | bytes 1000 | tf_op jit(solution)/shard_map/pallas_call | solution.py:68
  7.9 3.2 %shard_map.93 = (bf16[512,512]{1,0:T(8,128)(2,1)S(1)}, bf16[512,512]{1,0:T(8,128)(2,1)S(1)}, bf16[512,128]{1,0:T(8,128)(2,1)S(1)}, bf16[512,128]{1,0:T(8,128)(2,1)S(1)}, bf16[2048,512]{1,0:T(8,128)(2,1)S(1)}) custom-call(s32[4]{0:T(128)S(1)} %pad_add_fusion.c, bf16[512,2048]{1,0:T(8,128)(2,1)S(1)} %collective-permute-done.t.tp, ...), custom_call_target="tpu_custom_call" | custom-call | flops 1000000 | bytes 1000 | tf_op jit(solution)/shard_map/pallas_call | solution.py:68
  11.1 2.9 %collective-permute-start.3 = (bf16[512,128]{1,0:T(8,128)(2,1)S(1)}, bf16[512,128]{1,0:T(8,128)(2,1)S(1)}, u32[]{:S(2)}, u32[]{:S(2)}) collective-permute-start(bf16[512,128]{1,0:T(8,128)(2,1)S(1)} %get-tuple-element.101), channel_id=1, source_target_pairs={{0,16},{8,24},{16,0},{24,8},{1,17},{9,25},{17,1},{25,9},{2,18},{10... | collective-permute-start | bytes 393224 | tf_op jit(solution)/shard_map/ppermute | solution.py:466
  15.5 4.3 %shard_map.94 = (bf16[512,512]{1,0:T(8,128)(2,1)S(1)}, f32[512,512]{1,0:T(8,128)S(1)}, bf16[512,128]{1,0:T(8,128)(2,1)S(1)}, bf16[512,512]{1,0:T(8,128)(2,1)S(1)}, bf16[512,512]{1,0:T(8,128)(2,1)S(1)}) custom-call(s32[4]{0:T(128)S(1)} %pad_add_fusion.c, bf16[512,2048]{1,0:T(8,128)(2,1)S(1)} %bitcast.74, bf16[2048,512]{1,0:T(8,128)(2,1)S(1)} %get-tuple-element.102.a.refs_3_, ...), custom_call_target="tpu_custom_call" | custom-call | flops 1000000 | bytes 1000 | tf_op jit(solution)/shard_map/pallas_call | solution.py:68
  22.2 2.9 %collective-permute-start.6 = (bf16[512,128]{1,0:T(8,128)(2,1)S(1)}, bf16[512,128]{1,0:T(8,128)(2,1)S(1)}, u32[]{:S(2)}, u32[]{:S(2)}) collective-permute-start(bf16[512,128]{1,0:T(8,128)(2,1)S(1)} %add_convert_fusion.7), channel_id=1, source_target_pairs={{0,64},{32,96},{64,0},{96,32},{1,65},{33,97},{65,1},{97,33},{2,66}... | collective-permute-start | bytes 393224 | tf_op jit(solution)/shard_map/ppermute | solution.py:466
  26.5 2.3 %shard_map.95 = bf16[2048,1024]{1,0:T(8,128)(2,1)S(1)} custom-call(s32[4]{0:T(128)S(1)} %pad_add_fusion.c, bf16[512,2048]{1,0:T(8,128)(2,1)S(1)} %bitcast.75, bf16[512,2048]{1,0:T(8,128)(2,1)S(1)} %collective-permute-done.t.tp), custom_call_target="tpu_custom_call" | custom-call | flops 1000000 | bytes 8388608 | tf_op jit(solution)/shard_map/pallas_call | solution.py:50
  28.9 3.3 %shard_map.96 = (bf16[512,512]{1,0:T(8,128)(2,1)S(1)}, f32[512,512]{1,0:T(8,128)S(1)}, bf16[512,128]{1,0:T(8,128)(2,1)S(1)}) custom-call(s32[4]{0:T(128)S(1)} %pad_add_fusion.c, bf16[512,2048]{1,0:T(8,128)(2,1)S(1)} %collective-permute-done.t.tp, bf16[2048,512]{1,0:T(8,128)(2,1)S(1)} %get-tuple-element.102.a.refs_3_, ...), custom_call_target="tpu_custom_call" | custom-call | flops 1000000 | bytes 1000 | tf_op jit(solution)/shard_map/pallas_call | solution.py:68
  32.2 2.9 %shard_map.97 = (bf16[512,512]{1,0:T(8,128)(2,1)S(1)}, bf16[512,512]{1,0:T(8,128)(2,1)S(1)}, bf16[1024,512]{1,0:T(8,128)(2,1)S(1)}, bf16[512,128]{1,0:T(8,128)(2...) custom-call(s32[4]{0:T(128)S(1)} %pad_add_fusion.c, ...), custom_call_target="tpu_custom_call" | custom-call | flops 1000000 | bytes 1000 | tf_op jit(solution)/shard_map/pallas_call | solution.py:68
  36.1 2.3 %collective-permute-start.10 = (bf16[512,128]{1,0:T(8,128)(2,1)S(1)}, bf16[512,128]{1,0:T(8,128)(2,1)S(1)}, u32[]{:S(2)}, u32[]{:S(2)}) collective-permute-start(bf16[512,128]{1,0:T(8,128)(2,1)S(1)} %get-tuple-element.126), channel_id=1, source_target_pairs={{0,16},{8,24},{16,0},{24,8},{1,17},{9,25},{17,1},{25,9},{2,18},{10... | collective-permute-start | bytes 393224 | tf_op jit(solution)/shard_map/ppermute | solution.py:466
  39.8 2.3 %shard_map.98.g.refs_0_ = bf16[1024,512]{1,0:T(8,128)(2,1)S(1)} custom-call(s32[4]{0:T(128)S(1)} %pad_add_fusion.c, bf16[512,512]{1,0:T(8,128)(2,1)S(1)} %get-tuple-element.103.ko, bf16[512,512]{1,0:T(8,128)(2,1)S(1)} %get-tuple-element.113.ko.kp, bf16[512,512]{1,0:T(8,128)(2,1)S(1)} %get-tuple-element.104.vo, ...), custom_call_target="tpu_custom_call" | custom-call | flops 1000000 | bytes 1000 | tf_op jit(solution)/shard_map/pallas_call | solution.py:68
  42.1 3.4 %shard_map.99 = bf16[4,4,4,32,512]{4,3,2,1,0:T(8,128)(2,1)S(1)} custom-call(s32[4]{0:T(128)S(1)} %pad_add_fusion.c, bf16[4,4,128,1024]{3,2,1,0:T(8,128)(2,1)S(1)} %bitcast.68, bf16[1024,512]{1,0:T(8,128)(2,1)S(1)} %shard_map.98.g.refs_0_), custom_call_target="tpu_custom_call" | custom-call | flops 1000000 | bytes 1000 | tf_op jit(solution)/shard_map/pallas_call | solution.py:68
  45.7 2.4 %collective-permute-start.16 = (bf16[2,4,32,512]{3,2,1,0:T(8,128)(2,1)S(1)}, bf16[2,4,32,512]{3,2,1,0:T(8,128)(2,1)S(1)}, u32[]{:S(2)}, u32[]{:S(2)}) collective-permute-start(bf16[2,4,32,512]{3,2,1,0:T(8,128)(2,1)S(1)} %get-tuple-element.193), channel_id=1, source_target_pairs={{0,24},{8,0},{16,8},{24,16},{1,25},{9,1},{17,9},{25,17},{2,26},{10... | collective-permute-start | bytes 786440 | tf_op jit(solution)/shard_map/ppermute | solution.py:466
  48.1 2.2 %collective-permute-start.14 = (bf16[512,128]{1,0:T(8,128)(2,1)S(1)}, bf16[512,128]{1,0:T(8,128)(2,1)S(1)}, u32[]{:S(2)}, u32[]{:S(2)}) collective-permute-start(bf16[512,128]{1,0:T(8,128)(2,1)S(1)} %add_convert_fusion.6), channel_id=1, source_target_pairs={{0,64},{32,96},{64,0},{96,32},{1,65},{33,97},{65,1},{97,33},{2,66}... | collective-permute-start | bytes 393224 | tf_op jit(solution)/shard_map/ppermute | solution.py:466
  51.7 4.3 %shard_map.100 = (f32[1024,512]{1,0:T(8,128)S(1)}, f32[1024,512]{1,0:T(8,128)S(1)}) custom-call(s32[4]{0:T(128)S(1)} %pad_add_fusion.c, bf16[512,512]{1,0:T(8,128)(2,1)S(1)} %get-tuple-element.118.qo, bf16[512,512]{1,0:T(8,128)(2,1)S(1)} %get-tuple-element.119.qp, bf16[512,512]{1,0:T(8,128)(2,1)S(1)} %get-tuple-element.103.ko, ...), custom_call_target="tpu_custom_call" | custom-call | flops 1000000 | bytes 1000 | tf_op jit(solution)/shard_map/pallas_call | solution.py:68
  57.9 2.5 %collective-permute-start.21 = (bf16[4,4,32,512]{3,2,1,0:T(8,128)(2,1)S(1)}, bf16[4,4,32,512]{3,2,1,0:T(8,128)(2,1)S(1)}, u32[]{:S(2)}, u32[]{:S(2)}) collective-permute-start(bf16[4,4,32,512]{3,2,1,0:T(8,128)(2,1)S(1)} %pad_maximum_fusion.3), channel_id=1, source_target_pairs={{0,24},{8,0},{16,8},{24,16},{1,25},{9,1},{17,9},{25,17},{2,26},{10... | collective-permute-start | bytes 1572872 | tf_op jit(solution)/shard_map/ppermute | solution.py:466
  61.8 1.8 %shard_map.102 = (bf16[4,4,32,512]{3,2,1,0:T(8,128)(2,1)S(1)}, bf16[4,4,32,512]{3,2,1,0:T(8,128)(2,1)S(1)}) custom-call(s32[4]{0:T(128)S(1)} %pad_add_fusion.c, bf16[4,4,128,1024]{3,2,1,0:T(8,128)(2,1)S(1)} %bitcast.69, bf16[1024,512]{1,0:T(8,128)(2,1)S(1)} %get-tuple-element.163.refs_0_.refs_1_, bf16[1024,512]{1,0:T(8,128)(2,1)S(1)} %get-tuple-element.164.refs_1_.refs_2_.refs_3_), custom_call_target="tpu_custom_call" | custom-call | flops 1000000 | bytes 1000 | tf_op jit(solution)/shard_map/pallas_call | solution.py:68
  66.0 4.6 %shard_map.104 = bf16[512,2048]{1,0:T(8,128)(2,1)S(1)} custom-call(s32[4]{0:T(128)S(1)} %pad_add_fusion.c, bf16[1024,512]{1,0:T(8,128)(2,1)S(1)} %shard_map.98.g.refs_0_, bf16[1024,512]{1,0:T(8,128)(2,1)S(1)} %get-tuple-element.163.refs_0_.refs_1_, bf16[1024,512]{1,0:T(8,128)(2,1)S(1)} %get-tuple-element.164.refs_1_.refs_2_.refs_3_, ...), custom_call_target="tpu_custom_call" | custom-call | flops 1000000 | bytes 1000 | tf_op jit(solution)/shard_map/pallas_call | solution.py:68
  70.6 2.9 %shard_map.103 = (bf16[4,4,32,512]{3,2,1,0:T(8,128)(2,1)S(1)}, bf16[4,4,32,512]{3,2,1,0:T(8,128)(2,1)S(1)}, bf16[4,4,32,512]{3,2,1,0:T(8,128)(2,1)S(1)}, bf16[4,4,32,512]{3,2,1,0:T(8,128)(2,1)S(1)}) custom-call(s32[4]{0:T(128)S(1)} %pad_add_fusion.c, bf16[4,4,128,1024]{3,2,1,0:T(8,128)(2,1)S(1)} %bitcast.70, ...), custom_call_target="tpu_custom_call" | custom-call | flops 1000000 | bytes 1000 | tf_op jit(solution)/shard_map/pallas_call | solution.py:68
  73.5 1.7 %collective-permute-done.18 = bf16[2,4,32,512]{3,2,1,0:T(8,128)(2,1)S(1)} collective-permute-done((bf16[2,4,32,512]{3,2,1,0:T(8,128)(2,1)S(1)}, bf16[2,4,32,512]{3,2,1,0:T(8,128)(2,1)S(1)}, u32[]{:S(2)}, u32[]{:S(2)}) %collective-permute-start.18) | collective-permute-done | bytes 262176 | tf_op jit(solution)/shard_map/ppermute | solution.py:466
  76.1 3.1 %collective-permute-start.22 = (bf16[512,2048]{1,0:T(8,128)(2,1)S(1)}, bf16[512,2048]{1,0:T(8,128)(2,1)S(1)}, u32[]{:S(2)}, u32[]{:S(2)}) collective-permute-start(bf16[512,2048]{1,0:T(8,128)(2,1)S(1)} %shard_map.104), channel_id=1, source_target_pairs={{0,4},{4,0},{1,5},{5,1},{2,6},{6,2},{3,7},{7,3},{8,12},{12,8},{9,1... | collective-permute-start | bytes 6291464 | tf_op jit(solution)/shard_map/ppermute | solution.py:470
  79.4 2.5 %collective-permute-start.24 = (bf16[4,4,32,512]{3,2,1,0:T(8,128)(2,1)S(1)}, bf16[4,4,32,512]{3,2,1,0:T(8,128)(2,1)S(1)}, u32[]{:S(2)}, u32[]{:S(2)}) collective-permute-start(bf16[4,4,32,512]{3,2,1,0:T(8,128)(2,1)S(1)} %pad_maximum_fusion.5), channel_id=1, source_target_pairs={{0,24},{8,0},{16,8},{24,16},{1,25},{9,1},{17,9},{25,17},{2,26},{10... | collective-permute-start | bytes 1572872 | tf_op jit(solution)/shard_map/ppermute | solution.py:466
  83.3 2.0 %collective-permute-start.26 = (bf16[18,32,512]{2,1,0:T(8,128)(2,1)S(1)}, bf16[18,32,512]{2,1,0:T(8,128)(2,1)S(1)}, u32[]{:S(2)}, u32[]{:S(2)}) collective-permute-start(bf16[18,32,512]{2,1,0:T(8,128)(2,1)S(1)} %pad_maximum_fusion.1), channel_id=1, source_target_pairs={{0,96},{32,0},{64,32},{96,64},{1,97},{33,1},{65,33},{97,65},{2,98}... | collective-permute-start | bytes 1769480 | tf_op jit(solution)/shard_map/ppermute | solution.py:466
  85.8 1.8 %shard_map.105 = (bf16[4,4,32,512]{3,2,1,0:T(8,128)(2,1)S(1)}, bf16[4,4,32,512]{3,2,1,0:T(8,128)(2,1)S(1)}) custom-call(s32[4]{0:T(128)S(1)} %pad_add_fusion.c, bf16[4,4,128,1024]{3,2,1,0:T(8,128)(2,1)S(1)} %bitcast.71, bf16[1024,512]{1,0:T(8,128)(2,1)S(1)} %get-tuple-element.163.refs_0_.refs_1_, bf16[1024,512]{1,0:T(8,128)(2,1)S(1)} %get-tuple-element.164.refs_1_.refs_2_.refs_3_), custom_call_target="tpu_custom_call" | custom-call | flops 1000000 | bytes 1000 | tf_op jit(solution)/shard_map/pallas_call | solution.py:68
  89.1 5.4 %shard_map.106 = bf16[512,2048]{1,0:T(8,128)(2,1)} custom-call(s32[4]{0:T(128)S(1)} %pad_add_fusion.c, bf16[1024,512]{1,0:T(8,128)(2,1)S(1)} %shard_map.98.g.refs_0_, bf16[1024,512]{1,0:T(8,128)(2,1)S(1)} %get-tuple-element.163.refs_0_.refs_1_, bf16[1024,512]{1,0:T(8,128)(2,1)S(1)} %get-tuple-element.164.refs_1_.refs_2_.refs_3_, ...), custom_call_target="tpu_custom_call" | custom-call | flops 1000000 | bytes 1000 | tf_op jit(solution)/shard_map/pallas_call | solution.py:68
  94.5 5.0 %collective-permute-done.23 = bf16[4,4,32,512]{3,2,1,0:T(8,128)(2,1)S(1)} collective-permute-done((bf16[4,4,32,512]{3,2,1,0:T(8,128)(2,1)S(1)}, bf16[4,4,32,512]{3,2,1,0:T(8,128)(2,1)S(1)}, u32[]{:S(2)}, u32[]{:S(2)}) %collective-permute-start.23) | collective-permute-done | bytes 524320 | tf_op jit(solution)/shard_map/ppermute | solution.py:466
  103.8 2.3 %collective-permute-done.31 = bf16[4,32,512]{2,1,0:T(8,128)(2,1)S(1)} collective-permute-done((bf16[4,32,512]{2,1,0:T(8,128)(2,1)S(1)}, bf16[4,32,512]{2,1,0:T(8,128)(2,1)S(1)}, u32[]{:S(2)}, u32[]{:S(2)}) %collective-permute-start.31) | collective-permute-done | bytes 131104 | tf_op jit(solution)/shard_map/ppermute | solution.py:466
  106.1 4.1 %collective-permute-done.29 = bf16[4,32,512]{2,1,0:T(8,128)(2,1)S(1)} collective-permute-done((bf16[4,32,512]{2,1,0:T(8,128)(2,1)S(1)}, bf16[4,32,512]{2,1,0:T(8,128)(2,1)S(1)}, u32[]{:S(2)}, u32[]{:S(2)}) %collective-permute-start.29) | collective-permute-done | bytes 131104 | tf_op jit(solution)/shard_map/ppermute | solution.py:466
  110.8 2.1 %collective-permute-done.32 = bf16[4,32,512]{2,1,0:T(8,128)(2,1)S(1)} collective-permute-done((bf16[4,32,512]{2,1,0:T(8,128)(2,1)S(1)}, bf16[4,32,512]{2,1,0:T(8,128)(2,1)S(1)}, u32[]{:S(2)}, u32[]{:S(2)}) %collective-permute-start.32) | collective-permute-done | bytes 131104 | tf_op jit(solution)/shard_map/ppermute | solution.py:466
  113.0 3.7 %collective-permute-start.33 = (bf16[32,1536]{1,0:T(8,128)(2,1)S(1)}, bf16[32,1536]{1,0:T(8,128)(2,1)S(1)}, u32[]{:S(2)}, u32[]{:S(2)}) collective-permute-start(bf16[32,1536]{1,0:T(8,128)(2,1)S(1)} %get-tuple-element.211), channel_id=1, source_target_pairs={{0,2},{1,3},{2,0},{3,1},{4,6},{5,7},{6,4},{7,5},{8,10},{9,11},{10,... | collective-permute-start | bytes 294920 | tf_op jit(solution)/shard_map/ppermute | solution.py:466
  118.7 2.1 %collective-permute-done.35 = bf16[32,1536]{1,0:T(8,128)(2,1)S(1)} collective-permute-done((bf16[32,1536]{1,0:T(8,128)(2,1)S(1)}, bf16[32,1536]{1,0:T(8,128)(2,1)S(1)}, u32[]{:S(2)}, u32[]{:S(2)}) %collective-permute-start.35) | collective-permute-done | bytes 98336 | tf_op jit(solution)/shard_map/ppermute | solution.py:466
  120.8 1.9 %collective-permute-done.34 = bf16[32,1536]{1,0:T(8,128)(2,1)S(1)} collective-permute-done((bf16[32,1536]{1,0:T(8,128)(2,1)S(1)}, bf16[32,1536]{1,0:T(8,128)(2,1)S(1)}, u32[]{:S(2)}, u32[]{:S(2)}) %collective-permute-start.34) | collective-permute-done | bytes 98336 | tf_op jit(solution)/shard_map/ppermute | solution.py:466
  122.8 3.5 %collective-permute-start.36 = (bf16[16,1536]{1,0:T(8,128)(2,1)S(1)}, bf16[16,1536]{1,0:T(8,128)(2,1)S(1)}, u32[]{:S(2)}, u32[]{:S(2)}) collective-permute-start(bf16[16,1536]{1,0:T(8,128)(2,1)S(1)} %slice_select_fusion), channel_id=1, source_target_pairs={{0,4},{4,0},{1,5},{5,1},{2,6},{6,2},{3,7},{7,3},{8,12},{12,8},{9,1... | collective-permute-start | bytes 147464 | tf_op jit(solution)/shard_map/ppermute | solution.py:470
  (97 shorter events, 30.0 us)
Async XLA Ops:
  0.6 7.2 %collective-permute-start = (bf16[512,2048]{1,0:T(8,128)(2,1)}, bf16[512,2048]{1,0:T(8,128)(2,1)S(1)}, u32[]{:S(2)}, u32[]{:S(2)}) collective-permute-start(bf16[512,2048]{1,0:T(8,128)(2,1)} %bitcast.72), channel_id=1, source_target_pairs={{0,4},{4,0},{1,5},{5,1},{2,6},{6,2},{3,7},{7,3},{8,12},{12,8},{9,1... | collective-permute-start | bytes 6291464 | tf_op jit(solution)/shard_map/ppermute | solution.py:470
  11.1 8.7 %collective-permute-start.3 = (bf16[512,128]{1,0:T(8,128)(2,1)S(1)}, bf16[512,128]{1,0:T(8,128)(2,1)S(1)}, u32[]{:S(2)}, u32[]{:S(2)}) collective-permute-start(bf16[512,128]{1,0:T(8,128)(2,1)S(1)} %get-tuple-element.101), channel_id=1, source_target_pairs={{0,16},{8,24},{16,0},{24,8},{1,17},{9,25},{17,1},{25,9},{2,18},{10... | collective-permute-start | bytes 393224 | tf_op jit(solution)/shard_map/ppermute | solution.py:466
  14.0 6.8 %collective-permute-start.2 = (bf16[512,128]{1,0:T(8,128)(2,1)S(1)}, bf16[512,128]{1,0:T(8,128)(2,1)S(1)}, u32[]{:S(2)}, u32[]{:S(2)}) collective-permute-start(bf16[512,128]{1,0:T(8,128)(2,1)S(1)} %get-tuple-element.101), channel_id=1, source_target_pairs={{0,24},{8,0},{16,8},{24,16},{1,25},{9,1},{17,9},{25,17},{2,26},{10... | collective-permute-start | bytes 393224 | tf_op jit(solution)/shard_map/ppermute | solution.py:466
  14.9 5.9 %collective-permute-start.1 = (bf16[512,128]{1,0:T(8,128)(2,1)S(1)}, bf16[512,128]{1,0:T(8,128)(2,1)S(1)}, u32[]{:S(2)}, u32[]{:S(2)}) collective-permute-start(bf16[512,128]{1,0:T(8,128)(2,1)S(1)} %get-tuple-element.101), channel_id=1, source_target_pairs={{0,8},{8,16},{16,24},{24,0},{1,9},{9,17},{17,25},{25,1},{2,10},{10... | collective-permute-start | bytes 393224 | tf_op jit(solution)/shard_map/ppermute | solution.py:466
  20.9 11.3 %collective-permute-start.7 = (bf16[512,512]{1,0:T(8,128)(2,1)S(1)}, bf16[512,512]{1,0:T(8,128)(2,1)S(1)}, u32[]{:S(2)}, u32[]{:S(2)}) collective-permute-start(bf16[512,512]{1,0:T(8,128)(2,1)S(1)} %get-tuple-element.112), channel_id=1, source_target_pairs={{0,4},{4,0},{1,5},{5,1},{2,6},{6,2},{3,7},{7,3},{8,12},{12,8},{9,1... | collective-permute-start | bytes 1572872 | tf_op jit(solution)/shard_map/ppermute | solution.py:470
  22.2 10.0 %collective-permute-start.6 = (bf16[512,128]{1,0:T(8,128)(2,1)S(1)}, bf16[512,128]{1,0:T(8,128)(2,1)S(1)}, u32[]{:S(2)}, u32[]{:S(2)}) collective-permute-start(bf16[512,128]{1,0:T(8,128)(2,1)S(1)} %add_convert_fusion.7), channel_id=1, source_target_pairs={{0,64},{32,96},{64,0},{96,32},{1,65},{33,97},{65,1},{97,33},{2,66}... | collective-permute-start | bytes 393224 | tf_op jit(solution)/shard_map/ppermute | solution.py:466
  25.1 7.1 %collective-permute-start.5 = (bf16[512,128]{1,0:T(8,128)(2,1)S(1)}, bf16[512,128]{1,0:T(8,128)(2,1)S(1)}, u32[]{:S(2)}, u32[]{:S(2)}) collective-permute-start(bf16[512,128]{1,0:T(8,128)(2,1)S(1)} %add_convert_fusion.7), channel_id=1, source_target_pairs={{0,96},{32,0},{64,32},{96,64},{1,97},{33,1},{65,33},{97,65},{2,98}... | collective-permute-start | bytes 393224 | tf_op jit(solution)/shard_map/ppermute | solution.py:466
  25.9 6.3 %collective-permute-start.4 = (bf16[512,128]{1,0:T(8,128)(2,1)S(1)}, bf16[512,128]{1,0:T(8,128)(2,1)S(1)}, u32[]{:S(2)}, u32[]{:S(2)}) collective-permute-start(bf16[512,128]{1,0:T(8,128)(2,1)S(1)} %add_convert_fusion.7), channel_id=1, source_target_pairs={{0,32},{32,64},{64,96},{96,0},{1,33},{33,65},{65,97},{97,1},{2,34}... | collective-permute-start | bytes 393224 | tf_op jit(solution)/shard_map/ppermute | solution.py:466
  35.1 10.5 %collective-permute-start.11 = (bf16[512,512]{1,0:T(8,128)(2,1)S(1)}, bf16[512,512]{1,0:T(8,128)(2,1)S(1)}, u32[]{:S(2)}, u32[]{:S(2)}) collective-permute-start(bf16[512,512]{1,0:T(8,128)(2,1)S(1)} %get-tuple-element.133), channel_id=1, source_target_pairs={{0,4},{4,0},{1,5},{5,1},{2,6},{6,2},{3,7},{7,3},{8,12},{12,8},{9,1... | collective-permute-start | bytes 1572872 | tf_op jit(solution)/shard_map/ppermute | solution.py:470
  36.1 9.4 %collective-permute-start.10 = (bf16[512,128]{1,0:T(8,128)(2,1)S(1)}, bf16[512,128]{1,0:T(8,128)(2,1)S(1)}, u32[]{:S(2)}, u32[]{:S(2)}) collective-permute-start(bf16[512,128]{1,0:T(8,128)(2,1)S(1)} %get-tuple-element.126), channel_id=1, source_target_pairs={{0,16},{8,24},{16,0},{24,8},{1,17},{9,25},{17,1},{25,9},{2,18},{10... | collective-permute-start | bytes 393224 | tf_op jit(solution)/shard_map/ppermute | solution.py:466
  38.3 7.2 %collective-permute-start.9 = (bf16[512,128]{1,0:T(8,128)(2,1)S(1)}, bf16[512,128]{1,0:T(8,128)(2,1)S(1)}, u32[]{:S(2)}, u32[]{:S(2)}) collective-permute-start(bf16[512,128]{1,0:T(8,128)(2,1)S(1)} %get-tuple-element.126), channel_id=1, source_target_pairs={{0,24},{8,0},{16,8},{24,16},{1,25},{9,1},{17,9},{25,17},{2,26},{10... | collective-permute-start | bytes 393224 | tf_op jit(solution)/shard_map/ppermute | solution.py:466
  39.3 6.3 %collective-permute-start.8 = (bf16[512,128]{1,0:T(8,128)(2,1)S(1)}, bf16[512,128]{1,0:T(8,128)(2,1)S(1)}, u32[]{:S(2)}, u32[]{:S(2)}) collective-permute-start(bf16[512,128]{1,0:T(8,128)(2,1)S(1)} %get-tuple-element.126), channel_id=1, source_target_pairs={{0,8},{8,16},{16,24},{24,0},{1,9},{9,17},{17,25},{25,1},{2,10},{10... | collective-permute-start | bytes 393224 | tf_op jit(solution)/shard_map/ppermute | solution.py:466
  45.7 11.6 %collective-permute-start.16 = (bf16[2,4,32,512]{3,2,1,0:T(8,128)(2,1)S(1)}, bf16[2,4,32,512]{3,2,1,0:T(8,128)(2,1)S(1)}, u32[]{:S(2)}, u32[]{:S(2)}) collective-permute-start(bf16[2,4,32,512]{3,2,1,0:T(8,128)(2,1)S(1)} %get-tuple-element.193), channel_id=1, source_target_pairs={{0,24},{8,0},{16,8},{24,16},{1,25},{9,1},{17,9},{25,17},{2,26},{10... | collective-permute-start | bytes 786440 | tf_op jit(solution)/shard_map/ppermute | solution.py:466
  48.1 9.2 %collective-permute-start.15 = (bf16[2,4,32,512]{3,2,1,0:T(8,128)(2,1)S(1)}, bf16[2,4,32,512]{3,2,1,0:T(8,128)(2,1)S(1)}, u32[]{:S(2)}, u32[]{:S(2)}) collective-permute-start(bf16[2,4,32,512]{3,2,1,0:T(8,128)(2,1)S(1)} %get-tuple-element.194), channel_id=1, source_target_pairs={{0,8},{8,16},{16,24},{24,0},{1,9},{9,17},{17,25},{25,1},{2,10},{10... | collective-permute-start | bytes 786440 | tf_op jit(solution)/shard_map/ppermute | solution.py:466
  48.1 7.9 %collective-permute-start.14 = (bf16[512,128]{1,0:T(8,128)(2,1)S(1)}, bf16[512,128]{1,0:T(8,128)(2,1)S(1)}, u32[]{:S(2)}, u32[]{:S(2)}) collective-permute-start(bf16[512,128]{1,0:T(8,128)(2,1)S(1)} %add_convert_fusion.6), channel_id=1, source_target_pairs={{0,64},{32,96},{64,0},{96,32},{1,65},{33,97},{65,1},{97,33},{2,66}... | collective-permute-start | bytes 393224 | tf_op jit(solution)/shard_map/ppermute | solution.py:466
  50.3 5.8 %collective-permute-start.13 = (bf16[512,128]{1,0:T(8,128)(2,1)S(1)}, bf16[512,128]{1,0:T(8,128)(2,1)S(1)}, u32[]{:S(2)}, u32[]{:S(2)}) collective-permute-start(bf16[512,128]{1,0:T(8,128)(2,1)S(1)} %add_convert_fusion.6), channel_id=1, source_target_pairs={{0,96},{32,0},{64,32},{96,64},{1,97},{33,1},{65,33},{97,65},{2,98}... | collective-permute-start | bytes 393224 | tf_op jit(solution)/shard_map/ppermute | solution.py:466
  51.2 6.1 %collective-permute-start.12 = (bf16[512,128]{1,0:T(8,128)(2,1)S(1)}, bf16[512,128]{1,0:T(8,128)(2,1)S(1)}, u32[]{:S(2)}, u32[]{:S(2)}) collective-permute-start(bf16[512,128]{1,0:T(8,128)(2,1)S(1)} %add_convert_fusion.6), channel_id=1, source_target_pairs={{0,32},{32,64},{64,96},{96,0},{1,33},{33,65},{65,97},{97,1},{2,34}... | collective-permute-start | bytes 393224 | tf_op jit(solution)/shard_map/ppermute | solution.py:466
  57.5 18.6 %collective-permute-start.20 = (bf16[4,4,32,512]{3,2,1,0:T(8,128)(2,1)S(1)}, bf16[4,4,32,512]{3,2,1,0:T(8,128)(2,1)S(1)}, u32[]{:S(2)}, u32[]{:S(2)}) collective-permute-start(bf16[4,4,32,512]{3,2,1,0:T(8,128)(2,1)S(1)} %pad_maximum_fusion.2), channel_id=1, source_target_pairs={{0,8},{8,16},{16,24},{24,0},{1,9},{9,17},{17,25},{25,1},{2,10},{10... | collective-permute-start | bytes 1572872 | tf_op jit(solution)/shard_map/ppermute | solution.py:466
  57.9 18.2 %collective-permute-start.21 = (bf16[4,4,32,512]{3,2,1,0:T(8,128)(2,1)S(1)}, bf16[4,4,32,512]{3,2,1,0:T(8,128)(2,1)S(1)}, u32[]{:S(2)}, u32[]{:S(2)}) collective-permute-start(bf16[4,4,32,512]{3,2,1,0:T(8,128)(2,1)S(1)} %pad_maximum_fusion.3), channel_id=1, source_target_pairs={{0,24},{8,0},{16,8},{24,16},{1,25},{9,1},{17,9},{25,17},{2,26},{10... | collective-permute-start | bytes 1572872 | tf_op jit(solution)/shard_map/ppermute | solution.py:466
  63.6 12.5 %collective-permute-start.19 = (bf16[4,4,32,512]{3,2,1,0:T(8,128)(2,1)S(1)}, bf16[4,4,32,512]{3,2,1,0:T(8,128)(2,1)S(1)}, u32[]{:S(2)}, u32[]{:S(2)}) collective-permute-start(bf16[4,4,32,512]{3,2,1,0:T(8,128)(2,1)S(1)} %get-tuple-element.158), channel_id=1, source_target_pairs={{0,32},{32,64},{64,96},{96,0},{1,33},{33,65},{65,97},{97,1},{2,34}... | collective-permute-start | bytes 1572872 | tf_op jit(solution)/shard_map/ppermute | solution.py:466
  64.5 10.7 %collective-permute-start.18 = (bf16[2,4,32,512]{3,2,1,0:T(8,128)(2,1)S(1)}, bf16[2,4,32,512]{3,2,1,0:T(8,128)(2,1)S(1)}, u32[]{:S(2)}, u32[]{:S(2)}) collective-permute-start(bf16[2,4,32,512]{3,2,1,0:T(8,128)(2,1)S(1)} %get-tuple-element.209), channel_id=1, source_target_pairs={{0,24},{8,0},{16,8},{24,16},{1,25},{9,1},{17,9},{25,17},{2,26},{10... | collective-permute-start | bytes 786440 | tf_op jit(solution)/shard_map/ppermute | solution.py:466
  65.7 10.4 %collective-permute-start.17 = (bf16[2,4,32,512]{3,2,1,0:T(8,128)(2,1)S(1)}, bf16[2,4,32,512]{3,2,1,0:T(8,128)(2,1)S(1)}, u32[]{:S(2)}, u32[]{:S(2)}) collective-permute-start(bf16[2,4,32,512]{3,2,1,0:T(8,128)(2,1)S(1)} %get-tuple-element.210), channel_id=1, source_target_pairs={{0,8},{8,16},{16,24},{24,0},{1,9},{9,17},{17,25},{25,1},{2,10},{10... | collective-permute-start | bytes 786440 | tf_op jit(solution)/shard_map/ppermute | solution.py:466
  76.1 13.0 %collective-permute-start.22 = (bf16[512,2048]{1,0:T(8,128)(2,1)S(1)}, bf16[512,2048]{1,0:T(8,128)(2,1)S(1)}, u32[]{:S(2)}, u32[]{:S(2)}) collective-permute-start(bf16[512,2048]{1,0:T(8,128)(2,1)S(1)} %shard_map.104), channel_id=1, source_target_pairs={{0,4},{4,0},{1,5},{5,1},{2,6},{6,2},{3,7},{7,3},{8,12},{12,8},{9,1... | collective-permute-start | bytes 6291464 | tf_op jit(solution)/shard_map/ppermute | solution.py:470
  79.4 15.2 %collective-permute-start.24 = (bf16[4,4,32,512]{3,2,1,0:T(8,128)(2,1)S(1)}, bf16[4,4,32,512]{3,2,1,0:T(8,128)(2,1)S(1)}, u32[]{:S(2)}, u32[]{:S(2)}) collective-permute-start(bf16[4,4,32,512]{3,2,1,0:T(8,128)(2,1)S(1)} %pad_maximum_fusion.5), channel_id=1, source_target_pairs={{0,24},{8,0},{16,8},{24,16},{1,25},{9,1},{17,9},{25,17},{2,26},{10... | collective-permute-start | bytes 1572872 | tf_op jit(solution)/shard_map/ppermute | solution.py:466
  82.4 17.1 %collective-permute-start.25 = (bf16[18,32,512]{2,1,0:T(8,128)(2,1)S(1)}, bf16[18,32,512]{2,1,0:T(8,128)(2,1)S(1)}, u32[]{:S(2)}, u32[]{:S(2)}) collective-permute-start(bf16[18,32,512]{2,1,0:T(8,128)(2,1)S(1)} %pad_maximum_fusion), channel_id=1, source_target_pairs={{0,32},{32,64},{64,96},{96,0},{1,33},{33,65},{65,97},{97,1},{2,34}... | collective-permute-start | bytes 1769480 | tf_op jit(solution)/shard_map/ppermute | solution.py:466
  83.3 16.2 %collective-permute-start.26 = (bf16[18,32,512]{2,1,0:T(8,128)(2,1)S(1)}, bf16[18,32,512]{2,1,0:T(8,128)(2,1)S(1)}, u32[]{:S(2)}, u32[]{:S(2)}) collective-permute-start(bf16[18,32,512]{2,1,0:T(8,128)(2,1)S(1)} %pad_maximum_fusion.1), channel_id=1, source_target_pairs={{0,96},{32,0},{64,32},{96,64},{1,97},{33,1},{65,33},{97,65},{2,98}... | collective-permute-start | bytes 1769480 | tf_op jit(solution)/shard_map/ppermute | solution.py:466
  85.4 14.1 %collective-permute-start.23 = (bf16[4,4,32,512]{3,2,1,0:T(8,128)(2,1)S(1)}, bf16[4,4,32,512]{3,2,1,0:T(8,128)(2,1)S(1)}, u32[]{:S(2)}, u32[]{:S(2)}) collective-permute-start(bf16[4,4,32,512]{3,2,1,0:T(8,128)(2,1)S(1)} %pad_maximum_fusion.4), channel_id=1, source_target_pairs={{0,8},{8,16},{16,24},{24,0},{1,9},{9,17},{17,25},{25,1},{2,10},{10... | collective-permute-start | bytes 1572872 | tf_op jit(solution)/shard_map/ppermute | solution.py:466
  100.3 10.0 %collective-permute-start.28 = (bf16[2,4,32,512]{3,2,1,0:T(8,128)(2,1)S(1)}, bf16[2,4,32,512]{3,2,1,0:T(8,128)(2,1)S(1)}, u32[]{:S(2)}, u32[]{:S(2)}) collective-permute-start(bf16[2,4,32,512]{3,2,1,0:T(8,128)(2,1)S(1)} %pad_maximum_fusion.8), channel_id=1, source_target_pairs={{0,96},{32,0},{64,32},{96,64},{1,97},{33,1},{65,33},{97,65},{2,98}... | collective-permute-start | bytes 786440 | tf_op jit(solution)/shard_map/ppermute | solution.py:466
  101.6 9.0 %collective-permute-start.27 = (bf16[2,4,32,512]{3,2,1,0:T(8,128)(2,1)S(1)}, bf16[2,4,32,512]{3,2,1,0:T(8,128)(2,1)S(1)}, u32[]{:S(2)}, u32[]{:S(2)}) collective-permute-start(bf16[2,4,32,512]{3,2,1,0:T(8,128)(2,1)S(1)} %pad_maximum_fusion.7), channel_id=1, source_target_pairs={{0,32},{32,64},{64,96},{96,0},{1,33},{33,65},{65,97},{97,1},{2,34}... | collective-permute-start | bytes 786440 | tf_op jit(solution)/shard_map/ppermute | solution.py:466
  102.0 8.2 %collective-permute-start.29 = (bf16[4,32,512]{2,1,0:T(8,128)(2,1)S(1)}, bf16[4,32,512]{2,1,0:T(8,128)(2,1)S(1)}, u32[]{:S(2)}, u32[]{:S(2)}) collective-permute-start(bf16[4,32,512]{2,1,0:T(8,128)(2,1)S(1)} %get-tuple-element.198), channel_id=1, source_target_pairs={{0,64},{32,96},{64,0},{96,32},{1,65},{33,97},{65,1},{97,33},{2,66}... | collective-permute-start | bytes 393224 | tf_op jit(solution)/shard_map/ppermute | solution.py:466
  103.1 7.6 %collective-permute-start.30 = (bf16[4,32,512]{2,1,0:T(8,128)(2,1)S(1)}, bf16[4,32,512]{2,1,0:T(8,128)(2,1)S(1)}, u32[]{:S(2)}, u32[]{:S(2)}) collective-permute-start(bf16[4,32,512]{2,1,0:T(8,128)(2,1)S(1)} %get-tuple-element.204), channel_id=1, source_target_pairs={{0,16},{8,24},{16,0},{24,8},{1,17},{9,25},{17,1},{25,9},{2,18},{10... | collective-permute-start | bytes 393224 | tf_op jit(solution)/shard_map/ppermute | solution.py:466
  106.1 6.7 %collective-permute-start.32 = (bf16[4,32,512]{2,1,0:T(8,128)(2,1)S(1)}, bf16[4,32,512]{2,1,0:T(8,128)(2,1)S(1)}, u32[]{:S(2)}, u32[]{:S(2)}) collective-permute-start(bf16[4,32,512]{2,1,0:T(8,128)(2,1)S(1)} %get-tuple-element.187), channel_id=1, source_target_pairs={{0,8},{8,16},{16,24},{24,0},{1,9},{9,17},{17,25},{25,1},{2,10},{10... | collective-permute-start | bytes 393224 | tf_op jit(solution)/shard_map/ppermute | solution.py:466
  (6 other events, 31.7 us)
